TPU v7x, 32 devices: a whole 2x2x4 slice. The times are simulated.
32 devices in a mesh: groups: 2 (over x), seq: 16 (over z, y, core).
Axes of the slice: x: 2, y: 2, z: 4, core: 2. Of those that a mesh axis runs over, the one named last changes fastest.
Arguments:
- normed: bfloat16 [4096, 8192], P(('groups', 'seq')), parts along dimension 0, may hold values from -8 to 8
- shared_query_rows: bfloat16 [4096, 4096], P(('groups', 'seq')), parts along dimension 0, may hold values from -10 to 10
- shared_key_rows: bfloat16 [4096, 512], P(('groups', 'seq')), parts along dimension 0, may hold values from -4 to 4
- shared_value_rows: bfloat16 [4096, 512], P(('groups', 'seq')), parts along dimension 0, may hold values from -6 to 6
- token_adapter: int32 [4096, 1], P(('groups', 'seq')), parts along dimension 0, may hold values from 0 to 15; in each aligned block of 128 rows (0 to 127, 128 to 255, ...) at most 12 rows name the same one
- adapter_slot_table: int32 [16], replicated, may hold values from 0 to 15, each once
- adapter_down_factors: bfloat16 [16, 8192, 192], P('seq'), may hold values from -0.0625 to 0.0625
- adapter_up_query: bfloat16 [16, 64, 4096], P('seq'), may hold values from -0.375 to 0.375
- adapter_up_key_value: bfloat16 [16, 2, 64, 512], P('seq'), may hold values from -0.375 to 0.375
- token_request: int32 [4096], P('groups'), parts along dimension 0, may hold values from 0 to 3, never falling along the last dimension, each value on 1 to 1024 neighbouring positions
Outputs:
- attention: bfloat16 [4096, 4096], P(('groups', 'seq')), parts along dimension 0
- key_cache: bfloat16 [4096, 512], P(('groups', 'seq')), parts along dimension 0
- value_cache: bfloat16 [4096, 512], P(('groups', 'seq')), parts along dimension 0
There are 2 independent parts, one for each index of `groups`. A program takes and returns all parts, laid end to end along the dimension named above; an argument that names none is the same for every part. Nothing has to cross between parts.
Inputs may be any that keep to these rules, and one draw needn't show every extreme that they name: `token_adapter`: each token names one adapter; among the 128 tokens of one device no adapter is named more than 12 times. `adapter_slot_table`: each slot holds exactly one adapter. `token_request`: request numbers never fall; each request holds 1 to 1024 consecutive tokens.
All inputs are finite; a program needn't handle non-finite values.
Results may differ from a plain program's by a relative error of at most 0.012.
Values may be sent and summed in bfloat16 or wider, within the bound.
No kernel may reach another device: no remote copies, remote signals or barrier semaphores. Data moves between devices by JAX's collectives and lax.ppermute only.
A program may use at most 256 MiB of HBM per device.

v0:
```python
import math

import jax
import jax.numpy as jnp
from jax import lax
from jax.sharding import PartitionSpec as P

QUERY_HEADS = 32
KEY_VALUE_HEADS = 4
HEAD_SIZE = 128


def reduced_projection(incoming_rows, adapter_down_factors, adapter_up_query, adapter_up_key_value):
    sources, slots, width = incoming_rows.shape
    rank_width = adapter_up_query.shape[1]
    flattened_rows = incoming_rows.reshape(sources * slots, width)
    down_projected = jnp.dot(
        flattened_rows, adapter_down_factors[0], preferred_element_type=jnp.float32
    ).astype(jnp.bfloat16)
    adapter_query_update = jnp.dot(
        down_projected[:, :rank_width], adapter_up_query[0], preferred_element_type=jnp.float32
    ).astype(jnp.bfloat16)
    adapter_key_update = jnp.dot(
        down_projected[:, rank_width : 2 * rank_width],
        adapter_up_key_value[0, 0],
        preferred_element_type=jnp.float32,
    ).astype(jnp.bfloat16)
    adapter_value_update = jnp.dot(
        down_projected[:, 2 * rank_width :],
        adapter_up_key_value[0, 1],
        preferred_element_type=jnp.float32,
    ).astype(jnp.bfloat16)
    joined = jnp.concatenate(
        [adapter_query_update, adapter_key_update, adapter_value_update], axis=1
    )
    return joined.reshape(sources, slots, joined.shape[1])


def attend(query_rows, gathered_keys, gathered_values, allowed):
    resident_rows = query_rows.shape[0]
    token_group = QUERY_HEADS // KEY_VALUE_HEADS
    query_head_layout = query_rows.reshape(resident_rows, KEY_VALUE_HEADS, token_group, HEAD_SIZE)
    key_head_layout = gathered_keys.reshape(gathered_keys.shape[0], KEY_VALUE_HEADS, HEAD_SIZE)
    value_head_layout = gathered_values.reshape(
        gathered_values.shape[0], KEY_VALUE_HEADS, HEAD_SIZE
    )
    results = []
    for grouped_heads in range(KEY_VALUE_HEADS):
        scores = jnp.einsum(
            "tjd,sd->jts",
            query_head_layout[:, grouped_heads],
            key_head_layout[:, grouped_heads],
            preferred_element_type=jnp.float32,
        ) / math.sqrt(HEAD_SIZE)
        scores = jnp.where(allowed[None], scores, -1e30)
        largest = jnp.max(scores, axis=-1, keepdims=True)
        raised = jnp.exp(scores - largest)
        weights = (raised / jnp.sum(raised, axis=-1, keepdims=True)).astype(jnp.bfloat16)
        blended = jnp.einsum(
            "jts,sd->tjd",
            weights,
            value_head_layout[:, grouped_heads],
            preferred_element_type=jnp.float32,
        )
        results.append(blended.astype(jnp.bfloat16))
    return jnp.stack(results, axis=1).reshape(resident_rows, QUERY_HEADS * HEAD_SIZE)


def local(
    normed,
    shared_query_rows,
    shared_key_rows,
    shared_value_rows,
    token_adapter,
    adapter_slot_table,
    adapter_down_factors,
    adapter_up_query,
    adapter_up_key_value,
    token_request,
):
    resident_rows, width = normed.shape
    devices = lax.axis_size("seq")
    position = lax.axis_index("seq")
    reach = devices // 2
    stores = adapter_slot_table.shape[0]
    capacity = max(2, 3 * resident_rows // (2 * stores))
    chosen_ids = token_adapter[:, 0]
    owners = jnp.sum(
        jnp.where(
            chosen_ids[:, None] == jnp.arange(stores, dtype=jnp.int32)[None, :],
            adapter_slot_table[None, :],
            0,
        ),
        axis=1,
    )
    one_hot = (owners[:, None] == jnp.arange(devices, dtype=jnp.int32)[None, :]).astype(jnp.int32)
    places = jnp.sum((jnp.cumsum(one_hot, axis=0) - 1) * one_hot, axis=1)
    outgoing = jnp.zeros((devices, capacity, width), jnp.bfloat16).at[owners, places].set(normed)
    returned = lax.all_to_all(
        reduced_projection(
            lax.all_to_all(outgoing, "seq", split_axis=0, concat_axis=0, tiled=True),
            adapter_down_factors,
            adapter_up_query,
            adapter_up_key_value,
        ),
        "seq",
        split_axis=0,
        concat_axis=0,
        tiled=True,
    )
    deltas = returned[owners, places]
    query_width = shared_query_rows.shape[1]
    kv_width = shared_key_rows.shape[1]
    query_rows = (
        shared_query_rows.astype(jnp.float32) + deltas[:, :query_width].astype(jnp.float32)
    ).astype(jnp.bfloat16)
    keys_here = (
        shared_key_rows.astype(jnp.float32)
        + deltas[:, query_width : query_width + kv_width].astype(jnp.float32)
    ).astype(jnp.bfloat16)
    values_here = (
        shared_value_rows.astype(jnp.float32)
        + deltas[:, query_width + kv_width :].astype(jnp.float32)
    ).astype(jnp.bfloat16)
    pages = resident_rows // devices
    key_pages, value_pages = (
        lax.all_to_all(
            keys_here.reshape(devices, pages, kv_width),
            "seq",
            split_axis=0,
            concat_axis=0,
            tiled=True,
        ),
        lax.all_to_all(
            values_here.reshape(devices, pages, kv_width),
            "seq",
            split_axis=0,
            concat_axis=0,
            tiled=True,
        ),
    )
    key_cache = key_pages.reshape(resident_rows, kv_width)
    value_cache = value_pages.reshape(resident_rows, kv_width)
    window = (reach + 1) * resident_rows
    group_k, group_v = (
        lax.all_gather(keys_here, "seq", axis=0, tiled=True),
        lax.all_gather(values_here, "seq", axis=0, tiled=True),
    )
    front = jnp.zeros((reach * resident_rows, kv_width), jnp.bfloat16)
    gathered_keys = lax.dynamic_slice_in_dim(
        jnp.concatenate([front, group_k], axis=0), position * resident_rows, window, 0
    )
    gathered_values = lax.dynamic_slice_in_dim(
        jnp.concatenate([front, group_v], axis=0), position * resident_rows, window, 0
    )
    padded_ids = jnp.concatenate([jnp.full((reach * resident_rows,), -1, jnp.int32), token_request])
    key_ids = lax.dynamic_slice_in_dim(padded_ids, position * resident_rows, window)
    query_ids = lax.dynamic_slice_in_dim(token_request, position * resident_rows, resident_rows)
    offsets = jnp.arange(window) - reach * resident_rows
    allowed = (key_ids[None, :] == query_ids[:, None]) & (
        offsets[None, :] <= jnp.arange(resident_rows)[:, None]
    )
    attention = attend(query_rows, gathered_keys, gathered_values, allowed)
    return (attention, key_cache, value_cache)


def solution(mesh):
    placed = (
        P(("groups", "seq"), None),
        P(("groups", "seq"), None),
        P(("groups", "seq"), None),
        P(("groups", "seq"), None),
        P(("groups", "seq"), None),
        P(),
        P("seq", None, None),
        P("seq", None, None),
        P("seq", None, None, None),
        P("groups"),
    )
    return jax.shard_map(
        local,
        mesh=mesh,
        in_specs=placed,
        out_specs=(
            P(("groups", "seq"), None),
            P(("groups", "seq"), None),
            P(("groups", "seq"), None),
        ),
        check_vma=False,
    )
```

profile of v0, /device:TPU:0, one launch (start us, length us, event | category | flops | bytes accessed | tf_op | source)
XLA Modules:
  0.0 384.9 jit_solution(16206669510055014567)
XLA Ops:
  7.2 0.0 copy-start
  7.2 0.0 all-gather.5.cloned.1.call-start
  7.2 1.0 select_reduce_fusion.1
  8.2 0.1 fusion.43
  8.3 0.2 reduce_window_sum.11
  8.5 0.2 select_reduce_fusion
  8.7 2.0 broadcast_in_dim.38
  10.7 64.6 %scatter_fusion = bf16[16,12,8192]{2,0,1:T(8,128)(2,1)} fusion(bf16[16,12,8192]{2,0,1:T(8,128)(2,1)} %broadcast_in_dim.38, s32[128]{0:T(128)S(1)} %get-tuple-element.15, bf16[128,8192]{1,0:T(8,128)(2,1)} %param.10), kind=kCustom, calls=%fused_computation.1 | custom fusion | bytes 6292480 | tf_op jit(solution)/shard_map/scatter | solution.py:98
  75.3 3.7 copy.38
  78.9 99.9 %all_to_all.20 = bf16[16,12,8192]{2,1,0:T(8,128)(2,1)} all-to-all(bf16[16,12,8192]{2,1,0:T(8,128)(2,1)S(1)} %copy.38), channel_id=1, replica_groups=mesh['groups'=2,'seq'=16] {'seq'}, dimensions={0} | all-to-all | bytes 6291456 | tf_op jit(solution)/shard_map/all_to_all | solution.py:101
  178.8 4.7 %reshape.124 = bf16[192,8192]{1,0:T(8,128)(2,1)} reshape(bf16[16,12,8192]{2,1,0:T(8,128)(2,1)} %all_to_all.20) | data formatting | bytes 6291456 | tf_op jit(solution)/shard_map/reshape | solution.py:16
  183.5 0.0 copy-done
  183.5 0.0 copy-start.2
  183.5 0.0 copy-start.1
  183.5 2.9 fusion.34
  186.5 0.0 copy-done.2
  186.5 0.2 convolution_convert_fusion.1
  186.7 0.2 convolution_convert_fusion.2
  187.0 0.0 copy-done.1
  187.0 0.6 convolution_convert_fusion
  187.6 1.4 pad_maximum_fusion
  189.0 4.0 %reshape.125 = bf16[16,12,5120]{2,1,0:T(8,128)(2,1)} reshape(bf16[192,5120]{1,0:T(8,128)(2,1)} %pad_maximum_fusion) | data formatting | bytes 3932160 | tf_op jit(solution)/shard_map/reshape | solution.py:36
  193.0 63.9 %all_to_all.21 = bf16[16,12,5120]{2,1,0:T(8,128)(2,1)S(1)} all-to-all(bf16[16,12,5120]{2,1,0:T(8,128)(2,1)} %reshape.125), channel_id=1, replica_groups=mesh['groups'=2,'seq'=16] {'seq'}, dimensions={0} | all-to-all | bytes 3932160 | tf_op jit(solution)/shard_map/all_to_all | solution.py:99
  256.9 2.4 copy.39
  259.2 0.0 copy-start.3
  259.2 0.0 copy-start.4
  259.2 0.0 copy-start.5
  259.2 5.3 %gather_fusion = bf16[128,5120]{1,0:T(8,128)(2,1)} fusion(bf16[16,12,5120]{2,0,1:T(8,128)(2,1)} %copy.39, s32[128]{0:T(128)S(1)} %get-tuple-element.14), kind=kCustom, calls=%fused_computation | custom fusion | bytes 2622464 | tf_op jit(solution)/shard_map/gather | solution.py:111
  264.6 0.0 copy-done.3
  264.6 0.0 copy-done.4
  264.6 1.7 add_convert_fusion.2
  266.3 0.0 all-gather.5.cloned.1.call-update
  266.3 0.0 all-gather.3.cloned.1.call-start
  266.4 0.7 all-gather.3.cloned.1.call-update
  267.1 0.0 copy-done.5
  267.1 0.1 dynamic_slice.14
  267.2 0.1 pad_dynamic-slice_fusion.2
  267.2 5.1 %all-to-all-start.2 = ((bf16[16,8,512]{2,1,0:T(8,128)(2,1)}), bf16[16,8,512]{2,1,0:T(8,128)(2,1)S(1)}, u32[]{:S(2)}, u32[]{:S(2)}) async-start(bf16[16,8,512]{2,1,0:T(8,128)(2,1)} %bitcast.238), calls=%async_computation.2 | async-start | bytes 262144 | tf_op jit(solution)/shard_map/all_to_all | solution.py:127
  272.4 0.8 fusion.37
  273.2 7.3 %all-to-all-done.2 = bf16[16,8,512]{2,1,0:T(8,128)(2,1)S(1)} async-done(((bf16[16,8,512]{2,1,0:T(8,128)(2,1)}), bf16[16,8,512]{2,1,0:T(8,128)(2,1)S(1)}, u32[]{:S(2)}, u32[]{:S(2)}) %all-to-all-start.2) | async-done | bytes 131104 | tf_op jit(solution)/shard_map/all_to_all | solution.py:127
  280.4 3.7 all-to-all-start.3
  284.2 2.8 add_convert_fusion
  286.9 2.3 copy.43
  289.2 2.8 all-to-all-done.3
  292.0 16.4 %all-gather.5.cloned.1.call-done = bf16[2048,512]{1,0:T(8,128)(2,1)} async-done(((bf16[128,512]{1,0:T(8,128)(2,1)}), bf16[2048,512]{1,0:T(8,128)(2,1)}) %all-gather.5.cloned.1.call-update) | async-done | bytes 2097168 | tf_op jit(solution)/shard_map/all_gather | solution.py:146
  308.4 2.3 pad_dynamic-slice_fusion
  310.8 2.4 copy.41
  313.1 3.4 exponential_reduce_fusion.3
  316.5 3.4 exponential_reduce_fusion.2
  319.9 3.3 exponential_reduce_fusion.1
  323.2 3.4 exponential_reduce_fusion
  326.6 24.8 %all-gather.3.cloned.1.call-done = bf16[2048,512]{1,0:T(8,128)(2,1)} async-done(((bf16[128,512]{1,0:T(8,128)(2,1)}), bf16[2048,512]{1,0:T(8,128)(2,1)}) %all-gather.3.cloned.1.call-update) | async-done | bytes 2097168 | tf_op jit(solution)/shard_map/all_gather | solution.py:147
  351.4 2.3 pad_dynamic-slice_fusion.1
  353.7 2.4 copy.40
  356.1 4.0 %fusion.30 = bf16[128,1,8,128]{0,3,2,1:T(8,128)(2,1)} fusion(f32[8,128]{1,0:T(8,128)} %exponential_reduce_fusion.3, bf16[1152,4,128]{0,2,1:T(8,128)(2,1)} %bitcast.233, pred[128,1152]{0,1:T(8,128)(4,1)S(1)} %fusion.37, bf16[1152,4,128]{0,2,1:T(8,128)(2,1)} %bitcast.229, bf16[128,4,8,128]{0,3,2,1:T(8,128)(2,1)} %bitcast.243), kind=kOutput, calls=%fused_computation.55 | convolution fusion | flops 610011264 | bytes 1265664 | tf_op jit(solution)/shard_map/jts,sd->tjd/dot_general | solution.py:59
  360.1 4.0 %fusion.31 = bf16[128,1,8,128]{0,3,2,1:T(8,128)(2,1)} fusion(f32[8,128]{1,0:T(8,128)} %exponential_reduce_fusion.2, bf16[1152,4,128]{0,2,1:T(8,128)(2,1)} %bitcast.234, pred[128,1152]{0,1:T(8,128)(4,1)S(1)} %fusion.37, bf16[1152,4,128]{0,2,1:T(8,128)(2,1)} %bitcast.230, bf16[128,4,8,128]{0,3,2,1:T(8,128)(2,1)} %bitcast.244), kind=kOutput, calls=%fused_computation.56 | convolution fusion | flops 610011264 | bytes 1265664 | tf_op jit(solution)/shard_map/jts,sd->tjd/dot_general | solution.py:59
  364.1 4.0 %fusion.32 = bf16[128,1,8,128]{0,3,2,1:T(8,128)(2,1)} fusion(f32[8,128]{1,0:T(8,128)} %exponential_reduce_fusion.1, bf16[1152,4,128]{0,2,1:T(8,128)(2,1)} %bitcast.235, pred[128,1152]{0,1:T(8,128)(4,1)S(1)} %fusion.37, bf16[1152,4,128]{0,2,1:T(8,128)(2,1)} %bitcast.231, bf16[128,4,8,128]{0,3,2,1:T(8,128)(2,1)} %bitcast.245), kind=kOutput, calls=%fused_computation.57 | convolution fusion | flops 610011264 | bytes 1265664 | tf_op jit(solution)/shard_map/jts,sd->tjd/dot_general | solution.py:59
  368.1 4.0 %fusion.33 = bf16[128,1,8,128]{0,3,2,1:T(8,128)(2,1)} fusion(f32[8,128]{1,0:T(8,128)} %exponential_reduce_fusion, bf16[1152,4,128]{0,2,1:T(8,128)(2,1)} %bitcast.236, pred[128,1152]{0,1:T(8,128)(4,1)S(1)} %fusion.37, bf16[1152,4,128]{0,2,1:T(8,128)(2,1)} %bitcast.232, bf16[128,4,8,128]{0,3,2,1:T(8,128)(2,1)} %bitcast.246), kind=kOutput, calls=%fused_computation.58 | convolution fusion | flops 610011264 | bytes 1265664 | tf_op jit(solution)/shard_map/jts,sd->tjd/dot_general | solution.py:59
  372.1 2.3 pad_maximum_fusion.1
  374.4 2.3 copy.55
  376.7 0.7 copy.71
  377.4 0.7 copy.72
  (1 shorter events, 0.0 us)
Async XLA Ops:
  7.2 176.3 %copy-start = (bf16[1,8192,192]{1,2,0:T(8,128)(2,1)S(1)}, bf16[1,8192,192]{1,2,0:T(8,128)(2,1)}, u32[]{:S(2)}) copy-start(bf16[1,8192,192]{1,2,0:T(8,128)(2,1)} %param.16) | copy-start | bytes 9437188
  7.2 301.3 %all-gather.5.cloned.1.call-start = ((), (), s32[]{:S(2)}) async-start(), calls=%async_computation.5 | async-start | bytes 2228224 | tf_op jit(solution)/shard_map/all_gather | solution.py:146
  183.5 3.0 copy-start.2
  183.5 3.4 copy-start.1
  259.2 5.3 %copy-start.3 = (bf16[128,512]{1,0:T(8,128)(2,1)S(1)}, bf16[128,512]{1,0:T(8,128)(2,1)}, u32[]{:S(2)}) copy-start(bf16[128,512]{1,0:T(8,128)(2,1)} %param.13) | copy-start | bytes 393220
  259.2 5.3 %copy-start.4 = (bf16[128,512]{1,0:T(8,128)(2,1)S(1)}, bf16[128,512]{1,0:T(8,128)(2,1)}, u32[]{:S(2)}) copy-start(bf16[128,512]{1,0:T(8,128)(2,1)} %param.12) | copy-start | bytes 393220
  259.2 7.8 %copy-start.5 = (s32[2048]{0:T(1024)S(1)}, s32[2048]{0:T(1024)}, u32[]{:S(2)}) copy-start(s32[2048]{0:T(1024)} %param.19) | copy-start | bytes 24580
  266.3 85.1 %all-gather.3.cloned.1.call-start = ((), (), s32[]{:S(2)}) async-start(), calls=%async_computation.4 | async-start | bytes 2228224 | tf_op jit(solution)/shard_map/all_gather | solution.py:147
  267.2 13.2 %all-to-all-start.2 = ((bf16[16,8,512]{2,1,0:T(8,128)(2,1)}), bf16[16,8,512]{2,1,0:T(8,128)(2,1)S(1)}, u32[]{:S(2)}, u32[]{:S(2)}) async-start(bf16[16,8,512]{2,1,0:T(8,128)(2,1)} %bitcast.238), calls=%async_computation.2 | async-start | bytes 262144 | tf_op jit(solution)/shard_map/all_to_all | solution.py:127
  280.4 11.6 %all-to-all-start.3 = ((bf16[16,8,512]{2,1,0:T(8,128)(2,1)}), bf16[16,8,512]{2,1,0:T(8,128)(2,1)S(1)}, u32[]{:S(2)}, u32[]{:S(2)}) async-start(bf16[16,8,512]{2,1,0:T(8,128)(2,1)} %bitcast.237), calls=%async_computation.3 | async-start | bytes 262144 | tf_op jit(solution)/shard_map/all_to_all | solution.py:134
Sparse Core Ops, SparseCore 0:
  266.4 41.9 all-gather.4
  311.2 40.1 all-gather.2
where the time goes:
time: 386 us; the launch traced here: 385 us
  blocking collectives  164 us (42%)
  local copies, waits for them, and re-layouts  102 us (26%)
  waiting for transfers between devices  52.1 us (13%)
  matrix products  33.4 us (9%)
  between operations  14.2 us (4%)
  other arithmetic  10.6 us (3%)
  starting transfers between devices  8.91 us (2%)
    all_to_all x1, blocking collectives, local(): lax.all_to_all(outgoing, 'seq', split_axis=0, concat_axis=0, tiled=True)  99.9 us
    scatter x2, local copies, waits for them, and re-layouts, local(): jnp.zeros((devices, capacity, width), jnp.bfloat16).at[owners, places]  68.2 us
    all_to_all x1, blocking collectives, local(): lax.all_to_all(reduced_projection(lax.all_to_all(outgoing, 'seq', split_a...  63.9 us
    all_gather x1, waiting for transfers between devices, local(): lax.all_gather(values_here, 'seq', axis=0, tiled=True)  24.8 us
    all_gather x1, waiting for transfers between devices, local(): lax.all_gather(keys_here, 'seq', axis=0, tiled=True)  16.4 us
    dot_general x4, matrix products, attend(): jnp.einsum('jts,sd->tjd', weights, value_head_layout[:, grouped_heads], p...  16 us
    sub x4, matrix products, attend(): raised = jnp.exp(scores - largest)  13.4 us
  transfers between devices with their start and end apart: 4, of which 4 were waited for; matrix products, arithmetic and copies ran while one was open for 6% of the time, Pallas kernels for 0%

commit v1 on v0

v1 whole, which is shorter than its diff:
```python
import functools
import math

import jax
import jax.numpy as jnp
from jax import lax
from jax.experimental import pallas as pl
from jax.experimental.pallas import tpu as pltpu
from jax.sharding import PartitionSpec as P

KEY_VALUE_HEADS = 4
HEAD_SIZE = 128
SUBLANES = 8
PLANE = 4
VMEM_BYTES = 48 * 1024 * 1024


def params(**kw):
    return pltpu.CompilerParams(vmem_limit_bytes=VMEM_BYTES, **kw)


def f32_dot(a, b):
    return jnp.dot(a, b, preferred_element_type=jnp.float32)


def lane_iota(shape):
    return lax.broadcasted_iota(jnp.int32, shape, 1)


def row_iota(shape):
    return lax.broadcasted_iota(jnp.int32, shape, 0)


def place_tokens(adapter, table_ref, stores):
    count = adapter.shape[0]
    rows, lanes = row_iota((count, count)), lane_iota((count, count))
    as_row = jnp.sum(jnp.where(rows == lanes, adapter, 0.0), axis=0, keepdims=True)
    same = adapter == as_row
    place_col = jnp.sum(jnp.where(same & (lanes < rows), 1.0, 0.0), axis=1, keepdims=True)
    place_row = jnp.sum(jnp.where(same & (rows < lanes), 1.0, 0.0), axis=0, keepdims=True)

    def owner(ids):
        result = jnp.zeros_like(ids)
        for k in range(stores):
            result = jnp.where(ids == float(k), table_ref[k].astype(jnp.float32), result)
        return result

    out = []
    for ids, place in ((adapter, place_col), (as_row, place_row)):
        block = jnp.floor(place * (1.0 / SUBLANES))
        out.append((owner(ids) * SUBLANES + place - block * SUBLANES, block))
    return out


def dispatch_kernel(full, fold, per_width, stores, adapter_ref, table_ref, a_ref, b_ref, x_ref, ids_ref, row_scr):
    step = pl.program_id(0)
    tokens = adapter_ref.shape[0]
    rows = x_ref.shape[0]

    @pl.when(step == 0)
    def _():
        cols, lanes = place_tokens(adapter_ref[...].astype(jnp.float32), table_ref, stores)
        lane = lane_iota((tokens, 128))
        ids_ref[...] = jnp.where(lane == 0, cols[0], jnp.where(lane == 1, cols[1], 0.0)).astype(jnp.int32)
        row_scr[0:1, :] = lanes[0]
        row_scr[1:2, :] = lanes[1]

    at = row_scr[0:1, :].astype(jnp.int32)
    block = row_scr[1:2, :].astype(jnp.int32)
    target = row_iota((rows, tokens))

    if full:

        @pl.when(step < full * per_width)
        def _():
            pick = ((at == target) & (block == step // per_width)).astype(jnp.bfloat16)
            x_ref[...] = f32_dot(pick, a_ref[...]).astype(jnp.bfloat16)

    if fold:

        @pl.when(step >= full * per_width)
        def _():
            low = ((at == target) & (block == full)).astype(jnp.bfloat16)
            high = ((at + 4 == target) & (block == full)).astype(jnp.bfloat16)
            x_ref[...] = (f32_dot(low, a_ref[...]) + f32_dot(high, b_ref[...])).astype(jnp.bfloat16)


def dispatch(normed, token_adapter, table, full, fold):
    tokens, width = normed.shape
    stores = table.shape[0]
    column = width // 4
    per_width, half = width // column, width // 2 // column
    steps = full * per_width + fold * half

    def a_map(i):
        return (0, jnp.where(i < full * per_width, i % per_width, i - full * per_width))

    def b_map(i):
        return (0, jnp.where(i < full * per_width, half, i - full * per_width + half))

    return pl.pallas_call(
        functools.partial(dispatch_kernel, full, fold, per_width, stores),
        grid=(steps,),
        in_specs=[
            pl.BlockSpec((tokens, 1), lambda i: (0, 0)),
            pl.BlockSpec(memory_space=pltpu.SMEM),
            pl.BlockSpec((tokens, column), a_map),
            pl.BlockSpec((tokens, column), b_map),
        ],
        out_specs=[
            pl.BlockSpec((stores * SUBLANES, column), lambda i: (0, i)),
            pl.BlockSpec((tokens, 128), lambda i: (0, 0)),
        ],
        out_shape=[
            jax.ShapeDtypeStruct((stores * SUBLANES, steps * column), jnp.bfloat16),
            jax.ShapeDtypeStruct((tokens, 128), jnp.int32),
        ],
        scratch_shapes=[pltpu.VMEM((8, tokens), jnp.float32)],
        compiler_params=params(),
        name="dispatch",
    )(token_adapter, table, normed, normed)


def project_kernel(full, fold, steps, *refs):
    refs = list(refs)
    low_refs = [(refs.pop(0), refs.pop(0)) for _ in range(full)]
    fold_ref = refs.pop(0) if fold else None
    down_low, down_high, up_query, up_kv, dkv_ref, dq_ref, acc = refs
    step = pl.program_id(0)
    rank = up_query.shape[1]

    @pl.when(step == 0)
    def _():
        acc[...] = jnp.zeros_like(acc)

    low, high = down_low[0], down_high[0]
    for b, (x_low, x_high) in enumerate(low_refs):
        acc[b] += f32_dot(x_low[...], low) + f32_dot(x_high[...], high)
    if fold:
        acc[full] += f32_dot(fold_ref[...], low)
        acc[full + 1] += f32_dot(fold_ref[...], high)

    @pl.when(step == steps - 1)
    def _():
        kv_width, query_width = up_kv.shape[3], up_query.shape[2]
        for b in range(full):
            shrunk = acc[b].astype(jnp.bfloat16)
            at = b * 2 * kv_width
            for i in range(2):
                piece = shrunk[:, (i + 1) * rank : (i + 2) * rank]
                dkv_ref[:, at + i * kv_width : at + (i + 1) * kv_width] = f32_dot(piece, up_kv[0, i]).astype(jnp.bfloat16)
            dq_ref[:, b * query_width : (b + 1) * query_width] = f32_dot(shrunk[:, :rank], up_query[0]).astype(jnp.bfloat16)
        if fold:
            rows = acc.shape[1]
            upper = (row_iota((rows, 1)) % SUBLANES) >= 4
            mixed = jnp.where(upper, acc[full + 1], acc[full]).reshape(rows // SUBLANES, SUBLANES, 3 * rank)
            both = mixed + jnp.concatenate([mixed[:, 4:], mixed[:, :4]], axis=1)
            shrunk = both.reshape(rows, 3 * rank).astype(jnp.bfloat16)
            delta = [f32_dot(shrunk[:, (i + 1) * rank : (i + 2) * rank], up_kv[0, i]) for i in range(2)]
            dkv_ref[:, full * 2 * kv_width :] = jnp.where(upper, delta[1], delta[0]).astype(jnp.bfloat16)
            half = query_width // 2
            piece = shrunk[:, :rank]
            delta = [f32_dot(piece, up_query[0, :, i * half : (i + 1) * half]) for i in range(2)]
            dq_ref[:, full * query_width :] = jnp.where(upper, delta[1], delta[0]).astype(jnp.bfloat16)


def project(x, down, up_query, up_kv, full, fold):
    rows = x.shape[0]
    _, width, ranks = down.shape
    column = width // 8
    steps = width // 2 // column
    query_width, kv_width = up_query.shape[2], up_kv.shape[3]
    in_specs = []
    for b in range(full):
        in_specs.append(pl.BlockSpec((rows, column), lambda i, b=b: (0, 2 * b * steps + i)))
        in_specs.append(pl.BlockSpec((rows, column), lambda i, b=b: (0, (2 * b + 1) * steps + i)))
    if fold:
        in_specs.append(pl.BlockSpec((rows, column), lambda i: (0, 2 * full * steps + i)))
    blocks = len(in_specs)
    in_specs += [
        pl.BlockSpec((1, column, ranks), lambda i: (0, i, 0)),
        pl.BlockSpec((1, column, ranks), lambda i: (0, steps + i, 0)),
        pl.BlockSpec(up_query.shape, lambda i: (0, 0, 0)),
        pl.BlockSpec(up_kv.shape, lambda i: (0, 0, 0, 0)),
    ]
    shapes = [
        (rows, (2 * full + fold) * kv_width),
        (rows, full * query_width + fold * query_width // 2),
    ]
    return pl.pallas_call(
        functools.partial(project_kernel, full, fold, steps),
        grid=(steps,),
        in_specs=in_specs,
        out_specs=[pl.BlockSpec(s, lambda i: (0, 0)) for s in shapes],
        out_shape=[jax.ShapeDtypeStruct(s, jnp.bfloat16) for s in shapes],
        scratch_shapes=[pltpu.VMEM((full + 2 * fold, rows, ranks), jnp.float32)],
        compiler_params=params(),
        name="project",
    )(*([x] * blocks), down, down, up_query, up_kv)


def picks(ids, rows, block, shift):
    at, blocks = ids[:, 0:1], ids[:, 1:2]
    return ((at + shift == lane_iota((ids.shape[0], rows))) & (blocks == block)).astype(jnp.bfloat16)


def correct_kernel(full, fold, ids_ref, dkv_ref, sk_ref, sv_ref, k_ref, v_ref, kv_ref):
    rows = dkv_ref.shape[0]
    width = sk_ref.shape[1]
    ids = ids_ref[...]
    total = [None, None]
    for i in range(2):
        for b in range(full):
            at = (2 * b + i) * width
            term = f32_dot(picks(ids, rows, b, 0), dkv_ref[:, at : at + width])
            total[i] = term if total[i] is None else total[i] + term
        if fold:
            term = f32_dot(picks(ids, rows, full, 4 * i), dkv_ref[:, 2 * full * width :])
            total[i] = term if total[i] is None else total[i] + term
    keys = (sk_ref[...].astype(jnp.float32) + total[0]).astype(jnp.bfloat16)
    values = (sv_ref[...].astype(jnp.float32) + total[1]).astype(jnp.bfloat16)
    k_ref[...] = keys
    v_ref[...] = values
    kv_ref[:, :width] = keys
    kv_ref[:, width:] = values


def correct(ids, dkv, shared_keys, shared_values, full, fold):
    rows, width = shared_keys.shape
    one = jax.ShapeDtypeStruct((rows, width), jnp.bfloat16)
    return pl.pallas_call(
        functools.partial(correct_kernel, full, fold),
        out_shape=[one, one, jax.ShapeDtypeStruct((rows, 2 * width), jnp.bfloat16)],
        compiler_params=params(),
        name="correct",
    )(ids, dkv, shared_keys, shared_values)


def window_chunks(kv, devices, reach):
    planes = reach // PLANE
    chunks = [(0, 0, kv)]
    for back in range(1, planes + 1):
        hop = back * PLANE
        chunks.append((back, 0, lax.ppermute(kv, "seq", [(i, i + hop) for i in range(devices - hop)])))
    bit = PLANE // 2
    while bit:
        swap = [(i, i ^ bit) for i in range(devices)]
        chunks = chunks + [(back, mark ^ bit, lax.ppermute(rows, "seq", swap)) for back, mark, rows in chunks]
        bit //= 2
    return chunks


def attend_kernel(full, fold, reach, tags, *refs):
    refs = list(refs)
    me_ref, ids_ref, request_ref, sq_ref = (refs.pop(0) for _ in range(4))
    dq_refs = [refs.pop(0) for _ in range(full + fold)]
    chunk_refs = [(refs.pop(0), refs.pop(0)) for _ in tags]
    out_ref, bias, keys, values, query = refs
    head = pl.program_id(0)
    me = me_ref[0]
    tokens = sq_ref.shape[0]
    here = reach * tokens

    @pl.when(head == 0)
    def _():
        rows, lanes = row_iota((tokens, tokens)), lane_iota((tokens, tokens))
        own = request_ref[pl.ds(me, 1), :].astype(jnp.float32)
        own = jnp.sum(jnp.where(rows == lanes, own, 0.0), axis=1, keepdims=True)
        for at in range(reach + 1):
            source = me - reach + at
            theirs = request_ref[pl.ds(jnp.maximum(source, 0), 1), :].astype(jnp.float32)
            theirs = jnp.where(source >= 0, theirs, -1.0)
            allowed = own == theirs
            if at == reach:
                allowed = allowed & (lanes <= rows)
            bias[:, at * tokens : (at + 1) * tokens] = jnp.where(allowed, 0.0, -1e30)

    zeros = jnp.zeros((tokens, HEAD_SIZE), jnp.bfloat16)
    for at in range(reach):

        @pl.when(me - reach + at < 0)
        def _(at=at):
            keys[at * tokens : (at + 1) * tokens, :] = zeros
            values[at * tokens : (at + 1) * tokens, :] = zeros

    for (back, mark), (k_ref, v_ref) in zip(tags, chunk_refs):
        source = (me // PLANE - back) * PLANE + jnp.bitwise_xor(me % PLANE, mark)
        at = source - me + reach

        @pl.when((source >= 0) & (at >= 0) & (at <= reach))
        def _(at=at, k_ref=k_ref, v_ref=v_ref):
            place = pl.ds(pl.multiple_of(at * tokens, tokens), tokens)
            keys[place, :] = k_ref[...]
            values[place, :] = v_ref[...]

    ids = ids_ref[...]
    slots = dq_refs[0].shape[0]
    delta = sq_ref[...].astype(jnp.float32)
    correction = None
    for b in range(full):
        term = f32_dot(picks(ids, slots, b, 0), dq_refs[b][...])
        correction = term if correction is None else correction + term
    if fold:
        shift = 4 * (head // (KEY_VALUE_HEADS // 2))
        term = f32_dot(picks(ids, slots, full, shift), dq_refs[full][...])
        correction = term if correction is None else correction + term
    query[...] = (delta + correction).astype(jnp.bfloat16)

    scale = 1.0 / math.sqrt(HEAD_SIZE)
    for j in range(sq_ref.shape[1] // HEAD_SIZE):
        span = slice(j * HEAD_SIZE, (j + 1) * HEAD_SIZE)
        scores = lax.dot_general(
            query[:, span], keys[...], (((1,), (1,)), ((), ())), preferred_element_type=jnp.float32
        )
        scores = scores * scale + bias[...]
        raised = jnp.exp(scores - jnp.max(scores, axis=1, keepdims=True))
        total = jnp.sum(raised, axis=1, keepdims=True)
        blended = f32_dot(raised.astype(jnp.bfloat16), values[...])
        out_ref[:, span] = (blended / total).astype(jnp.bfloat16)


def attend(me, ids, requests, shared_query, dq, chunks, full, fold, reach):
    tokens, query_width = shared_query.shape
    slots = dq.shape[0]
    block = query_width // KEY_VALUE_HEADS
    in_specs = [
        pl.BlockSpec(memory_space=pltpu.SMEM),
        pl.BlockSpec(ids.shape, lambda g: (0, 0)),
        pl.BlockSpec(requests.shape, lambda g: (0, 0)),
        pl.BlockSpec((tokens, block), lambda g: (0, g)),
    ]
    for b in range(full):
        in_specs.append(pl.BlockSpec((slots, block), lambda g, b=b: (0, b * KEY_VALUE_HEADS + g)))
    if fold:
        in_specs.append(
            pl.BlockSpec((slots, block), lambda g: (0, full * KEY_VALUE_HEADS + g % (KEY_VALUE_HEADS // 2)))
        )
    operands = [me, ids, requests, shared_query] + [dq] * (full + fold)
    for _, _, rows in chunks:
        in_specs.append(pl.BlockSpec((tokens, HEAD_SIZE), lambda g: (0, g)))
        in_specs.append(pl.BlockSpec((tokens, HEAD_SIZE), lambda g: (0, KEY_VALUE_HEADS + g)))
        operands += [rows, rows]
    window = (reach + 1) * tokens
    return pl.pallas_call(
        functools.partial(attend_kernel, full, fold, reach, tuple((b, m) for b, m, _ in chunks)),
        grid=(KEY_VALUE_HEADS,),
        in_specs=in_specs,
        out_specs=pl.BlockSpec((tokens, block), lambda g: (0, g)),
        out_shape=jax.ShapeDtypeStruct((tokens, query_width), jnp.bfloat16),
        scratch_shapes=[
            pltpu.VMEM((tokens, window), jnp.float32),
            pltpu.VMEM((window, HEAD_SIZE), jnp.bfloat16),
            pltpu.VMEM((window, HEAD_SIZE), jnp.bfloat16),
            pltpu.VMEM((tokens, block), jnp.bfloat16),
        ],
        compiler_params=params(),
        name="attend",
    )(*operands)


def exchange(rows, devices):
    width = rows.shape[1]
    out = lax.all_to_all(
        rows.reshape(devices, rows.shape[0] // devices, width), "seq", split_axis=0, concat_axis=0, tiled=True
    )
    return out.reshape(rows.shape)


def local(
    normed,
    shared_query_rows,
    shared_key_rows,
    shared_value_rows,
    token_adapter,
    adapter_slot_table,
    adapter_down_factors,
    adapter_up_query,
    adapter_up_key_value,
    token_request,
):
    tokens = normed.shape[0]
    devices = lax.axis_size("seq")
    reach = devices // 2
    most = max(2, 3 * tokens // (2 * devices))
    fours = -(-most // 4)
    full, fold = fours // 2, fours % 2

    outgoing, ids = dispatch(normed, token_adapter, adapter_slot_table, full, fold)
    incoming = exchange(outgoing, devices)
    dkv, dq = project(incoming, adapter_down_factors, adapter_up_query, adapter_up_key_value, full, fold)
    dkv = exchange(dkv, devices)
    keys, values, kv = correct(ids, dkv, shared_key_rows, shared_value_rows, full, fold)
    dq = exchange(dq, devices)
    chunks = window_chunks(kv, devices, reach)
    key_cache = exchange(keys, devices)
    value_cache = exchange(values, devices)
    me = lax.axis_index("seq").astype(jnp.int32).reshape(1)
    attention = attend(
        me, ids, token_request.reshape(devices, tokens), shared_query_rows, dq, chunks, full, fold, reach
    )
    return (attention, key_cache, value_cache)


def solution(mesh):
    rows = P(("groups", "seq"), None)
    return jax.shard_map(
        local,
        mesh=mesh,
        in_specs=(
            rows,
            rows,
            rows,
            rows,
            rows,
            P(),
            P("seq", None, None),
            P("seq", None, None),
            P("seq", None, None, None),
            P("groups"),
        ),
        out_specs=(rows, rows, rows),
        check_vma=False,
    )
```

time: 386 us -> 219 us (0.57)
  the two profiles are of different devices: /device:TPU:0 before, /device:TPU:17 now
where the time goes in v1:
time: 219 us
  waiting for transfers between devices  113 us (52%)
  blocking collectives  37.3 us (17%)
  Pallas kernels  26.9 us (12%)
  starting transfers between devices  25.1 us (11%)
  local copies, waits for them, and re-layouts  15.8 us (7%)
    all_to_all x2, waiting for transfers between devices, exchange(): lax.all_to_all(rows.reshape(devices, rows.shape[0] // devices, width), 's...  63.7 us
    ppermute x2, waiting for transfers between devices, window_chunks(): lax.ppermute(kv, 'seq', [(i, i + hop) for i in range(devices - hop)])  44.1 us
    all_to_all x3, blocking collectives, exchange(): lax.all_to_all(rows.reshape(devices, rows.shape[0] // devices, width), 's...  37.3 us
    pallas_call x1, Pallas kernels, attend(): pl.pallas_call(functools.partial(attend_kernel, full, fold, reach, tuple(...  17.9 us
    unnamed x32, local copies, waits for them, and re-layouts  15.8 us
    all_to_all x2, starting transfers between devices, exchange(): lax.all_to_all(rows.reshape(devices, rows.shape[0] // devices, width), 's...  12.7 us
    ppermute x9, starting transfers between devices, window_chunks(): lax.ppermute(rows, 'seq', swap)  8.01 us
    pallas_call x1, Pallas kernels, project(): pl.pallas_call(functools.partial(project_kernel, full, fold, steps), grid...  5.07 us
  transfers between devices with their start and end apart: 13, of which 5 were waited for; matrix products, arithmetic and copies ran while one was open for 3% of the time, Pallas kernels for 0%

profile of v1, /device:TPU:17, one launch (start us, length us, event | category | flops | bytes accessed | tf_op | source)
XLA Modules:
  0.0 218.7 jit_solution(5468319467426394654)
XLA Ops:
  0.6 0.8 copy.13.adapter_ref
  1.4 0.0 copy-start
  1.4 1.6 copy-done
  3.0 0.0 copy-start.11
  3.0 0.7 copy-done.11
  3.6 3.5 %dispatch.1 = (bf16[128,12288]{1,0:T(8,128)(2,1)S(1)}, s32[128,128]{1,0:T(8,128)S(1)}) custom-call(s32[128,1]{1,0:T(8,128)S(1)} %copy.13.adapter_ref, s32[16]{0:T(128)S(1)} %copy-done.11, bf16[128,8192]{1,0:T(8,128)(2,1)S(1)} %copy-done, bf16[128,8192]{1,0:T(8,128)(2,1)S(1)} %copy-done), custom_call_target="tpu_custom_call" | custom-call | tf_op jit(solution)/shard_map/dispatch/pallas_call | solution.py:101
  7.2 0.0 copy-start.1
  7.2 1.7 copy-done.1
  8.8 6.5 %all-to-all-start = ((bf16[16,8,12288]{2,1,0:T(8,128)(2,1)}), bf16[16,8,12288]{2,1,0:T(8,128)(2,1)S(1)}, u32[]{:S(2)}, u32[]{:S(2)}) async-start(bf16[16,8,12288]{2,1,0:T(8,128)(2,1)} %bitcast.17), calls=%async_computation | async-start | bytes 6291456 | tf_op jit(solution)/shard_map/all_to_all | solution.py:363
  15.4 0.0 copy-start.7
  15.4 5.9 %copy.14.refs_3_.refs_4_ = bf16[1,8192,192]{2,1,0:T(8,128)(2,1)} copy(bf16[1,8192,192]{1,2,0:T(8,128)(2,1)} %param.16) | data formatting | bytes 6291456 | tf_op args[6]
  21.3 63.7 %all-to-all-done = bf16[16,8,12288]{2,1,0:T(8,128)(2,1)S(1)} async-done(((bf16[16,8,12288]{2,1,0:T(8,128)(2,1)}), bf16[16,8,12288]{2,1,0:T(8,128)(2,1)S(1)}, u32[]{:S(2)}, u32[]{:S(2)}) %all-to-all-start) | async-done | bytes 3145760 | tf_op jit(solution)/shard_map/all_to_all | solution.py:363
  85.0 0.0 copy-done.7
  85.0 0.0 copy-start.6
  85.0 1.0 copy-done.6
  86.0 0.0 copy-start.8
  86.0 0.0 copy-start.9
  86.0 5.1 %project.1 = (bf16[128,1536]{1,0:T(8,128)(2,1)S(1)}, bf16[128,6144]{1,0:T(8,128)(2,1)S(1)}) custom-call(bf16[128,12288]{1,0:T(8,128)(2,1)S(1)} %bitcast.12, bf16[128,12288]{1,0:T(8,128)(2,1)S(1)} %bitcast.13, bf16[128,12288]{1,0:T(8,128)(2,1)S(1)} %bitcast.14, bf16[1,8192,192]{2,1,0:T(8,128)(2,1)} %copy.14.refs_3_.refs_4_, ...), custom_call_target="tpu_custom_call" | custom-call | tf_op jit(solution)/shard_map/project/pallas_call | solution.py:190
  91.1 0.0 copy-start.2
  91.1 1.2 copy-done.2
  92.3 0.0 copy-start.3
  92.3 0.0 copy-start.10
  92.3 15.6 %all_to_all.25 = bf16[16,8,1536]{2,1,0:T(8,128)(2,1)S(1)} all-to-all(bf16[16,8,1536]{2,1,0:T(8,128)(2,1)S(1)} %bitcast.20), channel_id=1, replica_groups=mesh['groups'=2,'seq'=16] {'seq'}, dimensions={0} | all-to-all | bytes 786432 | tf_op jit(solution)/shard_map/all_to_all | solution.py:363
  107.9 0.0 copy-done.8
  107.9 0.0 copy-done.9
  107.9 0.4 correct.1
  108.2 10.6 %all_to_all.26 = bf16[16,8,512]{2,1,0:T(8,128)(2,1)} all-to-all(bf16[16,8,512]{2,1,0:T(8,128)(2,1)S(1)} %bitcast.22), channel_id=1, replica_groups=mesh['groups'=2,'seq'=16] {'seq'}, dimensions={0} | all-to-all | bytes 262144 | tf_op jit(solution)/shard_map/all_to_all | solution.py:363
  118.8 11.1 %all_to_all.27 = bf16[16,8,512]{2,1,0:T(8,128)(2,1)} all-to-all(bf16[16,8,512]{2,1,0:T(8,128)(2,1)S(1)} %bitcast.21), channel_id=1, replica_groups=mesh['groups'=2,'seq'=16] {'seq'}, dimensions={0} | all-to-all | bytes 262144 | tf_op jit(solution)/shard_map/all_to_all | solution.py:363
  130.0 6.2 %all-to-all-start.1 = ((bf16[16,8,6144]{2,1,0:T(8,128)(2,1)}), bf16[16,8,6144]{2,1,0:T(8,128)(2,1)S(1)}, u32[]{:S(2)}, u32[]{:S(2)}) async-start(bf16[16,8,6144]{2,1,0:T(8,128)(2,1)} %bitcast.18), calls=%async_computation.1 | async-start | bytes 3145728 | tf_op jit(solution)/shard_map/all_to_all | solution.py:363
  136.2 1.3 collective-permute-start.1
  137.4 3.1 %collective-permute-start = (bf16[128,1024]{1,0:T(8,128)(2,1)S(1)}, bf16[128,1024]{1,0:T(8,128)(2,1)S(1)}, u32[]{:S(2)}, u32[]{:S(2)}) collective-permute-start(bf16[128,1024]{1,0:T(8,128)(2,1)S(1)} %get-tuple-element.14.refs_6_.refs_7_), channel_id=1, source_target_pairs={{0,4},{1,5},{2,6},{3,7},{4,8},{5,9},{6,10},{7,11},{8,12},{9,13},{1... | collective-permute-start | bytes 786440 | tf_op jit(solution)/shard_map/ppermute | solution.py:244
  140.6 1.3 collective-permute-start.2
  141.8 0.9 collective-permute-start.5
  142.8 25.8 %collective-permute-done.1.refs_10_.refs_11_ = bf16[128,1024]{1,0:T(8,128)(2,1)S(1)} collective-permute-done((bf16[128,1024]{1,0:T(8,128)(2,1)S(1)}, bf16[128,1024]{1,0:T(8,128)(2,1)S(1)}, u32[]{:S(2)}, u32[]{:S(2)}) %collective-permute-start.1) | collective-permute-done | bytes 262176 | tf_op jit(solution)/shard_map/ppermute | solution.py:244
  168.5 1.3 collective-permute-start.4
  169.8 18.4 %collective-permute-done.refs_8_.refs_9_ = bf16[128,1024]{1,0:T(8,128)(2,1)S(1)} collective-permute-done((bf16[128,1024]{1,0:T(8,128)(2,1)S(1)}, bf16[128,1024]{1,0:T(8,128)(2,1)S(1)}, u32[]{:S(2)}, u32[]{:S(2)}) %collective-permute-start) | collective-permute-done | bytes 262176 | tf_op jit(solution)/shard_map/ppermute | solution.py:244
  188.2 1.1 collective-permute-start.3
  189.3 1.2 collective-permute-start.6
  190.4 0.0 collective-permute-done.2.refs_12_.refs_13_
  190.4 0.0 collective-permute-start.7
  190.4 0.0 collective-permute-done.5.refs_18_.refs_19_
  190.4 0.0 copy-start.4
  190.5 0.7 copy-done.4
  191.1 0.5 collective-permute-start.8
  191.6 0.0 collective-permute-done.4.refs_16_.refs_17_
  191.7 0.0 collective-permute-start.10
  191.7 3.5 %collective-permute-done.3.refs_14_.refs_15_ = bf16[128,1024]{1,0:T(8,128)(2,1)} collective-permute-done((bf16[128,1024]{1,0:T(8,128)(2,1)S(1)}, bf16[128,1024]{1,0:T(8,128)(2,1)}, u32[]{:S(2)}, u32[]{:S(2)}) %collective-permute-start.3) | collective-permute-done | bytes 262176 | tf_op jit(solution)/shard_map/ppermute | solution.py:248
  195.2 1.8 collective-permute-start.9
  197.0 0.0 collective-permute-done.6.refs_20_.refs_21_
  197.0 0.0 collective-permute-done.7.refs_22_.refs_23_
  197.0 0.0 collective-permute-done.8.refs_24_.refs_25_
  197.0 0.0 collective-permute-done.10.refs_28_.refs_29_
  197.0 1.5 collective-permute-done.9.refs_26_.refs_27_
  198.5 0.0 all-to-all-done.1
  198.5 0.0 copy-done.3
  198.5 0.0 copy-done.10
  198.5 0.0 copy-start.5
  198.5 0.9 copy-done.5
  199.4 0.0 copy-start.12
  199.5 17.9 %attend.1 = bf16[128,4096]{1,0:T(8,128)(2,1)} custom-call(s32[1]{0:T(128)} %bitcast.refs_0_, s32[128,128]{1,0:T(8,128)S(1)} %get-tuple-element.10.ids_ref.refs_1_, s32[16,128]{1,0:T(8,128)S(1)} %bitcast.23, bf16[128,4096]{1,0:T(8,128)(2,1)S(1)} %copy-done.3, bf16[128,6144]{1,0:T(8,128)(2,1)S(1)} %bitcast.15, bf16[128,6144]{1,0:T(8,128)(2,1)S(1)} %bitcast.16, ...), custom_call_target="tpu_custom_call" | custom-call | tf_op jit(solution)/shard_map/attend/pallas_call | solution.py:344
  217.4 0.0 copy-done.12
  217.4 0.7 copy.18
  218.1 0.0 copy-done.13
  218.1 0.7 copy.19
  (1 shorter events, 0.0 us)
Async XLA Ops:
  1.4 1.6 copy-start
  3.0 0.7 copy-start.11
  7.2 1.7 copy-start.1
  8.8 76.1 %all-to-all-start = ((bf16[16,8,12288]{2,1,0:T(8,128)(2,1)}), bf16[16,8,12288]{2,1,0:T(8,128)(2,1)S(1)}, u32[]{:S(2)}, u32[]{:S(2)}) async-start(bf16[16,8,12288]{2,1,0:T(8,128)(2,1)} %bitcast.17), calls=%async_computation | async-start | bytes 6291456 | tf_op jit(solution)/shard_map/all_to_all | solution.py:363
  15.4 69.6 %copy-start.7 = (bf16[1,2,64,512]{3,2,1,0:T(8,128)(2,1)S(1)}, bf16[1,2,64,512]{3,2,1,0:T(8,128)(2,1)}, u32[]{:S(2)}) copy-start(bf16[1,2,64,512]{3,2,1,0:T(8,128)(2,1)} %refs_6_.1) | copy-start | bytes 393220
  85.0 1.0 copy-start.6
  86.0 21.9 %copy-start.8 = (bf16[128,512]{1,0:T(8,128)(2,1)S(1)}, bf16[128,512]{1,0:T(8,128)(2,1)}, u32[]{:S(2)}) copy-start(bf16[128,512]{1,0:T(8,128)(2,1)} %sk_ref.1) | copy-start | bytes 393220
  86.0 21.9 %copy-start.9 = (bf16[128,512]{1,0:T(8,128)(2,1)S(1)}, bf16[128,512]{1,0:T(8,128)(2,1)}, u32[]{:S(2)}) copy-start(bf16[128,512]{1,0:T(8,128)(2,1)} %sv_ref.1) | copy-start | bytes 393220
  91.1 1.2 copy-start.2
  92.3 106.2 %copy-start.3 = (bf16[128,4096]{1,0:T(8,128)(2,1)S(1)}, bf16[128,4096]{1,0:T(8,128)(2,1)}, u32[]{:S(2)}) copy-start(bf16[128,4096]{1,0:T(8,128)(2,1)} %refs_3_.2) | copy-start | bytes 3145732
  92.3 106.2 %copy-start.10 = (s32[2048]{0:T(1024)S(1)}, s32[2048]{0:T(1024)}, u32[]{:S(2)}) copy-start(s32[2048]{0:T(1024)} %param.19) | copy-start | bytes 24580
  130.0 68.5 %all-to-all-start.1 = ((bf16[16,8,6144]{2,1,0:T(8,128)(2,1)}), bf16[16,8,6144]{2,1,0:T(8,128)(2,1)S(1)}, u32[]{:S(2)}, u32[]{:S(2)}) async-start(bf16[16,8,6144]{2,1,0:T(8,128)(2,1)} %bitcast.18), calls=%async_computation.1 | async-start | bytes 3145728 | tf_op jit(solution)/shard_map/all_to_all | solution.py:363
  136.2 32.4 %collective-permute-start.1 = (bf16[128,1024]{1,0:T(8,128)(2,1)S(1)}, bf16[128,1024]{1,0:T(8,128)(2,1)S(1)}, u32[]{:S(2)}, u32[]{:S(2)}) collective-permute-start(bf16[128,1024]{1,0:T(8,128)(2,1)S(1)} %get-tuple-element.14.refs_6_.refs_7_), channel_id=1, source_target_pairs={{0,8},{1,9},{2,10},{3,11},{4,12},{5,13},{6,14},{7,15},{16,24},{17,... | collective-permute-start | bytes 786440 | tf_op jit(solution)/shard_map/ppermute | solution.py:244
  137.4 50.7 %collective-permute-start = (bf16[128,1024]{1,0:T(8,128)(2,1)S(1)}, bf16[128,1024]{1,0:T(8,128)(2,1)S(1)}, u32[]{:S(2)}, u32[]{:S(2)}) collective-permute-start(bf16[128,1024]{1,0:T(8,128)(2,1)S(1)} %get-tuple-element.14.refs_6_.refs_7_), channel_id=1, source_target_pairs={{0,4},{1,5},{2,6},{3,7},{4,8},{5,9},{6,10},{7,11},{8,12},{9,13},{1... | collective-permute-start | bytes 786440 | tf_op jit(solution)/shard_map/ppermute | solution.py:244
  140.6 49.9 %collective-permute-start.2 = (bf16[128,1024]{1,0:T(8,128)(2,1)S(1)}, bf16[128,1024]{1,0:T(8,128)(2,1)}, u32[]{:S(2)}, u32[]{:S(2)}) collective-permute-start(bf16[128,1024]{1,0:T(8,128)(2,1)S(1)} %get-tuple-element.14.refs_6_.refs_7_), channel_id=1, source_target_pairs={{0,2},{1,3},{2,0},{3,1},{4,6},{5,7},{6,4},{7,5},{8,10},{9,11},{10,... | collective-permute-start | bytes 786440 | tf_op jit(solution)/shard_map/ppermute | solution.py:248
  141.8 48.6 %collective-permute-start.5 = (bf16[128,1024]{1,0:T(8,128)(2,1)S(1)}, bf16[128,1024]{1,0:T(8,128)(2,1)S(1)}, u32[]{:S(2)}, u32[]{:S(2)}) collective-permute-start(bf16[128,1024]{1,0:T(8,128)(2,1)S(1)} %get-tuple-element.14.refs_6_.refs_7_), channel_id=1, source_target_pairs={{0,1},{1,0},{2,3},{3,2},{4,5},{5,4},{6,7},{7,6},{8,9},{9,8},{10,11... | collective-permute-start | bytes 786440 | tf_op jit(solution)/shard_map/ppermute | solution.py:248
  168.5 23.1 %collective-permute-start.4 = (bf16[128,1024]{1,0:T(8,128)(2,1)S(1)}, bf16[128,1024]{1,0:T(8,128)(2,1)}, u32[]{:S(2)}, u32[]{:S(2)}) collective-permute-start(bf16[128,1024]{1,0:T(8,128)(2,1)S(1)} %collective-permute-done.1.refs_10_.refs_11_), channel_id=1, source_target_pairs={{0,2},{1,3},{2,0},{3,1},{4,6},{5,7},{6,4},{7,5},{8,10},{9,11},{10,... | collective-permute-start | bytes 786440 | tf_op jit(solution)/shard_map/ppermute | solution.py:248
  188.2 7.1 %collective-permute-start.3 = (bf16[128,1024]{1,0:T(8,128)(2,1)S(1)}, bf16[128,1024]{1,0:T(8,128)(2,1)}, u32[]{:S(2)}, u32[]{:S(2)}) collective-permute-start(bf16[128,1024]{1,0:T(8,128)(2,1)S(1)} %collective-permute-done.refs_8_.refs_9_), channel_id=1, source_target_pairs={{0,2},{1,3},{2,0},{3,1},{4,6},{5,7},{6,4},{7,5},{8,10},{9,11},{10,... | collective-permute-start | bytes 786440 | tf_op jit(solution)/shard_map/ppermute | solution.py:248
  189.3 7.7 %collective-permute-start.6 = (bf16[128,1024]{1,0:T(8,128)(2,1)S(1)}, bf16[128,1024]{1,0:T(8,128)(2,1)}, u32[]{:S(2)}, u32[]{:S(2)}) collective-permute-start(bf16[128,1024]{1,0:T(8,128)(2,1)S(1)} %collective-permute-done.refs_8_.refs_9_), channel_id=1, source_target_pairs={{0,1},{1,0},{2,3},{3,2},{4,5},{5,4},{6,7},{7,6},{8,9},{9,8},{10,11... | collective-permute-start | bytes 786440 | tf_op jit(solution)/shard_map/ppermute | solution.py:248
  190.4 6.6 %collective-permute-start.7 = (bf16[128,1024]{1,0:T(8,128)(2,1)S(1)}, bf16[128,1024]{1,0:T(8,128)(2,1)}, u32[]{:S(2)}, u32[]{:S(2)}) collective-permute-start(bf16[128,1024]{1,0:T(8,128)(2,1)S(1)} %collective-permute-done.1.refs_10_.refs_11_), channel_id=1, source_target_pairs={{0,1},{1,0},{2,3},{3,2},{4,5},{5,4},{6,7},{7,6},{8,9},{9,8},{10,11... | collective-permute-start | bytes 786440 | tf_op jit(solution)/shard_map/ppermute | solution.py:248
  190.4 0.7 copy-start.4
  191.1 5.8 %collective-permute-start.8 = (bf16[128,1024]{1,0:T(8,128)(2,1)}, bf16[128,1024]{1,0:T(8,128)(2,1)}, u32[]{:S(2)}, u32[]{:S(2)}) collective-permute-start(bf16[128,1024]{1,0:T(8,128)(2,1)} %collective-permute-done.2.refs_12_.refs_13_), channel_id=1, source_target_pairs={{0,1},{1,0},{2,3},{3,2},{4,5},{5,4},{6,7},{7,6},{8,9},{9,8},{10,11... | collective-permute-start | bytes 786440 | tf_op jit(solution)/shard_map/ppermute | solution.py:248
  191.7 5.3 %collective-permute-start.10 = (bf16[128,1024]{1,0:T(8,128)(2,1)}, bf16[128,1024]{1,0:T(8,128)(2,1)}, u32[]{:S(2)}, u32[]{:S(2)}) collective-permute-start(bf16[128,1024]{1,0:T(8,128)(2,1)} %collective-permute-done.4.refs_16_.refs_17_), channel_id=1, source_target_pairs={{0,1},{1,0},{2,3},{3,2},{4,5},{5,4},{6,7},{7,6},{8,9},{9,8},{10,11... | collective-permute-start | bytes 786440 | tf_op jit(solution)/shard_map/ppermute | solution.py:248
  195.2 3.3 %collective-permute-start.9 = (bf16[128,1024]{1,0:T(8,128)(2,1)}, bf16[128,1024]{1,0:T(8,128)(2,1)}, u32[]{:S(2)}, u32[]{:S(2)}) collective-permute-start(bf16[128,1024]{1,0:T(8,128)(2,1)} %collective-permute-done.3.refs_14_.refs_15_), channel_id=1, source_target_pairs={{0,1},{1,0},{2,3},{3,2},{4,5},{5,4},{6,7},{7,6},{8,9},{9,8},{10,11... | collective-permute-start | bytes 786440 | tf_op jit(solution)/shard_map/ppermute | solution.py:248
  198.5 1.0 copy-start.5
  199.4 17.9 %copy-start.12 = (bf16[16,8,512]{2,1,0:T(8,128)(2,1)S(1)}, bf16[16,8,512]{2,1,0:T(8,128)(2,1)}, u32[]{:S(2)}) copy-start(bf16[16,8,512]{2,1,0:T(8,128)(2,1)} %all_to_all.26) | copy-start | bytes 393220
  199.4 18.6 %copy-start.13 = (bf16[16,8,512]{2,1,0:T(8,128)(2,1)S(1)}, bf16[16,8,512]{2,1,0:T(8,128)(2,1)}, u32[]{:S(2)}) copy-start(bf16[16,8,512]{2,1,0:T(8,128)(2,1)} %all_to_all.27) | copy-start | bytes 393220

commit v2 on v1

--- a/solution.py
+++ b/solution.py
@@ -12,11 +12,15 @@
 HEAD_SIZE = 128
 SUBLANES = 8
 PLANE = 4
-VMEM_BYTES = 48 * 1024 * 1024
-
-
-def params(**kw):
-    return pltpu.CompilerParams(vmem_limit_bytes=VMEM_BYTES, **kw)
+MIB = 1024 * 1024
+
+
+def params(mib=40):
+    return pltpu.CompilerParams(vmem_limit_bytes=mib * MIB)
+
+
+def cost(flops, moved):
+    return pl.CostEstimate(flops=flops, bytes_accessed=moved, transcendentals=0)
 
 
 def f32_dot(a, b):
@@ -31,10 +35,10 @@
     return lax.broadcasted_iota(jnp.int32, shape, 0)
 
 
-def place_tokens(adapter, table_ref, stores):
-    count = adapter.shape[0]
+def place_tokens(as_row, table_ref, stores):
+    count = as_row.shape[1]
     rows, lanes = row_iota((count, count)), lane_iota((count, count))
-    as_row = jnp.sum(jnp.where(rows == lanes, adapter, 0.0), axis=0, keepdims=True)
+    adapter = jnp.sum(jnp.where(rows == lanes, as_row, 0.0), axis=1, keepdims=True)
     same = adapter == as_row
     place_col = jnp.sum(jnp.where(same & (lanes < rows), 1.0, 0.0), axis=1, keepdims=True)
     place_row = jnp.sum(jnp.where(same & (rows < lanes), 1.0, 0.0), axis=0, keepdims=True)
@@ -54,7 +58,7 @@
 
 def dispatch_kernel(full, fold, per_width, stores, adapter_ref, table_ref, a_ref, b_ref, x_ref, ids_ref, row_scr):
     step = pl.program_id(0)
-    tokens = adapter_ref.shape[0]
+    tokens = adapter_ref.shape[1]
     rows = x_ref.shape[0]
 
     @pl.when(step == 0)
@@ -102,7 +106,7 @@
         functools.partial(dispatch_kernel, full, fold, per_width, stores),
         grid=(steps,),
         in_specs=[
-            pl.BlockSpec((tokens, 1), lambda i: (0, 0)),
+            pl.BlockSpec((1, tokens), lambda i: (0, 0)),
             pl.BlockSpec(memory_space=pltpu.SMEM),
             pl.BlockSpec((tokens, column), a_map),
             pl.BlockSpec((tokens, column), b_map),
@@ -118,16 +122,16 @@
         scratch_shapes=[pltpu.VMEM((8, tokens), jnp.float32)],
         compiler_params=params(),
         name="dispatch",
-    )(token_adapter, table, normed, normed)
+    )(token_adapter.reshape(1, tokens), table, normed, normed)
 
 
 def project_kernel(full, fold, steps, *refs):
     refs = list(refs)
     low_refs = [(refs.pop(0), refs.pop(0)) for _ in range(full)]
     fold_ref = refs.pop(0) if fold else None
-    down_low, down_high, up_query, up_kv, dkv_ref, dq_ref, acc = refs
+    down_low, down_high, up_kv, dkv_ref, shrunk_ref, acc = refs
     step = pl.program_id(0)
-    rank = up_query.shape[1]
+    rank = up_kv.shape[2]
 
     @pl.when(step == 0)
     def _():
@@ -142,14 +146,14 @@
 
     @pl.when(step == steps - 1)
     def _():
-        kv_width, query_width = up_kv.shape[3], up_query.shape[2]
+        kv_width = up_kv.shape[3]
         for b in range(full):
             shrunk = acc[b].astype(jnp.bfloat16)
             at = b * 2 * kv_width
             for i in range(2):
                 piece = shrunk[:, (i + 1) * rank : (i + 2) * rank]
                 dkv_ref[:, at + i * kv_width : at + (i + 1) * kv_width] = f32_dot(piece, up_kv[0, i]).astype(jnp.bfloat16)
-            dq_ref[:, b * query_width : (b + 1) * query_width] = f32_dot(shrunk[:, :rank], up_query[0]).astype(jnp.bfloat16)
+            shrunk_ref[b] = shrunk[:, :rank]
         if fold:
             rows = acc.shape[1]
             upper = (row_iota((rows, 1)) % SUBLANES) >= 4
@@ -158,18 +162,15 @@
             shrunk = both.reshape(rows, 3 * rank).astype(jnp.bfloat16)
             delta = [f32_dot(shrunk[:, (i + 1) * rank : (i + 2) * rank], up_kv[0, i]) for i in range(2)]
             dkv_ref[:, full * 2 * kv_width :] = jnp.where(upper, delta[1], delta[0]).astype(jnp.bfloat16)
-            half = query_width // 2
-            piece = shrunk[:, :rank]
-            delta = [f32_dot(piece, up_query[0, :, i * half : (i + 1) * half]) for i in range(2)]
-            dq_ref[:, full * query_width :] = jnp.where(upper, delta[1], delta[0]).astype(jnp.bfloat16)
-
-
-def project(x, down, up_query, up_kv, full, fold):
+            shrunk_ref[full] = shrunk[:, :rank]
+
+
+def project(x, down, up_kv, full, fold):
     rows = x.shape[0]
     _, width, ranks = down.shape
     column = width // 8
     steps = width // 2 // column
-    query_width, kv_width = up_query.shape[2], up_kv.shape[3]
+    _, _, rank, kv_width = up_kv.shape
     in_specs = []
     for b in range(full):
         in_specs.append(pl.BlockSpec((rows, column), lambda i, b=b: (0, 2 * b * steps + i)))
@@ -180,23 +181,80 @@
     in_specs += [
         pl.BlockSpec((1, column, ranks), lambda i: (0, i, 0)),
         pl.BlockSpec((1, column, ranks), lambda i: (0, steps + i, 0)),
-        pl.BlockSpec(up_query.shape, lambda i: (0, 0, 0)),
         pl.BlockSpec(up_kv.shape, lambda i: (0, 0, 0, 0)),
     ]
-    shapes = [
-        (rows, (2 * full + fold) * kv_width),
-        (rows, full * query_width + fold * query_width // 2),
-    ]
+    shapes = [(rows, (2 * full + fold) * kv_width), (full + fold, rows, rank)]
     return pl.pallas_call(
         functools.partial(project_kernel, full, fold, steps),
         grid=(steps,),
         in_specs=in_specs,
-        out_specs=[pl.BlockSpec(s, lambda i: (0, 0)) for s in shapes],
+        out_specs=[pl.BlockSpec(s, lambda i, s=s: (0,) * len(s)) for s in shapes],
         out_shape=[jax.ShapeDtypeStruct(s, jnp.bfloat16) for s in shapes],
         scratch_shapes=[pltpu.VMEM((full + 2 * fold, rows, ranks), jnp.float32)],
         compiler_params=params(),
         name="project",
-    )(*([x] * blocks), down, down, up_query, up_kv)
+    )(*([x] * blocks), down, down, up_kv)
+
+
+def expand_kernel(full, fold, shrunk_ref, up_ref, other_ref, out_ref):
+    step = pl.program_id(0)
+    rows = out_ref.shape[0]
+
+    @pl.when(step < full * KEY_VALUE_HEADS)
+    def _():
+        if full:
+            piece = shrunk_ref[jnp.minimum(step // KEY_VALUE_HEADS, full - 1)]
+            out_ref[...] = f32_dot(piece, up_ref[0]).astype(jnp.bfloat16)
+
+    if fold:
+
+        @pl.when(step >= full * KEY_VALUE_HEADS)
+        def _():
+            upper = (row_iota((rows, 1)) % SUBLANES) >= 4
+            piece = shrunk_ref[full]
+            mixed = jnp.where(upper, f32_dot(piece, other_ref[0]), f32_dot(piece, up_ref[0]))
+            out_ref[...] = mixed.astype(jnp.bfloat16)
+
+
+def expand(shrunk, up_query, full, fold, spare):
+    _, rows, rank = shrunk.shape
+    width = up_query.shape[2]
+    block = width // KEY_VALUE_HEADS
+    half = KEY_VALUE_HEADS // 2
+    steps = full * KEY_VALUE_HEADS + fold * half
+    return pl.pallas_call(
+        functools.partial(expand_kernel, full, fold),
+        grid=(steps,),
+        in_specs=[
+            pl.BlockSpec(shrunk.shape, lambda i: (0, 0, 0)),
+            pl.BlockSpec((1, rank, block), lambda i: (0, 0, i % KEY_VALUE_HEADS)),
+            pl.BlockSpec((1, rank, block), lambda i: (0, 0, half + i % half)),
+        ],
+        out_specs=pl.BlockSpec((rows, block), lambda i: (0, i)),
+        out_shape=jax.ShapeDtypeStruct((rows, steps * block + spare), jnp.bfloat16),
+        compiler_params=params(),
+        cost_estimate=cost(2 * rows * rank * steps * block * 4, 4 * rows * steps * block),
+        name="expand",
+    )(shrunk, up_query, up_query)
+
+
+def append_kernel(rows_ref, *refs):
+    refs[-1][...] = rows_ref[...]
+
+
+def append(rows, into, *others):
+    height, width = rows.shape
+    anywhere = pl.BlockSpec(memory_space=pl.ANY)
+    return pl.pallas_call(
+        append_kernel,
+        grid=(1,),
+        in_specs=[pl.BlockSpec((height, width), lambda i: (0, 0))] + [anywhere] * (1 + len(others)),
+        out_specs=pl.BlockSpec((height, width), lambda i: (0, into.shape[1] // width - 1)),
+        out_shape=jax.ShapeDtypeStruct(into.shape, into.dtype),
+        input_output_aliases={1: 0},
+        compiler_params=params(),
+        name="append",
+    )(rows, into, *others)
 
 
 def picks(ids, rows, block, shift):
@@ -204,7 +262,7 @@
     return ((at + shift == lane_iota((ids.shape[0], rows))) & (blocks == block)).astype(jnp.bfloat16)
 
 
-def correct_kernel(full, fold, ids_ref, dkv_ref, sk_ref, sv_ref, k_ref, v_ref, kv_ref):
+def correct_kernel(full, fold, ids_ref, dkv_ref, sk_ref, sv_ref, kv_ref):
     rows = dkv_ref.shape[0]
     width = sk_ref.shape[1]
     ids = ids_ref[...]
@@ -219,18 +277,15 @@
             total[i] = term if total[i] is None else total[i] + term
     keys = (sk_ref[...].astype(jnp.float32) + total[0]).astype(jnp.bfloat16)
     values = (sv_ref[...].astype(jnp.float32) + total[1]).astype(jnp.bfloat16)
-    k_ref[...] = keys
-    v_ref[...] = values
     kv_ref[:, :width] = keys
     kv_ref[:, width:] = values
 
 
 def correct(ids, dkv, shared_keys, shared_values, full, fold):
     rows, width = shared_keys.shape
-    one = jax.ShapeDtypeStruct((rows, width), jnp.bfloat16)
     return pl.pallas_call(
         functools.partial(correct_kernel, full, fold),
-        out_shape=[one, one, jax.ShapeDtypeStruct((rows, 2 * width), jnp.bfloat16)],
+        out_shape=jax.ShapeDtypeStruct((rows, 2 * width), jnp.bfloat16),
         compiler_params=params(),
         name="correct",
     )(ids, dkv, shared_keys, shared_values)
@@ -255,11 +310,10 @@
     me_ref, ids_ref, request_ref, sq_ref = (refs.pop(0) for _ in range(4))
     dq_refs = [refs.pop(0) for _ in range(full + fold)]
     chunk_refs = [(refs.pop(0), refs.pop(0)) for _ in tags]
-    out_ref, bias, keys, values, query = refs
+    out_ref, bias, keys, values, query, scores = refs
     head = pl.program_id(0)
     me = me_ref[0]
     tokens = sq_ref.shape[0]
-    here = reach * tokens
 
     @pl.when(head == 0)
     def _():
@@ -274,6 +328,7 @@
             if at == reach:
                 allowed = allowed & (lanes <= rows)
             bias[:, at * tokens : (at + 1) * tokens] = jnp.where(allowed, 0.0, -1e30)
+        values[:, HEAD_SIZE:] = jnp.ones((values.shape[0], HEAD_SIZE), jnp.bfloat16)
 
     zeros = jnp.zeros((tokens, HEAD_SIZE), jnp.bfloat16)
     for at in range(reach):
@@ -281,7 +336,7 @@
         @pl.when(me - reach + at < 0)
         def _(at=at):
             keys[at * tokens : (at + 1) * tokens, :] = zeros
-            values[at * tokens : (at + 1) * tokens, :] = zeros
+            values[at * tokens : (at + 1) * tokens, :HEAD_SIZE] = zeros
 
     for (back, mark), (k_ref, v_ref) in zip(tags, chunk_refs):
         source = (me // PLANE - back) * PLANE + jnp.bitwise_xor(me % PLANE, mark)
@@ -291,7 +346,7 @@
         def _(at=at, k_ref=k_ref, v_ref=v_ref):
             place = pl.ds(pl.multiple_of(at * tokens, tokens), tokens)
             keys[place, :] = k_ref[...]
-            values[place, :] = v_ref[...]
+            values[place, :HEAD_SIZE] = v_ref[...]
 
     ids = ids_ref[...]
     slots = dq_refs[0].shape[0]
@@ -306,17 +361,27 @@
         correction = term if correction is None else correction + term
     query[...] = (delta + correction).astype(jnp.bfloat16)
 
-    scale = 1.0 / math.sqrt(HEAD_SIZE)
-    for j in range(sq_ref.shape[1] // HEAD_SIZE):
-        span = slice(j * HEAD_SIZE, (j + 1) * HEAD_SIZE)
-        scores = lax.dot_general(
-            query[:, span], keys[...], (((1,), (1,)), ((), ())), preferred_element_type=jnp.float32
+    factor = math.log2(math.e) / math.sqrt(HEAD_SIZE)
+    heads = sq_ref.shape[1] // HEAD_SIZE
+
+    def score(j):
+        scores[j % 2] = lax.dot_general(
+            query[:, j * HEAD_SIZE : (j + 1) * HEAD_SIZE],
+            keys[...],
+            (((1,), (1,)), ((), ())),
+            preferred_element_type=jnp.float32,
         )
-        scores = scores * scale + bias[...]
-        raised = jnp.exp(scores - jnp.max(scores, axis=1, keepdims=True))
-        total = jnp.sum(raised, axis=1, keepdims=True)
+
+    score(0)
+    for j in range(heads):
+        if j + 1 < heads:
+            score(j + 1)
+        masked = scores[j % 2] + bias[...]
+        raised = jnp.exp2((masked - jnp.max(masked, axis=1, keepdims=True)) * factor)
         blended = f32_dot(raised.astype(jnp.bfloat16), values[...])
-        out_ref[:, span] = (blended / total).astype(jnp.bfloat16)
+        out_ref[:, j * HEAD_SIZE : (j + 1) * HEAD_SIZE] = (
+            blended[:, :HEAD_SIZE] / blended[:, HEAD_SIZE:]
+        ).astype(jnp.bfloat16)
 
 
 def attend(me, ids, requests, shared_query, dq, chunks, full, fold, reach):
@@ -350,10 +415,12 @@
         scratch_shapes=[
             pltpu.VMEM((tokens, window), jnp.float32),
             pltpu.VMEM((window, HEAD_SIZE), jnp.bfloat16),
-            pltpu.VMEM((window, HEAD_SIZE), jnp.bfloat16),
+            pltpu.VMEM((window, 2 * HEAD_SIZE), jnp.bfloat16),
             pltpu.VMEM((tokens, block), jnp.bfloat16),
+            pltpu.VMEM((2, tokens, window), jnp.float32),
         ],
-        compiler_params=params(),
+        compiler_params=params(60),
+        cost_estimate=cost(16 * tokens * query_width * window, 8 * tokens * query_width),
         name="attend",
     )(*operands)
 
@@ -387,18 +454,23 @@
 
     outgoing, ids = dispatch(normed, token_adapter, adapter_slot_table, full, fold)
     incoming = exchange(outgoing, devices)
-    dkv, dq = project(incoming, adapter_down_factors, adapter_up_query, adapter_up_key_value, full, fold)
+    dkv, shrunk = project(incoming, adapter_down_factors, adapter_up_key_value, full, fold)
     dkv = exchange(dkv, devices)
-    keys, values, kv = correct(ids, dkv, shared_key_rows, shared_value_rows, full, fold)
-    dq = exchange(dq, devices)
+    kv_width = shared_key_rows.shape[1]
+    dq = expand(shrunk, adapter_up_query, full, fold, 2 * kv_width)
+    kv = correct(ids, dkv, shared_key_rows, shared_value_rows, full, fold)
     chunks = window_chunks(kv, devices, reach)
-    key_cache = exchange(keys, devices)
-    value_cache = exchange(values, devices)
+    if tokens == devices * SUBLANES:
+        dq = exchange(append(kv, dq, *(rows for back, mark, rows in chunks if back and not mark)), devices)
+        pages = dq[:, -2 * kv_width :]
+    else:
+        dq = exchange(dq, devices)
+        pages = exchange(kv, devices)
     me = lax.axis_index("seq").astype(jnp.int32).reshape(1)
     attention = attend(
         me, ids, token_request.reshape(devices, tokens), shared_query_rows, dq, chunks, full, fold, reach
     )
-    return (attention, key_cache, value_cache)
+    return (attention, pages[:, :kv_width], pages[:, kv_width:])
 
 
 def solution(mesh):

time: 219 us -> 190 us (0.87)
  the two profiles are of different devices: /device:TPU:17 before, /device:TPU:0 now
where the time goes in v2:
time: 190 us; the launch traced here: 189 us
  waiting for transfers between devices  95.3 us (50%)
  starting transfers between devices  27.8 us (15%)
  blocking collectives  27.6 us (15%)
  Pallas kernels  23.5 us (12%)
  local copies, waits for them, and re-layouts  13.5 us (7%)
    all_to_all x2, waiting for transfers between devices, exchange(): lax.all_to_all(rows.reshape(devices, rows.shape[0] // devices, width), 's...  53.4 us
    ppermute x9, waiting for transfers between devices, window_chunks(): lax.ppermute(rows, 'seq', swap)  36.3 us
    all_to_all x1, blocking collectives, exchange(): lax.all_to_all(rows.reshape(devices, rows.shape[0] // devices, width), 's...  27.6 us
    all_to_all x2, starting transfers between devices, exchange(): lax.all_to_all(rows.reshape(devices, rows.shape[0] // devices, width), 's...  17.7 us
    pallas_call x1, Pallas kernels, attend(): pl.pallas_call(functools.partial(attend_kernel, full, fold, reach, tuple(...  13.1 us
    unnamed x37, local copies, waits for them, and re-layouts  12.8 us
    ppermute x2, starting transfers between devices, window_chunks(): lax.ppermute(kv, 'seq', [(i, i + hop) for i in range(devices - hop)])  5.67 us
    ppermute x2, waiting for transfers between devices, window_chunks(): lax.ppermute(kv, 'seq', [(i, i + hop) for i in range(devices - hop)])  5.6 us
  transfers between devices with their start and end apart: 13, of which 7 were waited for; matrix products, arithmetic and copies ran while one was open for 4% of the time, Pallas kernels for 2%

profile of v2, /device:TPU:0, one launch (start us, length us, event | category | flops | bytes accessed | tf_op | source)
XLA Modules:
  0.0 188.6 jit_solution(9858322275176092800)
XLA Ops:
  0.6 0.0 copy-start.1
  0.6 1.6 copy-done.1
  2.2 0.0 copy-start.11
  2.2 0.7 copy-done.11
  2.9 0.0 copy-start.12
  2.9 0.7 copy-done.12
  3.5 3.5 %dispatch.1 = (bf16[128,12288]{1,0:T(8,128)(2,1)S(1)}, s32[128,128]{1,0:T(8,128)S(1)}) custom-call(s32[1,128]{1,0:T(1,128)S(1)} %bitcast.15, s32[16]{0:T(128)S(1)} %copy-done.12, bf16[128,8192]{1,0:T(8,128)(2,1)S(1)} %copy-done.1, bf16[128,8192]{1,0:T(8,128)(2,1)S(1)} %copy-done.1), custom_call_target="tpu_custom_call" | custom-call | tf_op jit(solution)/shard_map/dispatch/pallas_call | solution.py:105
  7.0 0.0 copy-start.2
  7.0 1.7 copy-done.2
  8.7 0.0 copy-start.10
  8.7 7.4 %all-to-all-start = ((bf16[16,8,12288]{2,1,0:T(8,128)(2,1)}), bf16[16,8,12288]{2,1,0:T(8,128)(2,1)S(1)}, u32[]{:S(2)}, u32[]{:S(2)}) async-start(bf16[16,8,12288]{2,1,0:T(8,128)(2,1)} %bitcast.12), calls=%async_computation | async-start | bytes 6291456 | tf_op jit(solution)/shard_map/all_to_all | solution.py:430
  16.1 0.0 copy-start.7
  16.1 6.0 %copy.14.refs_3_.refs_4_ = bf16[1,8192,192]{2,1,0:T(8,128)(2,1)} copy(bf16[1,8192,192]{1,2,0:T(8,128)(2,1)} %param.16) | data formatting | bytes 6291456 | tf_op args[6]
  22.0 53.4 %all-to-all-done = bf16[16,8,12288]{2,1,0:T(8,128)(2,1)S(1)} async-done(((bf16[16,8,12288]{2,1,0:T(8,128)(2,1)}), bf16[16,8,12288]{2,1,0:T(8,128)(2,1)S(1)}, u32[]{:S(2)}, u32[]{:S(2)}) %all-to-all-start) | async-done | bytes 3145760 | tf_op jit(solution)/shard_map/all_to_all | solution.py:430
  75.4 0.0 copy-done.7
  75.4 0.0 copy-start
  75.4 2.2 %copy-done = bf16[1,8192,192]{2,1,0:T(8,128)(2,1)S(1)} copy-done((bf16[1,8192,192]{2,1,0:T(8,128)(2,1)S(1)}, bf16[1,8192,192]{2,1,0:T(8,128)(2,1)}, u32[]{:S(2)}) %copy-start) | copy-done | bytes 3145752
  77.6 2.5 %project.1 = (bf16[128,1536]{1,0:T(8,128)(2,1)S(1)}, bf16[2,128,64]{2,1,0:T(8,128)(2,1)S(1)}) custom-call(bf16[128,12288]{1,0:T(8,128)(2,1)S(1)} %bitcast.9, bf16[128,12288]{1,0:T(8,128)(2,1)S(1)} %bitcast.10, bf16[128,12288]{1,0:T(8,128)(2,1)S(1)} %bitcast.11, bf16[1,8192,192]{2,1,0:T(8,128)(2,1)S(1)} %copy-done, bf16[1,8192,192]{2,1,0:T(8,128)(2,1)S(1)} %copy-done, ...), custom_call_target="tpu_custom_call" | custom-call | tf_op jit(solution)/shard_map/project/pallas_call | solution.py:187
  80.1 0.0 copy-start.3
  80.1 27.6 %all_to_all.15 = bf16[16,8,1536]{2,1,0:T(8,128)(2,1)S(1)} all-to-all(bf16[16,8,1536]{2,1,0:T(8,128)(2,1)S(1)} %bitcast.14), channel_id=1, replica_groups=mesh['groups'=2,'seq'=16] {'seq'}, dimensions={0} | all-to-all | bytes 786432 | tf_op jit(solution)/shard_map/all_to_all | solution.py:430
  107.7 0.0 copy-done.10
  107.7 0.0 copy-done.8
  107.7 0.0 copy-done.9
  107.7 0.4 correct.1.rows_ref.refs_6_.refs_7_
  108.1 0.0 copy-start.4
  108.1 2.6 %collective-permute-start = (bf16[128,1024]{1,0:T(8,128)(2,1)S(1)}, bf16[128,1024]{1,0:T(8,128)(2,1)S(1)}, u32[]{:S(2)}, u32[]{:S(2)}) collective-permute-start(bf16[128,1024]{1,0:T(8,128)(2,1)S(1)} %correct.1.rows_ref.refs_6_.refs_7_), channel_id=1, source_target_pairs={{0,4},{1,5},{2,6},{3,7},{4,8},{5,9},{6,10},{7,11},{8,12},{9,13},{1... | collective-permute-start | bytes 786440 | tf_op jit(solution)/shard_map/ppermute | solution.py:299
  110.7 3.0 %collective-permute-start.1 = (bf16[128,1024]{1,0:T(8,128)(2,1)S(1)}, bf16[128,1024]{1,0:T(8,128)(2,1)S(1)}, u32[]{:S(2)}, u32[]{:S(2)}) collective-permute-start(bf16[128,1024]{1,0:T(8,128)(2,1)S(1)} %correct.1.rows_ref.refs_6_.refs_7_), channel_id=1, source_target_pairs={{0,8},{1,9},{2,10},{3,11},{4,12},{5,13},{6,14},{7,15},{16,24},{17,... | collective-permute-start | bytes 786440 | tf_op jit(solution)/shard_map/ppermute | solution.py:299
  113.8 0.0 copy-done.3
  113.8 3.3 %expand.1.refs_0_ = bf16[128,7168]{1,0:T(8,128)(2,1)} custom-call(bf16[2,128,64]{2,1,0:T(8,128)(2,1)S(1)} %get-tuple-element.10.shrunk_ref, bf16[1,64,4096]{2,1,0:T(8,128)(2,1)S(1)} %copy-done.3, bf16[1,64,4096]{2,1,0:T(8,128)(2,1)S(1)} %copy-done.3), custom_call_target="tpu_custom_call" | custom-call | flops 402653184 | bytes 3145728 | tf_op jit(solution)/shard_map/expand/pallas_call | solution.py:225
  117.0 0.3 collective-permute-done.refs_1_.refs_8_.refs_9_
  117.3 5.3 %collective-permute-done.1.refs_2_.refs_10_.refs_11_ = bf16[128,1024]{1,0:T(8,128)(2,1)S(1)} collective-permute-done((bf16[128,1024]{1,0:T(8,128)(2,1)S(1)}, bf16[128,1024]{1,0:T(8,128)(2,1)S(1)}, u32[]{:S(2)}, u32[]{:S(2)}) %collective-permute-start.1) | collective-permute-done | bytes 262176 | tf_op jit(solution)/shard_map/ppermute | solution.py:299
  122.7 0.8 append.1
  123.5 10.3 %all-to-all-start.2 = ((bf16[16,8,7168]{2,1,0:T(8,128)(2,1)}), bf16[16,8,7168]{2,1,0:T(8,128)(2,1)S(1)}, u32[]{:S(2)}, u32[]{:S(2)}) async-start(bf16[16,8,7168]{2,1,0:T(8,128)(2,1)} %bitcast.7), calls=%async_computation.2 | async-start | bytes 3670016 | tf_op jit(solution)/shard_map/all_to_all | solution.py:430
  133.8 1.9 %collective-permute-start.2 = (bf16[128,1024]{1,0:T(8,128)(2,1)S(1)}, bf16[128,1024]{1,0:T(8,128)(2,1)S(1)}, u32[]{:S(2)}, u32[]{:S(2)}) collective-permute-start(bf16[128,1024]{1,0:T(8,128)(2,1)S(1)} %correct.1.rows_ref.refs_6_.refs_7_), channel_id=1, source_target_pairs={{0,2},{1,3},{2,0},{3,1},{4,6},{5,7},{6,4},{7,5},{8,10},{9,11},{10,... | collective-permute-start | bytes 786440 | tf_op jit(solution)/shard_map/ppermute | solution.py:303
  135.7 0.0 copy-done.4
  135.7 0.0 collective-permute-start.5
  135.7 0.2 collective-permute-start.4
  136.0 1.8 collective-permute-start.3
  137.8 0.0 copy-done.5
  137.8 0.0 collective-permute-start.6
  137.8 19.7 %collective-permute-done.2.refs_12_.refs_13_ = bf16[128,1024]{1,0:T(8,128)(2,1)S(1)} collective-permute-done((bf16[128,1024]{1,0:T(8,128)(2,1)S(1)}, bf16[128,1024]{1,0:T(8,128)(2,1)S(1)}, u32[]{:S(2)}, u32[]{:S(2)}) %collective-permute-start.2) | collective-permute-done | bytes 262176 | tf_op jit(solution)/shard_map/ppermute | solution.py:303
  157.5 0.0 copy-done.6
  157.5 0.0 collective-permute-start.7
  157.5 0.0 collective-permute-done.5.refs_18_.refs_19_
  157.5 0.0 copy-start.15
  157.5 0.5 collective-permute-start.8
  158.0 5.4 %collective-permute-done.4.refs_16_.refs_17_ = bf16[128,1024]{1,0:T(8,128)(2,1)S(1)} collective-permute-done((bf16[128,1024]{1,0:T(8,128)(2,1)S(1)}, bf16[128,1024]{1,0:T(8,128)(2,1)S(1)}, u32[]{:S(2)}, u32[]{:S(2)}) %collective-permute-start.4) | collective-permute-done | bytes 262176 | tf_op jit(solution)/shard_map/ppermute | solution.py:303
  163.5 0.0 collective-permute-start.10
  163.5 10.1 %collective-permute-done.3.refs_14_.refs_15_ = bf16[128,1024]{1,0:T(8,128)(2,1)} collective-permute-done((bf16[128,1024]{1,0:T(8,128)(2,1)S(1)}, bf16[128,1024]{1,0:T(8,128)(2,1)}, u32[]{:S(2)}, u32[]{:S(2)}) %collective-permute-start.3) | collective-permute-done | bytes 262176 | tf_op jit(solution)/shard_map/ppermute | solution.py:303
  173.5 0.0 collective-permute-start.9
  173.6 0.0 all-to-all-done.2
  173.6 0.8 fusion
  174.3 0.0 collective-permute-done.6.refs_20_.refs_21_
  174.3 0.0 collective-permute-done.7.refs_22_.refs_23_
  174.3 0.0 collective-permute-done.8.refs_24_.refs_25_
  174.3 0.0 copy-start.17
  174.3 0.0 collective-permute-done.10.refs_28_.refs_29_
  174.3 1.1 collective-permute-done.9.refs_26_.refs_27_
  175.4 0.0 copy-done.14
  175.4 0.0 copy-done.15
  175.4 0.0 copy-done.16
  175.4 0.0 copy-done.13
  175.4 0.0 copy-done.17
  175.5 13.1 %attend.1 = bf16[128,4096]{1,0:T(8,128)(2,1)} custom-call(s32[1]{0:T(128)} %bitcast.refs_0_, s32[128,128]{1,0:T(8,128)} %copy-done.10, s32[16,128]{1,0:T(8,128)} %bitcast.19, bf16[128,4096]{1,0:T(8,128)(2,1)} %refs_3_.2, bf16[128,7168]{1,0:T(8,128)(2,1)} %bitcast.17, bf16[128,7168]{1,0:T(8,128)(2,1)} %bitcast.18, bf16[128,1024]{1,0:T(8,128)(2,1)} %copy-done.4, ...), custom_call_target="tpu_custom_call" | custom-call | flops 9663676416 | bytes 4194304 | tf_op jit(solution)/shard_map/attend/pallas_call | solution.py:409
  (7 shorter events, 0.0 us)
Async XLA Ops:
  0.6 1.6 copy-start.1
  2.2 0.7 copy-start.11
  2.9 0.7 copy-start.12
  7.0 1.7 copy-start.2
  8.7 99.0 %copy-start.10 = (s32[128,128]{1,0:T(8,128)}, s32[128,128]{1,0:T(8,128)S(1)}, u32[]{:S(2)}) copy-start(s32[128,128]{1,0:T(8,128)S(1)} %get-tuple-element.7.ids_ref.refs_1_) | copy-start | bytes 196612
  8.7 66.8 %all-to-all-start = ((bf16[16,8,12288]{2,1,0:T(8,128)(2,1)}), bf16[16,8,12288]{2,1,0:T(8,128)(2,1)S(1)}, u32[]{:S(2)}, u32[]{:S(2)}) async-start(bf16[16,8,12288]{2,1,0:T(8,128)(2,1)} %bitcast.12), calls=%async_computation | async-start | bytes 6291456 | tf_op jit(solution)/shard_map/all_to_all | solution.py:430
  16.1 59.4 %copy-start.7 = (bf16[1,2,64,512]{3,2,1,0:T(8,128)(2,1)S(1)}, bf16[1,2,64,512]{3,2,1,0:T(8,128)(2,1)}, u32[]{:S(2)}) copy-start(bf16[1,2,64,512]{3,2,1,0:T(8,128)(2,1)} %refs_5_.1) | copy-start | bytes 393220
  75.4 2.2 %copy-start = (bf16[1,8192,192]{2,1,0:T(8,128)(2,1)S(1)}, bf16[1,8192,192]{2,1,0:T(8,128)(2,1)}, u32[]{:S(2)}) copy-start(bf16[1,8192,192]{2,1,0:T(8,128)(2,1)} %copy.14.refs_3_.refs_4_) | copy-start | bytes 9437188
  77.6 30.1 %copy-start.8 = (bf16[128,512]{1,0:T(8,128)(2,1)S(1)}, bf16[128,512]{1,0:T(8,128)(2,1)}, u32[]{:S(2)}) copy-start(bf16[128,512]{1,0:T(8,128)(2,1)} %sk_ref.1) | copy-start | bytes 393220
  77.6 30.1 %copy-start.9 = (bf16[128,512]{1,0:T(8,128)(2,1)S(1)}, bf16[128,512]{1,0:T(8,128)(2,1)}, u32[]{:S(2)}) copy-start(bf16[128,512]{1,0:T(8,128)(2,1)} %sv_ref.1) | copy-start | bytes 393220
  80.1 33.6 %copy-start.3 = (bf16[1,64,4096]{2,1,0:T(8,128)(2,1)S(1)}, bf16[1,64,4096]{2,1,0:T(8,128)(2,1)}, u32[]{:S(2)}) copy-start(bf16[1,64,4096]{2,1,0:T(8,128)(2,1)} %other_ref.1) | copy-start | bytes 1572868
  108.1 27.6 %copy-start.4 = (bf16[128,1024]{1,0:T(8,128)(2,1)}, bf16[128,1024]{1,0:T(8,128)(2,1)S(1)}, u32[]{:S(2)}) copy-start(bf16[128,1024]{1,0:T(8,128)(2,1)S(1)} %correct.1.rows_ref.refs_6_.refs_7_) | copy-start | bytes 786436
  108.1 9.2 %collective-permute-start = (bf16[128,1024]{1,0:T(8,128)(2,1)S(1)}, bf16[128,1024]{1,0:T(8,128)(2,1)S(1)}, u32[]{:S(2)}, u32[]{:S(2)}) collective-permute-start(bf16[128,1024]{1,0:T(8,128)(2,1)S(1)} %correct.1.rows_ref.refs_6_.refs_7_), channel_id=1, source_target_pairs={{0,4},{1,5},{2,6},{3,7},{4,8},{5,9},{6,10},{7,11},{8,12},{9,13},{1... | collective-permute-start | bytes 786440 | tf_op jit(solution)/shard_map/ppermute | solution.py:299
  110.7 11.9 %collective-permute-start.1 = (bf16[128,1024]{1,0:T(8,128)(2,1)S(1)}, bf16[128,1024]{1,0:T(8,128)(2,1)S(1)}, u32[]{:S(2)}, u32[]{:S(2)}) collective-permute-start(bf16[128,1024]{1,0:T(8,128)(2,1)S(1)} %correct.1.rows_ref.refs_6_.refs_7_), channel_id=1, source_target_pairs={{0,8},{1,9},{2,10},{3,11},{4,12},{5,13},{6,14},{7,15},{16,24},{17,... | collective-permute-start | bytes 786440 | tf_op jit(solution)/shard_map/ppermute | solution.py:299
  117.3 20.5 %copy-start.5 = (bf16[128,1024]{1,0:T(8,128)(2,1)}, bf16[128,1024]{1,0:T(8,128)(2,1)S(1)}, u32[]{:S(2)}) copy-start(bf16[128,1024]{1,0:T(8,128)(2,1)S(1)} %collective-permute-done.refs_1_.refs_8_.refs_9_) | copy-start | bytes 786436
  122.7 34.8 %copy-start.6 = (bf16[128,1024]{1,0:T(8,128)(2,1)}, bf16[128,1024]{1,0:T(8,128)(2,1)S(1)}, u32[]{:S(2)}) copy-start(bf16[128,1024]{1,0:T(8,128)(2,1)S(1)} %collective-permute-done.1.refs_2_.refs_10_.refs_11_) | copy-start | bytes 786436
  123.5 50.1 %all-to-all-start.2 = ((bf16[16,8,7168]{2,1,0:T(8,128)(2,1)}), bf16[16,8,7168]{2,1,0:T(8,128)(2,1)S(1)}, u32[]{:S(2)}, u32[]{:S(2)}) async-start(bf16[16,8,7168]{2,1,0:T(8,128)(2,1)} %bitcast.7), calls=%async_computation.2 | async-start | bytes 3670016 | tf_op jit(solution)/shard_map/all_to_all | solution.py:430
  133.8 23.7 %collective-permute-start.2 = (bf16[128,1024]{1,0:T(8,128)(2,1)S(1)}, bf16[128,1024]{1,0:T(8,128)(2,1)S(1)}, u32[]{:S(2)}, u32[]{:S(2)}) collective-permute-start(bf16[128,1024]{1,0:T(8,128)(2,1)S(1)} %correct.1.rows_ref.refs_6_.refs_7_), channel_id=1, source_target_pairs={{0,2},{1,3},{2,0},{3,1},{4,6},{5,7},{6,4},{7,5},{8,10},{9,11},{10,... | collective-permute-start | bytes 786440 | tf_op jit(solution)/shard_map/ppermute | solution.py:303
  135.7 21.8 %collective-permute-start.5 = (bf16[128,1024]{1,0:T(8,128)(2,1)S(1)}, bf16[128,1024]{1,0:T(8,128)(2,1)S(1)}, u32[]{:S(2)}, u32[]{:S(2)}) collective-permute-start(bf16[128,1024]{1,0:T(8,128)(2,1)S(1)} %correct.1.rows_ref.refs_6_.refs_7_), channel_id=1, source_target_pairs={{0,1},{1,0},{2,3},{3,2},{4,5},{5,4},{6,7},{7,6},{8,9},{9,8},{10,11... | collective-permute-start | bytes 786440 | tf_op jit(solution)/shard_map/ppermute | solution.py:303
  135.7 27.7 %collective-permute-start.4 = (bf16[128,1024]{1,0:T(8,128)(2,1)S(1)}, bf16[128,1024]{1,0:T(8,128)(2,1)S(1)}, u32[]{:S(2)}, u32[]{:S(2)}) collective-permute-start(bf16[128,1024]{1,0:T(8,128)(2,1)S(1)} %collective-permute-done.1.refs_2_.refs_10_.refs_11_), channel_id=1, source_target_pairs={{0,2},{1,3},{2,0},{3,1},{4,6},{5,7},{6,4},{7,5},{8,10},{9,11},{10,... | collective-permute-start | bytes 786440 | tf_op jit(solution)/shard_map/ppermute | solution.py:303
  136.0 37.6 %collective-permute-start.3 = (bf16[128,1024]{1,0:T(8,128)(2,1)S(1)}, bf16[128,1024]{1,0:T(8,128)(2,1)}, u32[]{:S(2)}, u32[]{:S(2)}) collective-permute-start(bf16[128,1024]{1,0:T(8,128)(2,1)S(1)} %collective-permute-done.refs_1_.refs_8_.refs_9_), channel_id=1, source_target_pairs={{0,2},{1,3},{2,0},{3,1},{4,6},{5,7},{6,4},{7,5},{8,10},{9,11},{10,... | collective-permute-start | bytes 786440 | tf_op jit(solution)/shard_map/ppermute | solution.py:303
  137.8 36.6 %collective-permute-start.6 = (bf16[128,1024]{1,0:T(8,128)(2,1)S(1)}, bf16[128,1024]{1,0:T(8,128)(2,1)}, u32[]{:S(2)}, u32[]{:S(2)}) collective-permute-start(bf16[128,1024]{1,0:T(8,128)(2,1)S(1)} %collective-permute-done.refs_1_.refs_8_.refs_9_), channel_id=1, source_target_pairs={{0,1},{1,0},{2,3},{3,2},{4,5},{5,4},{6,7},{7,6},{8,9},{9,8},{10,11... | collective-permute-start | bytes 786440 | tf_op jit(solution)/shard_map/ppermute | solution.py:303
  157.5 17.9 %copy-start.14 = (bf16[128,1024]{1,0:T(8,128)(2,1)}, bf16[128,1024]{1,0:T(8,128)(2,1)S(1)}, u32[]{:S(2)}) copy-start(bf16[128,1024]{1,0:T(8,128)(2,1)S(1)} %collective-permute-done.2.refs_12_.refs_13_) | copy-start | bytes 786436
  157.5 16.8 %collective-permute-start.7 = (bf16[128,1024]{1,0:T(8,128)(2,1)S(1)}, bf16[128,1024]{1,0:T(8,128)(2,1)}, u32[]{:S(2)}, u32[]{:S(2)}) collective-permute-start(bf16[128,1024]{1,0:T(8,128)(2,1)S(1)} %collective-permute-done.1.refs_2_.refs_10_.refs_11_), channel_id=1, source_target_pairs={{0,1},{1,0},{2,3},{3,2},{4,5},{5,4},{6,7},{7,6},{8,9},{9,8},{10,11... | collective-permute-start | bytes 786440 | tf_op jit(solution)/shard_map/ppermute | solution.py:303
  157.5 17.9 %copy-start.15 = (bf16[128,1024]{1,0:T(8,128)(2,1)}, bf16[128,1024]{1,0:T(8,128)(2,1)S(1)}, u32[]{:S(2)}) copy-start(bf16[128,1024]{1,0:T(8,128)(2,1)S(1)} %collective-permute-done.5.refs_18_.refs_19_) | copy-start | bytes 786436
  157.5 16.8 %collective-permute-start.8 = (bf16[128,1024]{1,0:T(8,128)(2,1)S(1)}, bf16[128,1024]{1,0:T(8,128)(2,1)S(1)}, u32[]{:S(2)}, u32[]{:S(2)}) collective-permute-start(bf16[128,1024]{1,0:T(8,128)(2,1)S(1)} %collective-permute-done.2.refs_12_.refs_13_), channel_id=1, source_target_pairs={{0,1},{1,0},{2,3},{3,2},{4,5},{5,4},{6,7},{7,6},{8,9},{9,8},{10,11... | collective-permute-start | bytes 786440 | tf_op jit(solution)/shard_map/ppermute | solution.py:303
  163.5 12.0 %copy-start.16 = (bf16[128,1024]{1,0:T(8,128)(2,1)}, bf16[128,1024]{1,0:T(8,128)(2,1)S(1)}, u32[]{:S(2)}) copy-start(bf16[128,1024]{1,0:T(8,128)(2,1)S(1)} %collective-permute-done.4.refs_16_.refs_17_) | copy-start | bytes 786436
  163.5 10.9 %collective-permute-start.10 = (bf16[128,1024]{1,0:T(8,128)(2,1)S(1)}, bf16[128,1024]{1,0:T(8,128)(2,1)}, u32[]{:S(2)}, u32[]{:S(2)}) collective-permute-start(bf16[128,1024]{1,0:T(8,128)(2,1)S(1)} %collective-permute-done.4.refs_16_.refs_17_), channel_id=1, source_target_pairs={{0,1},{1,0},{2,3},{3,2},{4,5},{5,4},{6,7},{7,6},{8,9},{9,8},{10,11... | collective-permute-start | bytes 786440 | tf_op jit(solution)/shard_map/ppermute | solution.py:303
  173.5 1.9 collective-permute-start.9
  173.6 1.9 copy-start.13
  174.3 1.1 copy-start.17

commit v3 on v2

--- a/solution.py
+++ b/solution.py
@@ -29,6 +29,10 @@
 
 def lane_iota(shape):
     return lax.broadcasted_iota(jnp.int32, shape, 1)
+
+
+def turned_dot(a, b):
+    return lax.dot_general(a, b, (((1,), (1,)), ((), ())), preferred_element_type=jnp.float32)
 
 
 def row_iota(shape):
@@ -129,7 +133,7 @@
     refs = list(refs)
     low_refs = [(refs.pop(0), refs.pop(0)) for _ in range(full)]
     fold_ref = refs.pop(0) if fold else None
-    down_low, down_high, up_kv, dkv_ref, shrunk_ref, acc = refs
+    (down_low, down_high, up_kv), (out_ref, acc) = refs[:3], refs[-2:]
     step = pl.program_id(0)
     rank = up_kv.shape[2]
 
@@ -139,21 +143,22 @@
 
     low, high = down_low[0], down_high[0]
     for b, (x_low, x_high) in enumerate(low_refs):
-        acc[b] += f32_dot(x_low[...], low) + f32_dot(x_high[...], high)
+        acc[b] += turned_dot(x_low[...], low) + turned_dot(x_high[...], high)
     if fold:
-        acc[full] += f32_dot(fold_ref[...], low)
-        acc[full + 1] += f32_dot(fold_ref[...], high)
+        acc[full] += turned_dot(fold_ref[...], low)
+        acc[full + 1] += turned_dot(fold_ref[...], high)
 
     @pl.when(step == steps - 1)
     def _():
         kv_width = up_kv.shape[3]
+        queries = []
         for b in range(full):
             shrunk = acc[b].astype(jnp.bfloat16)
             at = b * 2 * kv_width
             for i in range(2):
                 piece = shrunk[:, (i + 1) * rank : (i + 2) * rank]
-                dkv_ref[:, at + i * kv_width : at + (i + 1) * kv_width] = f32_dot(piece, up_kv[0, i]).astype(jnp.bfloat16)
-            shrunk_ref[b] = shrunk[:, :rank]
+                out_ref[:, at + i * kv_width : at + (i + 1) * kv_width] = f32_dot(piece, up_kv[0, i]).astype(jnp.bfloat16)
+            queries.append(shrunk[:, :rank])
         if fold:
             rows = acc.shape[1]
             upper = (row_iota((rows, 1)) % SUBLANES) >= 4
@@ -161,13 +166,17 @@
             both = mixed + jnp.concatenate([mixed[:, 4:], mixed[:, :4]], axis=1)
             shrunk = both.reshape(rows, 3 * rank).astype(jnp.bfloat16)
             delta = [f32_dot(shrunk[:, (i + 1) * rank : (i + 2) * rank], up_kv[0, i]) for i in range(2)]
-            dkv_ref[:, full * 2 * kv_width :] = jnp.where(upper, delta[1], delta[0]).astype(jnp.bfloat16)
-            shrunk_ref[full] = shrunk[:, :rank]
-
-
-def project(x, down, up_kv, full, fold):
+            at = full * 2 * kv_width
+            out_ref[:, at : at + kv_width] = jnp.where(upper, delta[1], delta[0]).astype(jnp.bfloat16)
+            queries.append(shrunk[:, :rank])
+        if len(queries) % 2:
+            queries.append(jnp.zeros_like(queries[0]))
+        out_ref[:, (2 * full + fold) * kv_width :] = jnp.concatenate(queries, axis=1)
+
+
+def project(x, down, up_kv, full, fold, *others):
     rows = x.shape[0]
-    _, width, ranks = down.shape
+    _, ranks, width = down.shape
     column = width // 8
     steps = width // 2 // column
     _, _, rank, kv_width = up_kv.shape
@@ -179,141 +188,207 @@
         in_specs.append(pl.BlockSpec((rows, column), lambda i: (0, 2 * full * steps + i)))
     blocks = len(in_specs)
     in_specs += [
-        pl.BlockSpec((1, column, ranks), lambda i: (0, i, 0)),
-        pl.BlockSpec((1, column, ranks), lambda i: (0, steps + i, 0)),
+        pl.BlockSpec((1, ranks, column), lambda i: (0, 0, i)),
+        pl.BlockSpec((1, ranks, column), lambda i: (0, 0, steps + i)),
         pl.BlockSpec(up_kv.shape, lambda i: (0, 0, 0, 0)),
     ]
-    shapes = [(rows, (2 * full + fold) * kv_width), (full + fold, rows, rank)]
+    in_specs += [pl.BlockSpec(memory_space=pltpu.HBM)] * len(others)
+    shape = (rows, (2 * full + fold) * kv_width + (full + fold + 1) // 2 * 2 * rank)
     return pl.pallas_call(
         functools.partial(project_kernel, full, fold, steps),
         grid=(steps,),
         in_specs=in_specs,
-        out_specs=[pl.BlockSpec(s, lambda i, s=s: (0,) * len(s)) for s in shapes],
-        out_shape=[jax.ShapeDtypeStruct(s, jnp.bfloat16) for s in shapes],
+        out_specs=pl.BlockSpec(shape, lambda i: (0, 0)),
+        out_shape=jax.ShapeDtypeStruct(shape, jnp.bfloat16),
         scratch_shapes=[pltpu.VMEM((full + 2 * fold, rows, ranks), jnp.float32)],
         compiler_params=params(),
         name="project",
-    )(*([x] * blocks), down, down, up_kv)
-
-
-def expand_kernel(full, fold, shrunk_ref, up_ref, other_ref, out_ref):
-    step = pl.program_id(0)
-    rows = out_ref.shape[0]
-
-    @pl.when(step < full * KEY_VALUE_HEADS)
-    def _():
-        if full:
-            piece = shrunk_ref[jnp.minimum(step // KEY_VALUE_HEADS, full - 1)]
-            out_ref[...] = f32_dot(piece, up_ref[0]).astype(jnp.bfloat16)
-
-    if fold:
-
-        @pl.when(step >= full * KEY_VALUE_HEADS)
-        def _():
-            upper = (row_iota((rows, 1)) % SUBLANES) >= 4
-            piece = shrunk_ref[full]
-            mixed = jnp.where(upper, f32_dot(piece, other_ref[0]), f32_dot(piece, up_ref[0]))
-            out_ref[...] = mixed.astype(jnp.bfloat16)
-
-
-def expand(shrunk, up_query, full, fold, spare):
-    _, rows, rank = shrunk.shape
-    width = up_query.shape[2]
-    block = width // KEY_VALUE_HEADS
-    half = KEY_VALUE_HEADS // 2
-    steps = full * KEY_VALUE_HEADS + fold * half
-    return pl.pallas_call(
-        functools.partial(expand_kernel, full, fold),
-        grid=(steps,),
-        in_specs=[
-            pl.BlockSpec(shrunk.shape, lambda i: (0, 0, 0)),
-            pl.BlockSpec((1, rank, block), lambda i: (0, 0, i % KEY_VALUE_HEADS)),
-            pl.BlockSpec((1, rank, block), lambda i: (0, 0, half + i % half)),
+    )(*([x] * blocks), down, down, up_kv, *others)
+
+
+def picks(at, chosen, rows):
+    return ((at == lane_iota((at.shape[0], rows))) & chosen).astype(jnp.bfloat16)
+
+
+def correct_kernel(full, fold, rank, ids_ref, back_ref, sk_ref, sv_ref, kv_ref, shrunk_ref):
+    rows = back_ref.shape[0]
+    width = sk_ref.shape[1]
+    place, block = ids_ref[:, 0:1], ids_ref[:, 1:2]
+    queries = (2 * full + fold) * width
+    total = [0.0, 0.0, 0.0]
+    for b in range(full + fold):
+        pick = picks(place, block == b, rows)
+        for i in range(2):
+            if b < full:
+                at = (2 * b + i) * width
+            else:
+                at = 2 * full * width
+                pick = pick if i == 0 else picks(place + 4, block == b, rows)
+            total[i] += f32_dot(pick, back_ref[:, at : at + width])
+    for b in range(full + fold):
+        at = queries + b // 2 * 2 * rank
+        both = f32_dot(picks(place, block == b, rows), back_ref[:, at : at + 2 * rank])
+        total[2] += both if b % 2 == 0 else pltpu.roll(both, rank, 1)
+    kv_ref[:, :width] = (sk_ref[...].astype(jnp.float32) + total[0]).astype(jnp.bfloat16)
+    kv_ref[:, width:] = (sv_ref[...].astype(jnp.float32) + total[1]).astype(jnp.bfloat16)
+    lanes = lane_iota(shrunk_ref.shape)
+    owner = (place // SUBLANES).astype(jnp.float32)
+    shrunk_ref[...] = jnp.where(lanes < rank, total[2], jnp.where(lanes == rank, owner, 0.0)).astype(jnp.bfloat16)
+
+
+def correct(ids, back, shared_keys, shared_values, rank, full, fold):
+    rows, width = shared_keys.shape
+    return pl.pallas_call(
+        functools.partial(correct_kernel, full, fold, rank),
+        out_shape=[
+            jax.ShapeDtypeStruct((rows, 2 * width), jnp.bfloat16),
+            jax.ShapeDtypeStruct((rows, 2 * rank), jnp.bfloat16),
         ],
-        out_specs=pl.BlockSpec((rows, block), lambda i: (0, i)),
-        out_shape=jax.ShapeDtypeStruct((rows, steps * block + spare), jnp.bfloat16),
-        compiler_params=params(),
-        cost_estimate=cost(2 * rows * rank * steps * block * 4, 4 * rows * steps * block),
-        name="expand",
-    )(shrunk, up_query, up_query)
-
-
-def append_kernel(rows_ref, *refs):
-    refs[-1][...] = rows_ref[...]
-
-
-def append(rows, into, *others):
-    height, width = rows.shape
-    anywhere = pl.BlockSpec(memory_space=pl.ANY)
-    return pl.pallas_call(
-        append_kernel,
-        grid=(1,),
-        in_specs=[pl.BlockSpec((height, width), lambda i: (0, 0))] + [anywhere] * (1 + len(others)),
-        out_specs=pl.BlockSpec((height, width), lambda i: (0, into.shape[1] // width - 1)),
-        out_shape=jax.ShapeDtypeStruct(into.shape, into.dtype),
-        input_output_aliases={1: 0},
-        compiler_params=params(),
-        name="append",
-    )(rows, into, *others)
-
-
-def picks(ids, rows, block, shift):
-    at, blocks = ids[:, 0:1], ids[:, 1:2]
-    return ((at + shift == lane_iota((ids.shape[0], rows))) & (blocks == block)).astype(jnp.bfloat16)
-
-
-def correct_kernel(full, fold, ids_ref, dkv_ref, sk_ref, sv_ref, kv_ref):
-    rows = dkv_ref.shape[0]
-    width = sk_ref.shape[1]
-    ids = ids_ref[...]
-    total = [None, None]
-    for i in range(2):
-        for b in range(full):
-            at = (2 * b + i) * width
-            term = f32_dot(picks(ids, rows, b, 0), dkv_ref[:, at : at + width])
-            total[i] = term if total[i] is None else total[i] + term
-        if fold:
-            term = f32_dot(picks(ids, rows, full, 4 * i), dkv_ref[:, 2 * full * width :])
-            total[i] = term if total[i] is None else total[i] + term
-    keys = (sk_ref[...].astype(jnp.float32) + total[0]).astype(jnp.bfloat16)
-    values = (sv_ref[...].astype(jnp.float32) + total[1]).astype(jnp.bfloat16)
-    kv_ref[:, :width] = keys
-    kv_ref[:, width:] = values
-
-
-def correct(ids, dkv, shared_keys, shared_values, full, fold):
-    rows, width = shared_keys.shape
-    return pl.pallas_call(
-        functools.partial(correct_kernel, full, fold),
-        out_shape=jax.ShapeDtypeStruct((rows, 2 * width), jnp.bfloat16),
         compiler_params=params(),
         name="correct",
-    )(ids, dkv, shared_keys, shared_values)
+    )(ids, back, shared_keys, shared_values)
+
+
+def expand_kernel(marks, me_ref, *refs):
+    shrunk_refs, refs = refs[:2], refs[2:]
+    up_refs, refs = refs[: len(marks)], refs[len(marks) :]
+    own_ref, far_refs, (wide, ups) = refs[0], refs[1:-2], refs[-2:]
+    rank = up_refs[0].shape[0]
+    tokens = own_ref.shape[0]
+
+    @pl.when(pl.program_id(0) == 0)
+    def _():
+        lanes = lane_iota((tokens, 2 * rank))
+        for i, shrunk_ref in enumerate(shrunk_refs):
+            rows = shrunk_ref[...].astype(jnp.float32)
+            apart = jnp.bitwise_xor(rows[:, rank : rank + 1].astype(jnp.int32), me_ref[0])
+            twice = jnp.where(lanes < rank, rows, pltpu.roll(rows, rank, 1))
+            for k in range(0, len(marks), 2):
+                wanted = jnp.where(lanes < rank, marks[k], marks[k + 1])
+                held = jnp.where(apart == wanted, twice, 0.0).astype(jnp.bfloat16)
+                wide[i * tokens : (i + 1) * tokens, k * rank : (k + 2) * rank] = held
+
+    for k, up_ref in enumerate(up_refs):
+        ups[k * rank : (k + 1) * rank, :] = up_ref[...]
+    result = f32_dot(wide[...], ups[...]).astype(jnp.bfloat16)
+    own_ref[...] = result[:tokens]
+    for i, far_ref in enumerate(far_refs):
+
+        @pl.when(pl.program_id(0) == i)
+        def _(far_ref=far_ref):
+            far_ref[...] = result[tokens:]
+
+
+def expand(me, shrunk, far_shrunk, ups):
+    tokens = shrunk.shape[0]
+    marks = tuple(sorted(ups))
+    rank, width = ups[0].shape
+    block = width // KEY_VALUE_HEADS
+    whole = pl.BlockSpec(shrunk.shape, lambda g: (0, 0))
+    part = pl.BlockSpec((tokens, block), lambda g: (0, g))
+    return pl.pallas_call(
+        functools.partial(expand_kernel, marks),
+        grid=(KEY_VALUE_HEADS,),
+        in_specs=[pl.BlockSpec(memory_space=pltpu.SMEM), whole, whole]
+        + [pl.BlockSpec((rank, block), lambda g: (0, g))] * len(marks),
+        out_specs=[part] + [pl.BlockSpec((tokens, block), lambda g: (0, 0))] * KEY_VALUE_HEADS,
+        out_shape=[jax.ShapeDtypeStruct((tokens, width), jnp.bfloat16)]
+        + [jax.ShapeDtypeStruct((tokens, block), jnp.bfloat16)] * KEY_VALUE_HEADS,
+        scratch_shapes=[
+            pltpu.VMEM((2 * tokens, len(marks) * rank), jnp.bfloat16),
+            pltpu.VMEM((len(marks) * rank, block), jnp.bfloat16),
+        ],
+        compiler_params=params(60),
+        cost_estimate=cost(16 * tokens * len(marks) * rank * width, 4 * tokens * width),
+        name="expand",
+    )(me, shrunk, far_shrunk, *(ups[k] for k in marks))
+
+
+def token_kernel(*refs):
+    refs[-1][...] = jnp.zeros_like(refs[-1])
+
+
+def token(*others):
+    return pl.pallas_call(
+        token_kernel,
+        in_specs=[pl.BlockSpec(memory_space=pltpu.HBM)] * len(others),
+        out_specs=pl.BlockSpec(memory_space=pltpu.VMEM),
+        out_shape=jax.ShapeDtypeStruct((SUBLANES, 128), jnp.float32),
+        compiler_params=params(62),
+        name="token",
+    )(*others)
+
+
+def hold(rows, *others):
+    anywhere = pl.BlockSpec(memory_space=pl.ANY)
+    return pl.pallas_call(
+        lambda *refs: None,
+        in_specs=[anywhere] + [pl.BlockSpec(memory_space=pltpu.HBM)] * len(others),
+        out_specs=anywhere,
+        out_shape=jax.ShapeDtypeStruct(rows.shape, rows.dtype),
+        input_output_aliases={0: 0},
+        compiler_params=params(),
+        name="hold",
+    )(rows, *others)
+
+
+def swap_pairs(devices, distance):
+    return [(i, i ^ distance) for i in range(devices)]
+
+
+def mirrored(rows, devices):
+    return lax.ppermute(rows, "seq", swap_pairs(devices, devices // 2))
+
+
+def crossed(factors, devices):
+    if lax.axis_size("groups") != 2:
+        return mirrored(factors, devices)
+    half = factors.shape[1] // 2
+    return mirrored(jnp.where(lax.axis_index("groups") == 0, factors[:, :half], factors[:, half:]), devices)
+
+
+def gathered_factors(factors, here, devices):
+    if here.shape != factors.shape:
+        first = lax.axis_index("groups") == 0
+        there = lax.ppermute(here, "groups", [(0, 1), (1, 0)])
+        here = jnp.concatenate([jnp.where(first, here, there), jnp.where(first, there, here)], axis=1)
+    held = {0: factors, devices // 2: here}
+    bit = devices // 4
+    while bit:
+        if bit != PLANE:
+            swap = swap_pairs(devices, bit)
+            held.update({k ^ bit: lax.ppermute(a, "seq", swap) for k, a in list(held.items())})
+        bit //= 2
+    return held
 
 
 def window_chunks(kv, devices, reach):
-    planes = reach // PLANE
     chunks = [(0, 0, kv)]
-    for back in range(1, planes + 1):
+    for back in range(1, reach // PLANE + 1):
         hop = back * PLANE
         chunks.append((back, 0, lax.ppermute(kv, "seq", [(i, i + hop) for i in range(devices - hop)])))
     bit = PLANE // 2
     while bit:
-        swap = [(i, i ^ bit) for i in range(devices)]
+        swap = swap_pairs(devices, bit)
         chunks = chunks + [(back, mark ^ bit, lax.ppermute(rows, "seq", swap)) for back, mark, rows in chunks]
         bit //= 2
     return chunks
 
 
-def attend_kernel(full, fold, reach, tags, *refs):
-    refs = list(refs)
-    me_ref, ids_ref, request_ref, sq_ref = (refs.pop(0) for _ in range(4))
-    dq_refs = [refs.pop(0) for _ in range(full + fold)]
-    chunk_refs = [(refs.pop(0), refs.pop(0)) for _ in tags]
-    out_ref, bias, keys, values, query, scores = refs
+def attend_kernel(reach, tags, *refs):
+    me_ref, request_ref, sq_ref, own_ref = refs[:4]
+    far_refs, refs = refs[4 : 4 + KEY_VALUE_HEADS], refs[4 + KEY_VALUE_HEADS :]
+    chunk_refs = [(refs[2 * i], refs[2 * i + 1]) for i in range(len(tags))]
+    out_ref, bias, keys, values, query, scores = refs[2 * len(tags) :]
     head = pl.program_id(0)
     me = me_ref[0]
     tokens = sq_ref.shape[0]
+    for i, far_ref in enumerate(far_refs):
+
+        @pl.when(head == i)
+        def _(far_ref=far_ref):
+            correction = own_ref[...].astype(jnp.float32) + far_ref[...].astype(jnp.float32)
+            query[...] = (sq_ref[...].astype(jnp.float32) + correction).astype(jnp.bfloat16)
 
     @pl.when(head == 0)
     def _():
@@ -348,21 +423,8 @@
             keys[place, :] = k_ref[...]
             values[place, :HEAD_SIZE] = v_ref[...]
 
-    ids = ids_ref[...]
-    slots = dq_refs[0].shape[0]
-    delta = sq_ref[...].astype(jnp.float32)
-    correction = None
-    for b in range(full):
-        term = f32_dot(picks(ids, slots, b, 0), dq_refs[b][...])
-        correction = term if correction is None else correction + term
-    if fold:
-        shift = 4 * (head // (KEY_VALUE_HEADS // 2))
-        term = f32_dot(picks(ids, slots, full, shift), dq_refs[full][...])
-        correction = term if correction is None else correction + term
-    query[...] = (delta + correction).astype(jnp.bfloat16)
-
     factor = math.log2(math.e) / math.sqrt(HEAD_SIZE)
-    heads = sq_ref.shape[1] // HEAD_SIZE
+    heads = query.shape[1] // HEAD_SIZE
 
     def score(j):
         scores[j % 2] = lax.dot_general(
@@ -384,30 +446,23 @@
         ).astype(jnp.bfloat16)
 
 
-def attend(me, ids, requests, shared_query, dq, chunks, full, fold, reach):
+def attend(me, requests, shared_query, own, far, chunks, reach):
     tokens, query_width = shared_query.shape
-    slots = dq.shape[0]
     block = query_width // KEY_VALUE_HEADS
     in_specs = [
         pl.BlockSpec(memory_space=pltpu.SMEM),
-        pl.BlockSpec(ids.shape, lambda g: (0, 0)),
         pl.BlockSpec(requests.shape, lambda g: (0, 0)),
         pl.BlockSpec((tokens, block), lambda g: (0, g)),
-    ]
-    for b in range(full):
-        in_specs.append(pl.BlockSpec((slots, block), lambda g, b=b: (0, b * KEY_VALUE_HEADS + g)))
-    if fold:
-        in_specs.append(
-            pl.BlockSpec((slots, block), lambda g: (0, full * KEY_VALUE_HEADS + g % (KEY_VALUE_HEADS // 2)))
-        )
-    operands = [me, ids, requests, shared_query] + [dq] * (full + fold)
+        pl.BlockSpec((tokens, block), lambda g: (0, g)),
+    ] + [pl.BlockSpec((tokens, block), lambda g: (0, 0))] * len(far)
+    operands = [me, requests, shared_query, own, *far]
     for _, _, rows in chunks:
         in_specs.append(pl.BlockSpec((tokens, HEAD_SIZE), lambda g: (0, g)))
         in_specs.append(pl.BlockSpec((tokens, HEAD_SIZE), lambda g: (0, KEY_VALUE_HEADS + g)))
         operands += [rows, rows]
     window = (reach + 1) * tokens
     return pl.pallas_call(
-        functools.partial(attend_kernel, full, fold, reach, tuple((b, m) for b, m, _ in chunks)),
+        functools.partial(attend_kernel, reach, tuple((b, m) for b, m, _ in chunks)),
         grid=(KEY_VALUE_HEADS,),
         in_specs=in_specs,
         out_specs=pl.BlockSpec((tokens, block), lambda g: (0, g)),
@@ -452,25 +507,25 @@
     fours = -(-most // 4)
     full, fold = fours // 2, fours % 2
 
+    me = lax.axis_index("seq").astype(jnp.int32).reshape(1)
+    factors = adapter_up_query[0]
+    rank = factors.shape[0]
+    here = crossed(factors, devices)
     outgoing, ids = dispatch(normed, token_adapter, adapter_slot_table, full, fold)
-    incoming = exchange(outgoing, devices)
-    dkv, shrunk = project(incoming, adapter_down_factors, adapter_up_key_value, full, fold)
-    dkv = exchange(dkv, devices)
-    kv_width = shared_key_rows.shape[1]
-    dq = expand(shrunk, adapter_up_query, full, fold, 2 * kv_width)
-    kv = correct(ids, dkv, shared_key_rows, shared_value_rows, full, fold)
+    incoming = exchange(hold(outgoing, here), devices)
+    ups = gathered_factors(factors, here, devices)
+    early = [token(*(ups[k] for k in ups if k))]
+    back = exchange(project(incoming, jnp.swapaxes(adapter_down_factors, 1, 2), adapter_up_key_value, full, fold, *early), devices)
+    kv, shrunk = correct(ids, back, shared_key_rows, shared_value_rows, rank, full, fold)
+    swap = swap_pairs(devices, PLANE)
+    own, *far = expand(me, shrunk, lax.ppermute(shrunk, "seq", swap), ups)
     chunks = window_chunks(kv, devices, reach)
-    if tokens == devices * SUBLANES:
-        dq = exchange(append(kv, dq, *(rows for back, mark, rows in chunks if back and not mark)), devices)
-        pages = dq[:, -2 * kv_width :]
-    else:
-        dq = exchange(dq, devices)
-        pages = exchange(kv, devices)
-    me = lax.axis_index("seq").astype(jnp.int32).reshape(1)
-    attention = attend(
-        me, ids, token_request.reshape(devices, tokens), shared_query_rows, dq, chunks, full, fold, reach
-    )
-    return (attention, pages[:, :kv_width], pages[:, kv_width:])
+    pages = exchange(kv, devices)
+    far = [lax.ppermute(a, "seq", swap) for a in far]
+    requests = token_request.reshape(devices, tokens)
+    attention = attend(me, requests, shared_query_rows, own, far, chunks, reach)
+    width = pages.shape[1] // 2
+    return (attention, pages[:, :width], pages[:, width:])
 
 
 def solution(mesh):

time: 190 us -> 180 us (0.947)
  waiting for transfers between devices: 95.3 us -> 73.9 us
  starting transfers between devices: 27.8 us -> 36.7 us
  Pallas kernels: 23.5 us -> 29.6 us
  local copies, waits for them, and re-layouts: 13.5 us -> 8.87 us
    ppermute x0 -> x13, waiting for transfers between devices: none -> 68.8 us  [the longest x6 42 us: gathered_factors(): lax.ppermute(a, 'seq', swap)]
    all_to_all x2, waiting for transfers between devices: 53.4 us -> 3.99 us  [exchange(): lax.all_to_all(rows.reshape(devices, rows.shape[0] // devices, width), 's...]
    ppermute x9, waiting for transfers between devices: 36.3 us -> 1.05 us  [window_chunks(): lax.ppermute(rows, 'seq', swap)]
    ppermute x0 -> x13, starting transfers between devices: none -> 14.7 us  [the longest x6 4.11 us: gathered_factors(): lax.ppermute(a, 'seq', swap)]
    all_to_all x2, starting transfers between devices: 17.7 us -> 10.8 us  [exchange(): lax.all_to_all(rows.reshape(devices, rows.shape[0] // devices, width), 's...]
    ppermute x2, waiting for transfers between devices: 5.6 us -> 0.01 us  [window_chunks(): lax.ppermute(kv, 'seq', [(i, i + hop) for i in range(devices - hop)])]
    unnamed x37 -> x58, local copies, waits for them, and re-layouts: 12.8 us -> 8.12 us
    pallas_call x1, Pallas kernels: 2.5 us -> 4.85 us  [project(): pl.pallas_call(functools.partial(project_kernel, full, fold, steps), grid...]
  transfers between devices with their start and end apart: 13 -> 26, of which waited for: 7 -> 11; matrix products, arithmetic and copies ran while one was open for 4% -> 0% of each run, Pallas kernels for 2% -> 6%
where the time goes in v3:
time: 180 us; the launch traced here: 179 us
  waiting for transfers between devices  73.9 us (41%)
  starting transfers between devices  36.7 us (20%)
  Pallas kernels  29.6 us (16%)
  blocking collectives  27.9 us (16%)
  local copies, waits for them, and re-layouts  8.87 us (5%)
    ppermute x6, waiting for transfers between devices, gathered_factors(): lax.ppermute(a, 'seq', swap)  42 us
    all_to_all x1, blocking collectives, exchange(): lax.all_to_all(rows.reshape(devices, rows.shape[0] // devices, width), 's...  27.9 us
    ppermute x4, waiting for transfers between devices, local(): far = [lax.ppermute(a, 'seq', swap) for a in far]  17.5 us
    pallas_call x1, Pallas kernels, attend(): pl.pallas_call(functools.partial(attend_kernel, reach, tuple(((b, m) for...  12.7 us
    all_to_all x2, starting transfers between devices, exchange(): lax.all_to_all(rows.reshape(devices, rows.shape[0] // devices, width), 's...  10.8 us
    unnamed x58, local copies, waits for them, and re-layouts  8.12 us
    ppermute x2, starting transfers between devices, window_chunks(): lax.ppermute(kv, 'seq', [(i, i + hop) for i in range(devices - hop)])  6.89 us
    pallas_call x1, Pallas kernels, expand(): pl.pallas_call(functools.partial(expand_kernel, marks), grid=(KEY_VALUE_H...  5.5 us
  transfers between devices with their start and end apart: 26, of which 11 were waited for; matrix products, arithmetic and copies ran while one was open for 0% of the time, Pallas kernels for 6%

profile of v3, /device:TPU:0, one launch (start us, length us, event | category | flops | bytes accessed | tf_op | source)
XLA Modules:
  0.0 179.1 jit_solution(12587315135822232197)
XLA Ops:
  0.6 1.1 slice_select_fusion
  1.7 4.1 %collective-permute-start = (bf16[64,2048]{1,0:T(8,128)(2,1)S(1)}, bf16[64,2048]{1,0:T(8,128)(2,1)S(1)}, u32[]{:S(2)}, u32[]{:S(2)}) collective-permute-start(bf16[64,2048]{1,0:T(8,128)(2,1)S(1)} %slice_select_fusion), channel_id=1, source_target_pairs={{0,8},{1,9},{2,10},{3,11},{4,12},{5,13},{6,14},{7,15},{8,0},{9,1},... | collective-permute-start | bytes 786440 | tf_op jit(solution)/shard_map/ppermute | solution.py:340
  5.8 1.6 copy-done.1
  7.4 0.7 copy-done.6
  8.1 0.7 copy-done.7
  8.7 4.9 %dispatch.1 = (bf16[128,12288]{1,0:T(8,128)(2,1)}, s32[128,128]{1,0:T(8,128)S(1)}) custom-call(s32[1,128]{1,0:T(1,128)S(1)} %bitcast.15, s32[16]{0:T(128)S(1)} %copy-done.7, bf16[128,8192]{1,0:T(8,128)(2,1)S(1)} %copy-done.1, bf16[128,8192]{1,0:T(8,128)(2,1)S(1)} %copy-done.1), custom_call_target="tpu_custom_call" | custom-call | tf_op jit(solution)/shard_map/dispatch/pallas_call | solution.py:109
  13.6 4.1 %collective-permute-done.refs_1_ = bf16[64,2048]{1,0:T(8,128)(2,1)S(1)} collective-permute-done((bf16[64,2048]{1,0:T(8,128)(2,1)S(1)}, bf16[64,2048]{1,0:T(8,128)(2,1)S(1)}, u32[]{:S(2)}, u32[]{:S(2)}) %collective-permute-start) | collective-permute-done | bytes 262176 | tf_op jit(solution)/shard_map/ppermute | solution.py:340
  17.7 6.1 %all-to-all-start = ((bf16[16,8,12288]{2,1,0:T(8,128)(2,1)}), bf16[16,8,12288]{2,1,0:T(8,128)(2,1)}, u32[]{:S(2)}, u32[]{:S(2)}) async-start(bf16[16,8,12288]{2,1,0:T(8,128)(2,1)} %bitcast.4), calls=%async_computation | async-start | bytes 6291456 | tf_op jit(solution)/shard_map/all_to_all | solution.py:485
  23.8 0.0 copy-start.2
  23.8 1.6 collective-permute-start.1
  25.4 1.9 %collective-permute-start.2 = (bf16[64,4096]{1,0:T(8,128)(2,1)S(1)}, bf16[64,4096]{1,0:T(8,128)(2,1)S(1)}, u32[]{:S(2)}, u32[]{:S(2)}) collective-permute-start(bf16[64,4096]{1,0:T(8,128)(2,1)S(1)} %bitcast.19), channel_id=1, source_target_pairs={{0,2},{1,3},{2,0},{3,1},{4,6},{5,7},{6,4},{7,5},{8,10},{9,11},{10,... | collective-permute-start | bytes 1572872 | tf_op jit(solution)/shard_map/ppermute | solution.py:360
  27.2 5.2 %collective-permute-done.1 = bf16[64,2048]{1,0:T(8,128)(2,1)S(1)} collective-permute-done((bf16[64,2048]{1,0:T(8,128)(2,1)S(1)}, bf16[64,2048]{1,0:T(8,128)(2,1)S(1)}, u32[]{:S(2)}, u32[]{:S(2)}) %collective-permute-start.1) | collective-permute-done | bytes 262176 | tf_op jit(solution)/shard_map/ppermute | solution.py:353
  32.5 0.0 copy-start.9
  32.5 1.7 collective-permute-start.3
  34.3 0.0 collective-permute-start.4
  34.3 0.5 collective-permute-start.5
  34.8 29.1 %collective-permute-done.2.refs_1_.refs_4_ = bf16[64,4096]{1,0:T(8,128)(2,1)S(1)} collective-permute-done((bf16[64,4096]{1,0:T(8,128)(2,1)S(1)}, bf16[64,4096]{1,0:T(8,128)(2,1)S(1)}, u32[]{:S(2)}, u32[]{:S(2)}) %collective-permute-start.2) | collective-permute-done | bytes 524320 | tf_op jit(solution)/shard_map/ppermute | solution.py:360
  63.9 0.0 collective-permute-start.6
  63.9 12.9 %collective-permute-done.3.refs_2_.refs_8_ = bf16[64,4096]{1,0:T(8,128)(2,1)S(1)} collective-permute-done((bf16[64,4096]{1,0:T(8,128)(2,1)S(1)}, bf16[64,4096]{1,0:T(8,128)(2,1)S(1)}, u32[]{:S(2)}, u32[]{:S(2)}) %collective-permute-start.3) | collective-permute-done | bytes 524320 | tf_op jit(solution)/shard_map/ppermute | solution.py:360
  76.8 0.0 collective-permute-done.6.refs_5_
  76.8 0.8 copy-done.12
  77.5 0.3 copy-done.13
  77.8 0.1 copy-done.14
  77.9 0.8 copy-done.15
  78.7 0.0 collective-permute-done.7.refs_6_.refs_9_
  78.8 0.6 token_.1.refs_6_
  79.4 4.0 %all-to-all-done = bf16[16,8,12288]{2,1,0:T(8,128)(2,1)} async-done(((bf16[16,8,12288]{2,1,0:T(8,128)(2,1)}), bf16[16,8,12288]{2,1,0:T(8,128)(2,1)}, u32[]{:S(2)}, u32[]{:S(2)}) %all-to-all-start) | async-done | bytes 3145760 | tf_op jit(solution)/shard_map/all_to_all | solution.py:485
  83.4 1.9 %copy-done = bf16[1,8192,192]{1,2,0:T(8,128)(2,1)S(1)} copy-done((bf16[1,8192,192]{1,2,0:T(8,128)(2,1)S(1)}, bf16[1,8192,192]{1,2,0:T(8,128)(2,1)}, u32[]{:S(2)}) %copy-start) | copy-done | bytes 3145752
  85.2 0.7 copy-done.5
  85.9 4.9 %project.1 = bf16[128,1664]{1,0:T(8,128)(2,1)S(1)} custom-call(bf16[128,12288]{1,0:T(8,128)(2,1)} %bitcast.5.refs_0_.refs_1_.refs_2_, bf16[128,12288]{1,0:T(8,128)(2,1)} %bitcast.5.refs_0_.refs_1_.refs_2_, bf16[128,12288]{1,0:T(8,128)(2,1)} %bitcast.5.refs_0_.refs_1_.refs_2_, bf16[1,192,8192]{2,1,0:T(8,128)(2,1)S(1)} %bitcast.11, ...), custom_call_target="tpu_custom_call" | custom-call | tf_op jit(solution)/shard_map/project/pallas_call | solution.py:197
  90.8 27.9 %all_to_all.15 = bf16[16,8,1664]{2,1,0:T(8,128)(2,1)S(1)} all-to-all(bf16[16,8,1664]{2,1,0:T(8,128)(2,1)S(1)} %bitcast.14), channel_id=1, replica_groups=mesh['groups'=2,'seq'=16] {'seq'}, dimensions={0} | all-to-all | bytes 851968 | tf_op jit(solution)/shard_map/all_to_all | solution.py:485
  118.7 1.1 correct.1
  119.8 0.8 collective-permute-start.8
  120.6 3.1 %collective-permute-start.13 = (bf16[128,1024]{1,0:T(8,128)(2,1)}, bf16[128,1024]{1,0:T(8,128)(2,1)S(1)}, u32[]{:S(2)}, u32[]{:S(2)}) collective-permute-start(bf16[128,1024]{1,0:T(8,128)(2,1)} %get-tuple-element.20.refs_8_.refs_9_), channel_id=1, source_target_pairs={{0,4},{1,5},{2,6},{3,7},{4,8},{5,9},{6,10},{7,11},{8,12},{9,13},{1... | collective-permute-start | bytes 786440 | tf_op jit(solution)/shard_map/ppermute | solution.py:369
  123.7 3.8 %collective-permute-start.14 = (bf16[128,1024]{1,0:T(8,128)(2,1)}, bf16[128,1024]{1,0:T(8,128)(2,1)S(1)}, u32[]{:S(2)}, u32[]{:S(2)}) collective-permute-start(bf16[128,1024]{1,0:T(8,128)(2,1)} %get-tuple-element.20.refs_8_.refs_9_), channel_id=1, source_target_pairs={{0,8},{1,9},{2,10},{3,11},{4,12},{5,13},{6,14},{7,15},{16,24},{17,... | collective-permute-start | bytes 786440 | tf_op jit(solution)/shard_map/ppermute | solution.py:369
  127.5 0.1 collective-permute-start.15
  127.6 0.1 collective-permute-start.18
  127.7 0.0 collective-permute-done.8.refs_1_
  127.7 0.0 copy-start.28
  127.7 0.6 copy-done.28
  128.3 5.5 %expand.1 = (bf16[128,4096]{1,0:T(8,128)(2,1)}, bf16[128,1024]{1,0:T(8,128)(2,1)}, bf16[128,1024]{1,0:T(8,128)(2,1)}, bf16[128,1024]{1,0:T(8,128)(2,1)}, bf16[128,1024]{1,0:T(8,128)(2,1)}) custom-call(s32[1]{0:T(128)} %bitcast.me_ref.refs_0_, bf16[128,128]{1,0:T(8,128)(2,1)} %copy-done.8, bf16[128,128]{1,0:T(8,128)(2,1)} %copy-done.28, ...), custom_call_target="tpu_custom_call" | custom-call | flops 4294967296 | bytes 2097152 | tf_op jit(solution)/shard_map/expand/pallas_call | solution.py:289
  133.8 0.1 collective-permute-start.9
  133.9 4.8 %all-to-all-start.2 = ((bf16[16,8,1024]{2,1,0:T(8,128)(2,1)}), bf16[16,8,1024]{2,1,0:T(8,128)(2,1)S(1)}, u32[]{:S(2)}, u32[]{:S(2)}) async-start(bf16[16,8,1024]{2,1,0:T(8,128)(2,1)} %bitcast.9), calls=%async_computation.2 | async-start | bytes 524288 | tf_op jit(solution)/shard_map/all_to_all | solution.py:485
  138.7 0.0 collective-permute-done.13.refs_10_.refs_11_
  138.7 2.0 %collective-permute-start.10 = (bf16[128,1024]{1,0:T(8,128)(2,1)}, bf16[128,1024]{1,0:T(8,128)(2,1)S(1)}, u32[]{:S(2)}, u32[]{:S(2)}) collective-permute-start(bf16[128,1024]{1,0:T(8,128)(2,1)} %get-tuple-element.17), channel_id=1, source_target_pairs={{0,4},{1,5},{2,6},{3,7},{4,0},{5,1},{6,2},{7,3},{8,12},{9,13},{10,... | collective-permute-start | bytes 786440 | tf_op jit(solution)/shard_map/ppermute | solution.py:524
  140.7 1.1 collective-permute-start.11
  141.8 1.0 collective-permute-start.12
  142.7 1.5 collective-permute-start.16
  144.2 0.0 collective-permute-done.9.refs_4_
  144.2 2.1 %collective-permute-start.17 = (bf16[128,1024]{1,0:T(8,128)(2,1)S(1)}, bf16[128,1024]{1,0:T(8,128)(2,1)S(1)}, u32[]{:S(2)}, u32[]{:S(2)}) collective-permute-start(bf16[128,1024]{1,0:T(8,128)(2,1)S(1)} %collective-permute-done.14.refs_12_.refs_13_), channel_id=1, source_target_pairs={{0,2},{1,3},{2,0},{3,1},{4,6},{5,7},{6,4},{7,5},{8,10},{9,11},{10,... | collective-permute-start | bytes 786440 | tf_op jit(solution)/shard_map/ppermute | solution.py:373
  146.4 6.7 %collective-permute-done.10.refs_5_ = bf16[128,1024]{1,0:T(8,128)(2,1)S(1)} collective-permute-done((bf16[128,1024]{1,0:T(8,128)(2,1)}, bf16[128,1024]{1,0:T(8,128)(2,1)S(1)}, u32[]{:S(2)}, u32[]{:S(2)}) %collective-permute-start.10) | collective-permute-done | bytes 262176 | tf_op jit(solution)/shard_map/ppermute | solution.py:524
  153.1 5.6 %collective-permute-done.11.refs_6_ = bf16[128,1024]{1,0:T(8,128)(2,1)S(1)} collective-permute-done((bf16[128,1024]{1,0:T(8,128)(2,1)}, bf16[128,1024]{1,0:T(8,128)(2,1)S(1)}, u32[]{:S(2)}, u32[]{:S(2)}) %collective-permute-start.11) | collective-permute-done | bytes 262176 | tf_op jit(solution)/shard_map/ppermute | solution.py:524
  158.7 5.2 %collective-permute-done.12.refs_7_ = bf16[128,1024]{1,0:T(8,128)(2,1)S(1)} collective-permute-done((bf16[128,1024]{1,0:T(8,128)(2,1)}, bf16[128,1024]{1,0:T(8,128)(2,1)S(1)}, u32[]{:S(2)}, u32[]{:S(2)}) %collective-permute-start.12) | collective-permute-done | bytes 262176 | tf_op jit(solution)/shard_map/ppermute | solution.py:524
  163.9 0.0 collective-permute-start.21
  163.9 0.0 collective-permute-done.16.refs_16_.refs_17_
  163.9 0.5 collective-permute-start.22
  164.4 0.1 collective-permute-start.23
  164.5 0.0 all-to-all-done.2
  164.5 0.7 fusion
  165.2 0.0 collective-permute-done.19.refs_22_.refs_23_
  165.3 0.3 collective-permute-done.21.refs_26_.refs_27_
  165.5 0.4 collective-permute-done.22.refs_28_.refs_29_
  165.9 0.4 collective-permute-done.23.refs_30_.refs_31_
  166.4 12.7 %attend.1 = bf16[128,4096]{1,0:T(8,128)(2,1)} custom-call(s32[1]{0:T(128)} %bitcast.me_ref.refs_0_, s32[16,128]{1,0:T(8,128)} %bitcast.21, bf16[128,4096]{1,0:T(8,128)(2,1)} %refs_2_.1, bf16[128,4096]{1,0:T(8,128)(2,1)} %get-tuple-element.15.refs_3_, bf16[128,1024]{1,0:T(8,128)(2,1)} %copy-done.20, bf16[128,1024]{1,0:T(8,128)(2,1)} %copy-done.21, ...), custom_call_target="tpu_custom_call" | custom-call | flops 9663676416 | bytes 4194304 | tf_op jit(solution)/shard_map/attend/pallas_call | solution.py:464
  (58 shorter events, 0.2 us)
Async XLA Ops:
  1.7 16.0 %collective-permute-start = (bf16[64,2048]{1,0:T(8,128)(2,1)S(1)}, bf16[64,2048]{1,0:T(8,128)(2,1)S(1)}, u32[]{:S(2)}, u32[]{:S(2)}) collective-permute-start(bf16[64,2048]{1,0:T(8,128)(2,1)S(1)} %slice_select_fusion), channel_id=1, source_target_pairs={{0,8},{1,9},{2,10},{3,11},{4,12},{5,13},{6,14},{7,15},{8,0},{9,1},... | collective-permute-start | bytes 786440 | tf_op jit(solution)/shard_map/ppermute | solution.py:340
  5.8 1.6 copy-start.1
  7.4 0.7 copy-start.6
  8.1 0.7 copy-start.7
  17.7 7.6 %copy-start.10 = (bf16[1,64,4096]{2,1,0:T(8,128)(2,1)S(1)}, bf16[1,64,4096]{2,1,0:T(8,128)(2,1)}, u32[]{:S(2)}) copy-start(bf16[1,64,4096]{2,1,0:T(8,128)(2,1)} %param.17) | copy-start | bytes 1572868
  17.7 65.6 %all-to-all-start = ((bf16[16,8,12288]{2,1,0:T(8,128)(2,1)}), bf16[16,8,12288]{2,1,0:T(8,128)(2,1)}, u32[]{:S(2)}, u32[]{:S(2)}) async-start(bf16[16,8,12288]{2,1,0:T(8,128)(2,1)} %bitcast.4), calls=%async_computation | async-start | bytes 6291456 | tf_op jit(solution)/shard_map/all_to_all | solution.py:485
  23.8 59.6 %copy-start.2 = (bf16[1,2,64,512]{3,2,1,0:T(8,128)(2,1)S(1)}, bf16[1,2,64,512]{3,2,1,0:T(8,128)(2,1)}, u32[]{:S(2)}) copy-start(bf16[1,2,64,512]{3,2,1,0:T(8,128)(2,1)} %refs_5_.1) | copy-start | bytes 393220
  23.8 8.6 %collective-permute-start.1 = (bf16[64,2048]{1,0:T(8,128)(2,1)S(1)}, bf16[64,2048]{1,0:T(8,128)(2,1)S(1)}, u32[]{:S(2)}, u32[]{:S(2)}) collective-permute-start(bf16[64,2048]{1,0:T(8,128)(2,1)S(1)} %collective-permute-done.refs_1_), channel_id=1, source_target_pairs={{0,16},{16,0},{1,17},{17,1},{2,18},{18,2},{3,19},{19,3},{4,20},{20... | collective-permute-start | bytes 786440 | tf_op jit(solution)/shard_map/ppermute | solution.py:353
  25.4 38.5 %collective-permute-start.2 = (bf16[64,4096]{1,0:T(8,128)(2,1)S(1)}, bf16[64,4096]{1,0:T(8,128)(2,1)S(1)}, u32[]{:S(2)}, u32[]{:S(2)}) collective-permute-start(bf16[64,4096]{1,0:T(8,128)(2,1)S(1)} %bitcast.19), channel_id=1, source_target_pairs={{0,2},{1,3},{2,0},{3,1},{4,6},{5,7},{6,4},{7,5},{8,10},{9,11},{10,... | collective-permute-start | bytes 1572872 | tf_op jit(solution)/shard_map/ppermute | solution.py:360
  32.5 46.2 %copy-start.9 = (bf16[64,4096]{1,0:T(8,128)(2,1)}, bf16[64,4096]{1,0:T(8,128)(2,1)S(1)}, u32[]{:S(2)}) copy-start(bf16[64,4096]{1,0:T(8,128)(2,1)S(1)} %pad_maximum_fusion.refs_0_.refs_6_) | copy-start | bytes 1572868
  32.5 44.2 %collective-permute-start.3 = (bf16[64,4096]{1,0:T(8,128)(2,1)S(1)}, bf16[64,4096]{1,0:T(8,128)(2,1)S(1)}, u32[]{:S(2)}, u32[]{:S(2)}) collective-permute-start(bf16[64,4096]{1,0:T(8,128)(2,1)S(1)} %pad_maximum_fusion.refs_0_.refs_6_), channel_id=1, source_target_pairs={{0,2},{1,3},{2,0},{3,1},{4,6},{5,7},{6,4},{7,5},{8,10},{9,11},{10,... | collective-permute-start | bytes 1572872 | tf_op jit(solution)/shard_map/ppermute | solution.py:360
  34.3 42.5 %collective-permute-start.4 = (bf16[64,4096]{1,0:T(8,128)(2,1)S(1)}, bf16[64,4096]{1,0:T(8,128)(2,1)S(1)}, u32[]{:S(2)}, u32[]{:S(2)}) collective-permute-start(bf16[64,4096]{1,0:T(8,128)(2,1)S(1)} %bitcast.20), channel_id=1, source_target_pairs={{0,1},{1,0},{2,3},{3,2},{4,5},{5,4},{6,7},{7,6},{8,9},{9,8},{10,11... | collective-permute-start | bytes 1572872 | tf_op jit(solution)/shard_map/ppermute | solution.py:360
  34.3 42.5 %collective-permute-start.5 = (bf16[64,4096]{1,0:T(8,128)(2,1)S(1)}, bf16[64,4096]{1,0:T(8,128)(2,1)S(1)}, u32[]{:S(2)}, u32[]{:S(2)}) collective-permute-start(bf16[64,4096]{1,0:T(8,128)(2,1)S(1)} %pad_maximum_fusion.refs_0_.refs_6_), channel_id=1, source_target_pairs={{0,1},{1,0},{2,3},{3,2},{4,5},{5,4},{6,7},{7,6},{8,9},{9,8},{10,11... | collective-permute-start | bytes 1572872 | tf_op jit(solution)/shard_map/ppermute | solution.py:360
  63.9 14.9 %copy-start.11 = (bf16[64,4096]{1,0:T(8,128)(2,1)}, bf16[64,4096]{1,0:T(8,128)(2,1)S(1)}, u32[]{:S(2)}) copy-start(bf16[64,4096]{1,0:T(8,128)(2,1)S(1)} %collective-permute-done.2.refs_1_.refs_4_) | copy-start | bytes 1572868
  63.9 12.9 %collective-permute-start.6 = (bf16[64,4096]{1,0:T(8,128)(2,1)S(1)}, bf16[64,4096]{1,0:T(8,128)(2,1)S(1)}, u32[]{:S(2)}, u32[]{:S(2)}) collective-permute-start(bf16[64,4096]{1,0:T(8,128)(2,1)S(1)} %collective-permute-done.2.refs_1_.refs_4_), channel_id=1, source_target_pairs={{0,1},{1,0},{2,3},{3,2},{4,5},{5,4},{6,7},{7,6},{8,9},{9,8},{10,11... | collective-permute-start | bytes 1572872 | tf_op jit(solution)/shard_map/ppermute | solution.py:360
  76.7 0.8 copy-start.12
  76.7 2.0 %collective-permute-start.7 = (bf16[64,4096]{1,0:T(8,128)(2,1)S(1)}, bf16[64,4096]{1,0:T(8,128)(2,1)}, u32[]{:S(2)}, u32[]{:S(2)}) collective-permute-start(bf16[64,4096]{1,0:T(8,128)(2,1)S(1)} %collective-permute-done.3.refs_2_.refs_8_), channel_id=1, source_target_pairs={{0,1},{1,0},{2,3},{3,2},{4,5},{5,4},{6,7},{7,6},{8,9},{9,8},{10,11... | collective-permute-start | bytes 1572872 | tf_op jit(solution)/shard_map/ppermute | solution.py:360
  76.7 1.1 copy-start.13
  76.7 1.2 copy-start.14
  77.9 0.8 copy-start.15
  83.3 1.9 %copy-start = (bf16[1,8192,192]{1,2,0:T(8,128)(2,1)S(1)}, bf16[1,8192,192]{1,2,0:T(8,128)(2,1)}, u32[]{:S(2)}) copy-start(bf16[1,8192,192]{1,2,0:T(8,128)(2,1)} %param.16) | copy-start | bytes 9437188
  85.2 0.7 copy-start.5
  85.9 32.8 %copy-start.3 = (bf16[128,512]{1,0:T(8,128)(2,1)S(1)}, bf16[128,512]{1,0:T(8,128)(2,1)}, u32[]{:S(2)}) copy-start(bf16[128,512]{1,0:T(8,128)(2,1)} %sk_ref.1) | copy-start | bytes 393220
  85.9 32.8 %copy-start.4 = (bf16[128,512]{1,0:T(8,128)(2,1)S(1)}, bf16[128,512]{1,0:T(8,128)(2,1)}, u32[]{:S(2)}) copy-start(bf16[128,512]{1,0:T(8,128)(2,1)} %sv_ref.1) | copy-start | bytes 393220
  119.8 7.9 %copy-start.8 = (bf16[128,128]{1,0:T(8,128)(2,1)}, bf16[128,128]{1,0:T(8,128)(2,1)S(1)}, u32[]{:S(2)}) copy-start(bf16[128,128]{1,0:T(8,128)(2,1)S(1)} %get-tuple-element.14.refs_0_) | copy-start | bytes 98308
  119.8 7.9 %collective-permute-start.8 = (bf16[128,128]{1,0:T(8,128)(2,1)S(1)}, bf16[128,128]{1,0:T(8,128)(2,1)S(1)}, u32[]{:S(2)}, u32[]{:S(2)}) collective-permute-start(bf16[128,128]{1,0:T(8,128)(2,1)S(1)} %get-tuple-element.14.refs_0_), channel_id=1, source_target_pairs={{0,4},{1,5},{2,6},{3,7},{4,0},{5,1},{6,2},{7,3},{8,12},{9,13},{10,... | collective-permute-start | bytes 98312 | tf_op jit(solution)/shard_map/ppermute | solution.py:521
  120.6 18.0 %collective-permute-start.13 = (bf16[128,1024]{1,0:T(8,128)(2,1)}, bf16[128,1024]{1,0:T(8,128)(2,1)S(1)}, u32[]{:S(2)}, u32[]{:S(2)}) collective-permute-start(bf16[128,1024]{1,0:T(8,128)(2,1)} %get-tuple-element.20.refs_8_.refs_9_), channel_id=1, source_target_pairs={{0,4},{1,5},{2,6},{3,7},{4,8},{5,9},{6,10},{7,11},{8,12},{9,13},{1... | collective-permute-start | bytes 786440 | tf_op jit(solution)/shard_map/ppermute | solution.py:369
  123.7 17.0 %collective-permute-start.14 = (bf16[128,1024]{1,0:T(8,128)(2,1)}, bf16[128,1024]{1,0:T(8,128)(2,1)S(1)}, u32[]{:S(2)}, u32[]{:S(2)}) collective-permute-start(bf16[128,1024]{1,0:T(8,128)(2,1)} %get-tuple-element.20.refs_8_.refs_9_), channel_id=1, source_target_pairs={{0,8},{1,9},{2,10},{3,11},{4,12},{5,13},{6,14},{7,15},{16,24},{17,... | collective-permute-start | bytes 786440 | tf_op jit(solution)/shard_map/ppermute | solution.py:369
  127.5 14.2 %collective-permute-start.15 = (bf16[128,1024]{1,0:T(8,128)(2,1)}, bf16[128,1024]{1,0:T(8,128)(2,1)S(1)}, u32[]{:S(2)}, u32[]{:S(2)}) collective-permute-start(bf16[128,1024]{1,0:T(8,128)(2,1)} %get-tuple-element.20.refs_8_.refs_9_), channel_id=1, source_target_pairs={{0,2},{1,3},{2,0},{3,1},{4,6},{5,7},{6,4},{7,5},{8,10},{9,11},{10,... | collective-permute-start | bytes 786440 | tf_op jit(solution)/shard_map/ppermute | solution.py:373
  127.6 15.1 %collective-permute-start.18 = (bf16[128,1024]{1,0:T(8,128)(2,1)}, bf16[128,1024]{1,0:T(8,128)(2,1)S(1)}, u32[]{:S(2)}, u32[]{:S(2)}) collective-permute-start(bf16[128,1024]{1,0:T(8,128)(2,1)} %get-tuple-element.20.refs_8_.refs_9_), channel_id=1, source_target_pairs={{0,1},{1,0},{2,3},{3,2},{4,5},{5,4},{6,7},{7,6},{8,9},{9,8},{10,11... | collective-permute-start | bytes 786440 | tf_op jit(solution)/shard_map/ppermute | solution.py:373
  127.7 0.6 copy-start.28
  133.8 10.4 %collective-permute-start.9 = (bf16[128,1024]{1,0:T(8,128)(2,1)}, bf16[128,1024]{1,0:T(8,128)(2,1)S(1)}, u32[]{:S(2)}, u32[]{:S(2)}) collective-permute-start(bf16[128,1024]{1,0:T(8,128)(2,1)} %get-tuple-element.16), channel_id=1, source_target_pairs={{0,4},{1,5},{2,6},{3,7},{4,0},{5,1},{6,2},{7,3},{8,12},{9,13},{10,... | collective-permute-start | bytes 786440 | tf_op jit(solution)/shard_map/ppermute | solution.py:524
  133.9 30.6 %all-to-all-start.2 = ((bf16[16,8,1024]{2,1,0:T(8,128)(2,1)}), bf16[16,8,1024]{2,1,0:T(8,128)(2,1)S(1)}, u32[]{:S(2)}, u32[]{:S(2)}) async-start(bf16[16,8,1024]{2,1,0:T(8,128)(2,1)} %bitcast.9), calls=%async_computation.2 | async-start | bytes 524288 | tf_op jit(solution)/shard_map/all_to_all | solution.py:485
  138.7 27.6 %copy-start.16 = (bf16[128,1024]{1,0:T(8,128)(2,1)}, bf16[128,1024]{1,0:T(8,128)(2,1)S(1)}, u32[]{:S(2)}) copy-start(bf16[128,1024]{1,0:T(8,128)(2,1)S(1)} %collective-permute-done.13.refs_10_.refs_11_) | copy-start | bytes 786436
  138.7 14.3 %collective-permute-start.10 = (bf16[128,1024]{1,0:T(8,128)(2,1)}, bf16[128,1024]{1,0:T(8,128)(2,1)S(1)}, u32[]{:S(2)}, u32[]{:S(2)}) collective-permute-start(bf16[128,1024]{1,0:T(8,128)(2,1)} %get-tuple-element.17), channel_id=1, source_target_pairs={{0,4},{1,5},{2,6},{3,7},{4,0},{5,1},{6,2},{7,3},{8,12},{9,13},{10,... | collective-permute-start | bytes 786440 | tf_op jit(solution)/shard_map/ppermute | solution.py:524
  140.7 25.6 %copy-start.17 = (bf16[128,1024]{1,0:T(8,128)(2,1)}, bf16[128,1024]{1,0:T(8,128)(2,1)S(1)}, u32[]{:S(2)}) copy-start(bf16[128,1024]{1,0:T(8,128)(2,1)S(1)} %collective-permute-done.14.refs_12_.refs_13_) | copy-start | bytes 786436
  140.7 18.0 %collective-permute-start.11 = (bf16[128,1024]{1,0:T(8,128)(2,1)}, bf16[128,1024]{1,0:T(8,128)(2,1)S(1)}, u32[]{:S(2)}, u32[]{:S(2)}) collective-permute-start(bf16[128,1024]{1,0:T(8,128)(2,1)} %get-tuple-element.18), channel_id=1, source_target_pairs={{0,4},{1,5},{2,6},{3,7},{4,0},{5,1},{6,2},{7,3},{8,12},{9,13},{10,... | collective-permute-start | bytes 786440 | tf_op jit(solution)/shard_map/ppermute | solution.py:524
  141.8 24.6 %copy-start.18 = (bf16[128,1024]{1,0:T(8,128)(2,1)}, bf16[128,1024]{1,0:T(8,128)(2,1)S(1)}, u32[]{:S(2)}) copy-start(bf16[128,1024]{1,0:T(8,128)(2,1)S(1)} %collective-permute-done.15.refs_14_.refs_15_) | copy-start | bytes 786436
  141.8 22.1 %collective-permute-start.12 = (bf16[128,1024]{1,0:T(8,128)(2,1)}, bf16[128,1024]{1,0:T(8,128)(2,1)S(1)}, u32[]{:S(2)}, u32[]{:S(2)}) collective-permute-start(bf16[128,1024]{1,0:T(8,128)(2,1)} %get-tuple-element.19), channel_id=1, source_target_pairs={{0,4},{1,5},{2,6},{3,7},{4,0},{5,1},{6,2},{7,3},{8,12},{9,13},{10,... | collective-permute-start | bytes 786440 | tf_op jit(solution)/shard_map/ppermute | solution.py:524
  142.7 23.6 %copy-start.19 = (bf16[128,1024]{1,0:T(8,128)(2,1)}, bf16[128,1024]{1,0:T(8,128)(2,1)S(1)}, u32[]{:S(2)}) copy-start(bf16[128,1024]{1,0:T(8,128)(2,1)S(1)} %collective-permute-done.18.refs_20_.refs_21_) | copy-start | bytes 786436
  142.7 21.1 %collective-permute-start.16 = (bf16[128,1024]{1,0:T(8,128)(2,1)S(1)}, bf16[128,1024]{1,0:T(8,128)(2,1)S(1)}, u32[]{:S(2)}, u32[]{:S(2)}) collective-permute-start(bf16[128,1024]{1,0:T(8,128)(2,1)S(1)} %collective-permute-done.13.refs_10_.refs_11_), channel_id=1, source_target_pairs={{0,2},{1,3},{2,0},{3,1},{4,6},{5,7},{6,4},{7,5},{8,10},{9,11},{10,... | collective-permute-start | bytes 786440 | tf_op jit(solution)/shard_map/ppermute | solution.py:373
  144.2 22.1 %copy-start.20 = (bf16[128,1024]{1,0:T(8,128)(2,1)}, bf16[128,1024]{1,0:T(8,128)(2,1)S(1)}, u32[]{:S(2)}) copy-start(bf16[128,1024]{1,0:T(8,128)(2,1)S(1)} %collective-permute-done.9.refs_4_) | copy-start | bytes 786436
  144.2 20.2 %collective-permute-start.17 = (bf16[128,1024]{1,0:T(8,128)(2,1)S(1)}, bf16[128,1024]{1,0:T(8,128)(2,1)S(1)}, u32[]{:S(2)}, u32[]{:S(2)}) collective-permute-start(bf16[128,1024]{1,0:T(8,128)(2,1)S(1)} %collective-permute-done.14.refs_12_.refs_13_), channel_id=1, source_target_pairs={{0,2},{1,3},{2,0},{3,1},{4,6},{5,7},{6,4},{7,5},{8,10},{9,11},{10,... | collective-permute-start | bytes 786440 | tf_op jit(solution)/shard_map/ppermute | solution.py:373
  153.0 13.3 %copy-start.21 = (bf16[128,1024]{1,0:T(8,128)(2,1)}, bf16[128,1024]{1,0:T(8,128)(2,1)S(1)}, u32[]{:S(2)}) copy-start(bf16[128,1024]{1,0:T(8,128)(2,1)S(1)} %collective-permute-done.10.refs_5_) | copy-start | bytes 786436
  153.1 12.2 %collective-permute-start.19 = (bf16[128,1024]{1,0:T(8,128)(2,1)S(1)}, bf16[128,1024]{1,0:T(8,128)(2,1)S(1)}, u32[]{:S(2)}, u32[]{:S(2)}) collective-permute-start(bf16[128,1024]{1,0:T(8,128)(2,1)S(1)} %collective-permute-done.13.refs_10_.refs_11_), channel_id=1, source_target_pairs={{0,1},{1,0},{2,3},{3,2},{4,5},{5,4},{6,7},{7,6},{8,9},{9,8},{10,11... | collective-permute-start | bytes 786440 | tf_op jit(solution)/shard_map/ppermute | solution.py:373
  158.7 7.7 %copy-start.22 = (bf16[128,1024]{1,0:T(8,128)(2,1)}, bf16[128,1024]{1,0:T(8,128)(2,1)S(1)}, u32[]{:S(2)}) copy-start(bf16[128,1024]{1,0:T(8,128)(2,1)S(1)} %collective-permute-done.11.refs_6_) | copy-start | bytes 786436
  158.7 6.6 %collective-permute-start.20 = (bf16[128,1024]{1,0:T(8,128)(2,1)S(1)}, bf16[128,1024]{1,0:T(8,128)(2,1)S(1)}, u32[]{:S(2)}, u32[]{:S(2)}) collective-permute-start(bf16[128,1024]{1,0:T(8,128)(2,1)S(1)} %collective-permute-done.14.refs_12_.refs_13_), channel_id=1, source_target_pairs={{0,1},{1,0},{2,3},{3,2},{4,5},{5,4},{6,7},{7,6},{8,9},{9,8},{10,11... | collective-permute-start | bytes 786440 | tf_op jit(solution)/shard_map/ppermute | solution.py:373
  163.9 2.5 %copy-start.23 = (bf16[128,1024]{1,0:T(8,128)(2,1)}, bf16[128,1024]{1,0:T(8,128)(2,1)S(1)}, u32[]{:S(2)}) copy-start(bf16[128,1024]{1,0:T(8,128)(2,1)S(1)} %collective-permute-done.12.refs_7_) | copy-start | bytes 786436
  163.9 1.7 collective-permute-start.21
  163.9 2.5 %copy-start.24 = (bf16[128,1024]{1,0:T(8,128)(2,1)}, bf16[128,1024]{1,0:T(8,128)(2,1)S(1)}, u32[]{:S(2)}) copy-start(bf16[128,1024]{1,0:T(8,128)(2,1)S(1)} %collective-permute-done.16.refs_16_.refs_17_) | copy-start | bytes 786436
  163.9 2.0 %collective-permute-start.22 = (bf16[128,1024]{1,0:T(8,128)(2,1)S(1)}, bf16[128,1024]{1,0:T(8,128)(2,1)}, u32[]{:S(2)}, u32[]{:S(2)}) collective-permute-start(bf16[128,1024]{1,0:T(8,128)(2,1)S(1)} %collective-permute-done.16.refs_16_.refs_17_), channel_id=1, source_target_pairs={{0,1},{1,0},{2,3},{3,2},{4,5},{5,4},{6,7},{7,6},{8,9},{9,8},{10,11... | collective-permute-start | bytes 786440 | tf_op jit(solution)/shard_map/ppermute | solution.py:373
  164.4 2.0 %copy-start.25 = (bf16[128,1024]{1,0:T(8,128)(2,1)}, bf16[128,1024]{1,0:T(8,128)(2,1)S(1)}, u32[]{:S(2)}) copy-start(bf16[128,1024]{1,0:T(8,128)(2,1)S(1)} %collective-permute-done.17.refs_18_.refs_19_) | copy-start | bytes 786436
  164.4 1.9 %collective-permute-start.23 = (bf16[128,1024]{1,0:T(8,128)(2,1)S(1)}, bf16[128,1024]{1,0:T(8,128)(2,1)}, u32[]{:S(2)}, u32[]{:S(2)}) collective-permute-start(bf16[128,1024]{1,0:T(8,128)(2,1)S(1)} %collective-permute-done.17.refs_18_.refs_19_), channel_id=1, source_target_pairs={{0,1},{1,0},{2,3},{3,2},{4,5},{5,4},{6,7},{7,6},{8,9},{9,8},{10,11... | collective-permute-start | bytes 786440 | tf_op jit(solution)/shard_map/ppermute | solution.py:373
  165.2 1.1 copy-start.26
  165.3 1.1 copy-start.27

commit v4 on v3

--- a/solution.py
+++ b/solution.py
@@ -12,6 +12,8 @@
 HEAD_SIZE = 128
 SUBLANES = 8
 PLANE = 4
+FAR_PARTS = 1
+ATTEND_CALLS = 1
 MIB = 1024 * 1024
 
 
@@ -29,10 +31,6 @@
 
 def lane_iota(shape):
     return lax.broadcasted_iota(jnp.int32, shape, 1)
-
-
-def turned_dot(a, b):
-    return lax.dot_general(a, b, (((1,), (1,)), ((), ())), preferred_element_type=jnp.float32)
 
 
 def row_iota(shape):
@@ -143,10 +141,10 @@
 
     low, high = down_low[0], down_high[0]
     for b, (x_low, x_high) in enumerate(low_refs):
-        acc[b] += turned_dot(x_low[...], low) + turned_dot(x_high[...], high)
+        acc[b] += f32_dot(x_low[...], low) + f32_dot(x_high[...], high)
     if fold:
-        acc[full] += turned_dot(fold_ref[...], low)
-        acc[full + 1] += turned_dot(fold_ref[...], high)
+        acc[full] += f32_dot(fold_ref[...], low)
+        acc[full + 1] += f32_dot(fold_ref[...], high)
 
     @pl.when(step == steps - 1)
     def _():
@@ -176,7 +174,7 @@
 
 def project(x, down, up_kv, full, fold, *others):
     rows = x.shape[0]
-    _, ranks, width = down.shape
+    _, width, ranks = down.shape
     column = width // 8
     steps = width // 2 // column
     _, _, rank, kv_width = up_kv.shape
@@ -188,8 +186,8 @@
         in_specs.append(pl.BlockSpec((rows, column), lambda i: (0, 2 * full * steps + i)))
     blocks = len(in_specs)
     in_specs += [
-        pl.BlockSpec((1, ranks, column), lambda i: (0, 0, i)),
-        pl.BlockSpec((1, ranks, column), lambda i: (0, 0, steps + i)),
+        pl.BlockSpec((1, column, ranks), lambda i: (0, i, 0)),
+        pl.BlockSpec((1, column, ranks), lambda i: (0, steps + i, 0)),
         pl.BlockSpec(up_kv.shape, lambda i: (0, 0, 0, 0)),
     ]
     in_specs += [pl.BlockSpec(memory_space=pltpu.HBM)] * len(others)
@@ -249,24 +247,46 @@
     )(ids, back, shared_keys, shared_values)
 
 
-def expand_kernel(marks, me_ref, *refs):
-    shrunk_refs, refs = refs[:2], refs[2:]
+def packing(owner, me, rows):
+    tokens = owner.shape[0]
+    held = jnp.bitwise_and(jnp.bitwise_xor(owner, me), PLANE) == 0
+    flags = jnp.broadcast_to(held.astype(jnp.float32), (tokens, tokens)).astype(jnp.bfloat16)
+    before = (lane_iota((tokens, tokens)) < row_iota((tokens, tokens))).astype(jnp.bfloat16)
+    place = f32_dot(before, flags)[:, :1].astype(jnp.int32)
+    return ((place == lane_iota((tokens, rows))) & held).astype(jnp.bfloat16)
+
+
+def expand_kernel(marks, me_ref, own_rows_ref, far_rows_ref, kv_ref, *refs):
     up_refs, refs = refs[: len(marks)], refs[len(marks) :]
-    own_ref, far_refs, (wide, ups) = refs[0], refs[1:-2], refs[-2:]
+    (own_ref, unpack_ref, pages_ref), far_refs, (wide, ups) = refs[:3], refs[3:-2], refs[-2:]
     rank = up_refs[0].shape[0]
-    tokens = own_ref.shape[0]
+    tokens, packed = unpack_ref.shape
 
     @pl.when(pl.program_id(0) == 0)
     def _():
-        lanes = lane_iota((tokens, 2 * rank))
-        for i, shrunk_ref in enumerate(shrunk_refs):
-            rows = shrunk_ref[...].astype(jnp.float32)
-            apart = jnp.bitwise_xor(rows[:, rank : rank + 1].astype(jnp.int32), me_ref[0])
+        me = me_ref[0]
+        pages_ref[...] = kv_ref[...]
+
+        def owners(rows):
+            return rows[:, rank : rank + 1].astype(jnp.float32).astype(jnp.int32)
+
+        def widen(rows, owner, at):
+            count = rows.shape[0]
+            lanes = lane_iota((count, 2 * rank))
+            apart = jnp.bitwise_xor(owner, me)
             twice = jnp.where(lanes < rank, rows, pltpu.roll(rows, rank, 1))
             for k in range(0, len(marks), 2):
                 wanted = jnp.where(lanes < rank, marks[k], marks[k + 1])
                 held = jnp.where(apart == wanted, twice, 0.0).astype(jnp.bfloat16)
-                wide[i * tokens : (i + 1) * tokens, k * rank : (k + 2) * rank] = held
+                wide[at : at + count, k * rank : (k + 2) * rank] = held
+
+        own_rows, far_rows = own_rows_ref[...], far_rows_ref[...]
+        own_owner = owners(own_rows)
+        unpack_ref[...] = packing(own_owner, jnp.bitwise_xor(me, PLANE), packed)
+        widen(own_rows.astype(jnp.float32), own_owner, 0)
+        pack = packing(owners(far_rows), me, packed)
+        far_rows = lax.dot_general(pack, far_rows, (((0,), (0,)), ((), ())), preferred_element_type=jnp.float32)
+        widen(far_rows, owners(far_rows), tokens)
 
     for k, up_ref in enumerate(up_refs):
         ups[k * rank : (k + 1) * rank, :] = up_ref[...]
@@ -274,34 +294,46 @@
     own_ref[...] = result[:tokens]
     for i, far_ref in enumerate(far_refs):
 
-        @pl.when(pl.program_id(0) == i)
+        @pl.when(pl.program_id(0) * len(far_refs) // KEY_VALUE_HEADS == i)
         def _(far_ref=far_ref):
             far_ref[...] = result[tokens:]
 
 
-def expand(me, shrunk, far_shrunk, ups):
+def expand(me, shrunk, far_shrunk, kv, ups, packed):
     tokens = shrunk.shape[0]
     marks = tuple(sorted(ups))
     rank, width = ups[0].shape
     block = width // KEY_VALUE_HEADS
-    whole = pl.BlockSpec(shrunk.shape, lambda g: (0, 0))
-    part = pl.BlockSpec((tokens, block), lambda g: (0, g))
+    per = KEY_VALUE_HEADS // FAR_PARTS
+    whole = [pl.BlockSpec(a.shape, lambda g: (0, 0)) for a in (shrunk, shrunk, kv)]
     return pl.pallas_call(
         functools.partial(expand_kernel, marks),
         grid=(KEY_VALUE_HEADS,),
-        in_specs=[pl.BlockSpec(memory_space=pltpu.SMEM), whole, whole]
+        in_specs=[pl.BlockSpec(memory_space=pltpu.SMEM), *whole]
         + [pl.BlockSpec((rank, block), lambda g: (0, g))] * len(marks),
-        out_specs=[part] + [pl.BlockSpec((tokens, block), lambda g: (0, 0))] * KEY_VALUE_HEADS,
-        out_shape=[jax.ShapeDtypeStruct((tokens, width), jnp.bfloat16)]
-        + [jax.ShapeDtypeStruct((tokens, block), jnp.bfloat16)] * KEY_VALUE_HEADS,
+        out_specs=[
+            pl.BlockSpec((tokens, block), lambda g: (0, g)),
+            pl.BlockSpec((tokens, packed), lambda g: (0, 0)),
+            pl.BlockSpec(kv.shape, lambda g: (0, 0)),
+        ]
+        + [
+            pl.BlockSpec((packed, block), lambda g, i=i: (0, jnp.clip(g - i * per, 0, per - 1)))
+            for i in range(FAR_PARTS)
+        ],
+        out_shape=[
+            jax.ShapeDtypeStruct((tokens, width), jnp.bfloat16),
+            jax.ShapeDtypeStruct((tokens, packed), jnp.bfloat16),
+            jax.ShapeDtypeStruct(kv.shape, kv.dtype),
+        ]
+        + [jax.ShapeDtypeStruct((packed, per * block), jnp.bfloat16)] * FAR_PARTS,
         scratch_shapes=[
-            pltpu.VMEM((2 * tokens, len(marks) * rank), jnp.bfloat16),
+            pltpu.VMEM((tokens + packed, len(marks) * rank), jnp.bfloat16),
             pltpu.VMEM((len(marks) * rank, block), jnp.bfloat16),
         ],
-        compiler_params=params(60),
+        compiler_params=params(),
         cost_estimate=cost(16 * tokens * len(marks) * rank * width, 4 * tokens * width),
         name="expand",
-    )(me, shrunk, far_shrunk, *(ups[k] for k in marks))
+    )(me, shrunk, far_shrunk, kv, *(ups[k] for k in marks))
 
 
 def token_kernel(*refs):
@@ -311,10 +343,10 @@
 def token(*others):
     return pl.pallas_call(
         token_kernel,
-        in_specs=[pl.BlockSpec(memory_space=pltpu.HBM)] * len(others),
+        in_specs=[pl.BlockSpec(memory_space=pl.ANY)] * len(others),
         out_specs=pl.BlockSpec(memory_space=pltpu.VMEM),
         out_shape=jax.ShapeDtypeStruct((SUBLANES, 128), jnp.float32),
-        compiler_params=params(62),
+        compiler_params=params(),
         name="token",
     )(*others)
 
@@ -375,19 +407,19 @@
     return chunks
 
 
-def attend_kernel(reach, tags, *refs):
-    me_ref, request_ref, sq_ref, own_ref = refs[:4]
-    far_refs, refs = refs[4 : 4 + KEY_VALUE_HEADS], refs[4 + KEY_VALUE_HEADS :]
+def attend_kernel(reach, tags, parts, per, *refs):
+    me_ref, request_ref, sq_ref, own_ref, unpack_ref = refs[:5]
+    far_refs, refs = refs[5 : 5 + parts], refs[5 + parts :]
     chunk_refs = [(refs[2 * i], refs[2 * i + 1]) for i in range(len(tags))]
-    out_ref, bias, keys, values, query, scores = refs[2 * len(tags) :]
+    out_ref, bias, keys, values, query, scores = refs[-6:]
     head = pl.program_id(0)
     me = me_ref[0]
     tokens = sq_ref.shape[0]
     for i, far_ref in enumerate(far_refs):
 
-        @pl.when(head == i)
+        @pl.when(head // per == i)
         def _(far_ref=far_ref):
-            correction = own_ref[...].astype(jnp.float32) + far_ref[...].astype(jnp.float32)
+            correction = own_ref[...].astype(jnp.float32) + f32_dot(unpack_ref[...], far_ref[...])
             query[...] = (sq_ref[...].astype(jnp.float32) + correction).astype(jnp.bfloat16)
 
     @pl.when(head == 0)
@@ -446,26 +478,35 @@
         ).astype(jnp.bfloat16)
 
 
-def attend(me, requests, shared_query, own, far, chunks, reach):
+def attend(me, requests, shared_query, own, unpack, far, chunks, reach, first, into=None):
     tokens, query_width = shared_query.shape
     block = query_width // KEY_VALUE_HEADS
+    per = far[0].shape[1] // block
+    heads = len(far) * per
+    columns = pl.BlockSpec((tokens, block), lambda g: (0, first + g))
     in_specs = [
         pl.BlockSpec(memory_space=pltpu.SMEM),
         pl.BlockSpec(requests.shape, lambda g: (0, 0)),
-        pl.BlockSpec((tokens, block), lambda g: (0, g)),
-        pl.BlockSpec((tokens, block), lambda g: (0, g)),
-    ] + [pl.BlockSpec((tokens, block), lambda g: (0, 0))] * len(far)
-    operands = [me, requests, shared_query, own, *far]
+        columns,
+        columns,
+        pl.BlockSpec(unpack.shape, lambda g: (0, 0)),
+    ] + [pl.BlockSpec((a.shape[0], block), lambda g: (0, g % per)) for a in far]
+    operands = [me, requests, shared_query, own, unpack, *far]
     for _, _, rows in chunks:
-        in_specs.append(pl.BlockSpec((tokens, HEAD_SIZE), lambda g: (0, g)))
-        in_specs.append(pl.BlockSpec((tokens, HEAD_SIZE), lambda g: (0, KEY_VALUE_HEADS + g)))
+        in_specs.append(pl.BlockSpec((tokens, HEAD_SIZE), lambda g: (0, first + g)))
+        in_specs.append(pl.BlockSpec((tokens, HEAD_SIZE), lambda g: (0, KEY_VALUE_HEADS + first + g)))
         operands += [rows, rows]
+    aliases = {}
+    if into is not None:
+        aliases = {len(operands): 0}
+        in_specs.append(pl.BlockSpec(memory_space=pl.ANY))
+        operands.append(into)
     window = (reach + 1) * tokens
     return pl.pallas_call(
-        functools.partial(attend_kernel, reach, tuple((b, m) for b, m, _ in chunks)),
-        grid=(KEY_VALUE_HEADS,),
+        functools.partial(attend_kernel, reach, tuple((b, m) for b, m, _ in chunks), len(far), per),
+        grid=(heads,),
         in_specs=in_specs,
-        out_specs=pl.BlockSpec((tokens, block), lambda g: (0, g)),
+        out_specs=columns,
         out_shape=jax.ShapeDtypeStruct((tokens, query_width), jnp.bfloat16),
         scratch_shapes=[
             pltpu.VMEM((tokens, window), jnp.float32),
@@ -474,8 +515,9 @@
             pltpu.VMEM((tokens, block), jnp.bfloat16),
             pltpu.VMEM((2, tokens, window), jnp.float32),
         ],
+        input_output_aliases=aliases,
         compiler_params=params(60),
-        cost_estimate=cost(16 * tokens * query_width * window, 8 * tokens * query_width),
+        cost_estimate=cost(16 * heads * tokens * block * window, 8 * heads * tokens * block),
         name="attend",
     )(*operands)
 
@@ -515,15 +557,21 @@
     incoming = exchange(hold(outgoing, here), devices)
     ups = gathered_factors(factors, here, devices)
     early = [token(*(ups[k] for k in ups if k))]
-    back = exchange(project(incoming, jnp.swapaxes(adapter_down_factors, 1, 2), adapter_up_key_value, full, fold, *early), devices)
+    back = exchange(project(incoming, adapter_down_factors, adapter_up_key_value, full, fold, *early), devices)
     kv, shrunk = correct(ids, back, shared_key_rows, shared_value_rows, rank, full, fold)
     swap = swap_pairs(devices, PLANE)
-    own, *far = expand(me, shrunk, lax.ppermute(shrunk, "seq", swap), ups)
+    packed = min(tokens, -(-devices // 2 * most // 16) * 16)
+    far_shrunk = lax.ppermute(shrunk, "seq", swap)
+    own, unpack, pages, *far = expand(me, shrunk, far_shrunk, kv, ups, packed)
     chunks = window_chunks(kv, devices, reach)
-    pages = exchange(kv, devices)
+    pages = exchange(pages, devices)
     far = [lax.ppermute(a, "seq", swap) for a in far]
     requests = token_request.reshape(devices, tokens)
-    attention = attend(me, requests, shared_query_rows, own, far, chunks, reach)
+    attention = None
+    for i in range(ATTEND_CALLS):
+        some = far[i * FAR_PARTS // ATTEND_CALLS : (i + 1) * FAR_PARTS // ATTEND_CALLS]
+        first = i * KEY_VALUE_HEADS // ATTEND_CALLS
+        attention = attend(me, requests, shared_query_rows, own, unpack, some, chunks, reach, first, attention)
     width = pages.shape[1] // 2
     return (attention, pages[:, :width], pages[:, width:])
 

time: 180 us -> 172 us (0.956)
  local copies, waits for them, and re-layouts: 8.87 us -> 17.3 us
  waiting for transfers between devices: 73.9 us -> 67.6 us
  starting transfers between devices: 36.7 us -> 31.4 us
  Pallas kernels: 29.6 us -> 24.3 us
    ppermute x4 -> x1, waiting for transfers between devices: 17.5 us -> 0.01 us  [local(): far = [lax.ppermute(a, 'seq', swap) for a in far]]
    ppermute x9, waiting for transfers between devices: 1.05 us -> 13.8 us  [window_chunks(): lax.ppermute(rows, 'seq', swap)]
    unnamed x58 -> x39, local copies, waits for them, and re-layouts: 8.12 us -> 16.5 us
    ppermute x4 -> x1, starting transfers between devices: 4.09 us -> 0.01 us  [local(): far = [lax.ppermute(a, 'seq', swap) for a in far]]
    pallas_call x1, Pallas kernels: 4.85 us -> 2.5 us  [project(): pl.pallas_call(functools.partial(project_kernel, full, fold, steps), grid...]
    all_to_all x2, waiting for transfers between devices: 3.99 us -> 1.69 us  [exchange(): lax.all_to_all(rows.reshape(devices, rows.shape[0] // devices, width), 's...]
  transfers between devices with their start and end apart: 26 -> 23, of which waited for: 11 -> 8; matrix products, arithmetic and copies ran while one was open for 0% -> 4% of each run, Pallas kernels for 6% -> 5%
where the time goes in v4:
time: 172 us; the launch traced here: 171 us
  waiting for transfers between devices  67.6 us (39%)
  starting transfers between devices  31.4 us (18%)
  blocking collectives  27.5 us (16%)
  Pallas kernels  24.3 us (14%)
  local copies, waits for them, and re-layouts  17.3 us (10%)
  other arithmetic  1.95 us (1%)
    ppermute x6, waiting for transfers between devices, gathered_factors(): lax.ppermute(a, 'seq', swap)  41.4 us
    all_to_all x1, blocking collectives, exchange(): lax.all_to_all(rows.reshape(devices, rows.shape[0] // devices, width), 's...  27.5 us
    unnamed x39, local copies, waits for them, and re-layouts  16.5 us
    ppermute x9, waiting for transfers between devices, window_chunks(): lax.ppermute(rows, 'seq', swap)  13.8 us
    pallas_call x1, Pallas kernels, attend(): pl.pallas_call(functools.partial(attend_kernel, reach, tuple(((b, m) for...  12.6 us
    all_to_all x2, starting transfers between devices, exchange(): lax.all_to_all(rows.reshape(devices, rows.shape[0] // devices, width), 's...  10.7 us
    ppermute x2, starting transfers between devices, window_chunks(): lax.ppermute(kv, 'seq', [(i, i + hop) for i in range(devices - hop)])  5.77 us
    ppermute x1, waiting for transfers between devices, mirrored(): return lax.ppermute(rows, 'seq', swap_pairs(devices, devices // 2))  5.56 us
  transfers between devices with their start and end apart: 23, of which 8 were waited for; matrix products, arithmetic and copies ran while one was open for 4% of the time, Pallas kernels for 5%

profile of v4, /device:TPU:0, one launch (start us, length us, event | category | flops | bytes accessed | tf_op | source)
XLA Modules:
  0.0 170.9 jit_solution(6064441498669287641)
XLA Ops:
  0.6 1.1 slice_select_fusion
  1.7 4.1 %collective-permute-start = (bf16[64,2048]{1,0:T(8,128)(2,1)S(1)}, bf16[64,2048]{1,0:T(8,128)(2,1)S(1)}, u32[]{:S(2)}, u32[]{:S(2)}) collective-permute-start(bf16[64,2048]{1,0:T(8,128)(2,1)S(1)} %slice_select_fusion), channel_id=1, source_target_pairs={{0,8},{1,9},{2,10},{3,11},{4,12},{5,13},{6,14},{7,15},{8,0},{9,1},... | collective-permute-start | bytes 786440 | tf_op jit(solution)/shard_map/ppermute | solution.py:372
  5.8 1.6 copy-done.2
  7.4 0.7 copy-done.7
  8.1 0.7 copy-done.8
  8.7 3.5 %dispatch.1 = (bf16[128,12288]{1,0:T(8,128)(2,1)S(1)}, s32[128,128]{1,0:T(8,128)S(1)}) custom-call(s32[1,128]{1,0:T(1,128)S(1)} %bitcast.20, s32[16]{0:T(128)S(1)} %copy-done.8, bf16[128,8192]{1,0:T(8,128)(2,1)S(1)} %copy-done.2, bf16[128,8192]{1,0:T(8,128)(2,1)S(1)} %copy-done.2), custom_call_target="tpu_custom_call" | custom-call | tf_op jit(solution)/shard_map/dispatch/pallas_call | solution.py:107
  12.2 5.6 %collective-permute-done.refs_1_ = bf16[64,2048]{1,0:T(8,128)(2,1)S(1)} collective-permute-done((bf16[64,2048]{1,0:T(8,128)(2,1)S(1)}, bf16[64,2048]{1,0:T(8,128)(2,1)S(1)}, u32[]{:S(2)}, u32[]{:S(2)}) %collective-permute-start) | collective-permute-done | bytes 262176 | tf_op jit(solution)/shard_map/ppermute | solution.py:372
  17.7 1.6 copy-done.1
  19.3 5.9 %all-to-all-start = ((bf16[16,8,12288]{2,1,0:T(8,128)(2,1)}), bf16[16,8,12288]{2,1,0:T(8,128)(2,1)S(1)}, u32[]{:S(2)}, u32[]{:S(2)}) async-start(bf16[16,8,12288]{2,1,0:T(8,128)(2,1)} %bitcast.13), calls=%async_computation | async-start | bytes 6291456 | tf_op jit(solution)/shard_map/all_to_all | solution.py:527
  25.2 1.6 collective-permute-start.1
  26.8 1.9 %collective-permute-start.2 = (bf16[64,4096]{1,0:T(8,128)(2,1)}, bf16[64,4096]{1,0:T(8,128)(2,1)}, u32[]{:S(2)}, u32[]{:S(2)}) collective-permute-start(bf16[64,4096]{1,0:T(8,128)(2,1)} %bitcast.17), channel_id=1, source_target_pairs={{0,2},{1,3},{2,0},{3,1},{4,6},{5,7},{6,4},{7,5},{8,10},{9,11},{10,... | collective-permute-start | bytes 1572872 | tf_op jit(solution)/shard_map/ppermute | solution.py:392
  28.6 5.2 %collective-permute-done.1 = bf16[64,2048]{1,0:T(8,128)(2,1)S(1)} collective-permute-done((bf16[64,2048]{1,0:T(8,128)(2,1)S(1)}, bf16[64,2048]{1,0:T(8,128)(2,1)S(1)}, u32[]{:S(2)}, u32[]{:S(2)}) %collective-permute-start.1) | collective-permute-done | bytes 262176 | tf_op jit(solution)/shard_map/ppermute | solution.py:385
  33.9 0.1 broadcast_select_fusion.1
  33.9 0.8 pad_maximum_fusion.refs_0_.refs_4_
  34.7 1.7 collective-permute-start.3
  36.4 0.0 collective-permute-start.4
  36.4 0.5 collective-permute-start.5
  36.9 28.5 %collective-permute-done.2.refs_1_.refs_2_ = bf16[64,4096]{1,0:T(8,128)(2,1)} collective-permute-done((bf16[64,4096]{1,0:T(8,128)(2,1)}, bf16[64,4096]{1,0:T(8,128)(2,1)}, u32[]{:S(2)}, u32[]{:S(2)}) %collective-permute-start.2) | collective-permute-done | bytes 524320 | tf_op jit(solution)/shard_map/ppermute | solution.py:392
  65.5 0.0 collective-permute-start.6
  65.5 12.9 %collective-permute-done.3.refs_2_.refs_6_ = bf16[64,4096]{1,0:T(8,128)(2,1)} collective-permute-done((bf16[64,4096]{1,0:T(8,128)(2,1)}, bf16[64,4096]{1,0:T(8,128)(2,1)}, u32[]{:S(2)}, u32[]{:S(2)}) %collective-permute-start.3) | collective-permute-done | bytes 524320 | tf_op jit(solution)/shard_map/ppermute | solution.py:392
  78.3 0.0 collective-permute-start.7
  78.3 5.9 %copy.14.refs_3_.refs_4_ = bf16[1,8192,192]{2,1,0:T(8,128)(2,1)} copy(bf16[1,8192,192]{1,2,0:T(8,128)(2,1)} %param.16) | data formatting | bytes 6291456 | tf_op args[6]
  84.2 0.0 collective-permute-done.4.refs_3_.refs_1_
  84.2 0.0 collective-permute-done.5.refs_4_.refs_5_
  84.2 0.0 collective-permute-done.6.refs_5_.refs_3_
  84.2 0.0 collective-permute-done.7.refs_6_.refs_7_
  84.2 0.5 all-to-all-done
  84.7 0.4 copy-done.4
  85.1 2.2 %copy-done = bf16[1,8192,192]{2,1,0:T(8,128)(2,1)S(1)} copy-done((bf16[1,8192,192]{2,1,0:T(8,128)(2,1)S(1)}, bf16[1,8192,192]{2,1,0:T(8,128)(2,1)}, u32[]{:S(2)}) %copy-start) | copy-done | bytes 3145752
  87.3 2.5 %project.1 = bf16[128,1664]{1,0:T(8,128)(2,1)S(1)} custom-call(bf16[128,12288]{1,0:T(8,128)(2,1)S(1)} %bitcast.10, bf16[128,12288]{1,0:T(8,128)(2,1)S(1)} %bitcast.11, bf16[128,12288]{1,0:T(8,128)(2,1)S(1)} %bitcast.12, bf16[1,8192,192]{2,1,0:T(8,128)(2,1)S(1)} %copy-done, bf16[1,8192,192]{2,1,0:T(8,128)(2,1)S(1)} %copy-done, ...), custom_call_target="tpu_custom_call" | custom-call | tf_op jit(solution)/shard_map/project/pallas_call | solution.py:195
  89.8 27.5 %all_to_all.15 = bf16[16,8,1664]{2,1,0:T(8,128)(2,1)S(1)} all-to-all(bf16[16,8,1664]{2,1,0:T(8,128)(2,1)S(1)} %bitcast.15), channel_id=1, replica_groups=mesh['groups'=2,'seq'=16] {'seq'}, dimensions={0} | all-to-all | bytes 851968 | tf_op jit(solution)/shard_map/all_to_all | solution.py:527
  117.3 0.5 correct.1
  117.8 0.9 collective-permute-start.8
  118.7 1.1 collective-permute-start.12
  119.9 3.4 %collective-permute-start.11 = (bf16[128,1024]{1,0:T(8,128)(2,1)S(1)}, bf16[128,1024]{1,0:T(8,128)(2,1)S(1)}, u32[]{:S(2)}, u32[]{:S(2)}) collective-permute-start(bf16[128,1024]{1,0:T(8,128)(2,1)S(1)} %get-tuple-element.14.kv_ref.refs_6_.refs_7_), channel_id=1, source_target_pairs={{0,8},{1,9},{2,10},{3,11},{4,12},{5,13},{6,14},{7,15},{16,24},{17,... | collective-permute-start | bytes 786440 | tf_op jit(solution)/shard_map/ppermute | solution.py:401
  123.2 2.4 %collective-permute-start.10 = (bf16[128,1024]{1,0:T(8,128)(2,1)S(1)}, bf16[128,1024]{1,0:T(8,128)(2,1)S(1)}, u32[]{:S(2)}, u32[]{:S(2)}) collective-permute-start(bf16[128,1024]{1,0:T(8,128)(2,1)S(1)} %get-tuple-element.14.kv_ref.refs_6_.refs_7_), channel_id=1, source_target_pairs={{0,4},{1,5},{2,6},{3,7},{4,8},{5,9},{6,10},{7,11},{8,12},{9,13},{1... | collective-permute-start | bytes 786440 | tf_op jit(solution)/shard_map/ppermute | solution.py:401
  125.6 0.0 collective-permute-done.8.far_rows_ref
  125.7 0.0 copy-start.3
  125.7 1.0 copy-done.3
  126.7 5.2 %expand.1 = (bf16[128,4096]{1,0:T(8,128)(2,1)S(1)}, bf16[128,96]{1,0:T(8,128)(2,1)S(1)}, bf16[128,1024]{1,0:T(8,128)(2,1)}, bf16[96,4096]{1,0:T(8,128)(2,1)S(1)}) custom-call(s32[1]{0:T(128)} %bitcast.me_ref.refs_0_, bf16[128,128]{1,0:T(8,128)(2,1)S(1)} %get-tuple-element.13.own_rows_ref, bf16[128,128]{1,0:T(8,128)(2,1)S(1)} %collective-permute-done.8.far_rows_ref, ...), custom_call_target="tpu_custom_call" | custom-call | flops 4294967296 | bytes 2097152 | tf_op jit(solution)/shard_map/expand/pallas_call | solution.py:309
  131.9 1.0 copy-done.10
  132.9 0.6 copy-done.11
  133.6 0.0 collective-permute-start.9
  133.6 4.9 %all-to-all-start.2 = ((bf16[16,8,1024]{2,1,0:T(8,128)(2,1)}), bf16[16,8,1024]{2,1,0:T(8,128)(2,1)S(1)}, u32[]{:S(2)}, u32[]{:S(2)}) async-start(bf16[16,8,1024]{2,1,0:T(8,128)(2,1)} %bitcast.8), calls=%async_computation.2 | async-start | bytes 524288 | tf_op jit(solution)/shard_map/all_to_all | solution.py:527
  138.4 0.5 collective-permute-start.15
  138.9 0.0 collective-permute-done.12.refs_12_.refs_13_
  138.9 0.1 collective-permute-start.18
  139.0 0.0 collective-permute-done.11.refs_10_.refs_11_
  139.0 1.9 %collective-permute-start.14 = (bf16[128,1024]{1,0:T(8,128)(2,1)S(1)}, bf16[128,1024]{1,0:T(8,128)(2,1)}, u32[]{:S(2)}, u32[]{:S(2)}) collective-permute-start(bf16[128,1024]{1,0:T(8,128)(2,1)S(1)} %collective-permute-done.11.refs_10_.refs_11_), channel_id=1, source_target_pairs={{0,2},{1,3},{2,0},{3,1},{4,6},{5,7},{6,4},{7,5},{8,10},{9,11},{10,... | collective-permute-start | bytes 786440 | tf_op jit(solution)/shard_map/ppermute | solution.py:405
  141.0 0.1 collective-permute-start.13
  141.1 0.0 collective-permute-done.15.refs_18_.refs_19_
  141.1 0.0 collective-permute-start.17
  141.1 0.5 collective-permute-start.16
  141.6 7.6 %collective-permute-done.14.refs_16_.refs_17_ = bf16[128,1024]{1,0:T(8,128)(2,1)} collective-permute-done((bf16[128,1024]{1,0:T(8,128)(2,1)S(1)}, bf16[128,1024]{1,0:T(8,128)(2,1)}, u32[]{:S(2)}, u32[]{:S(2)}) %collective-permute-start.14) | collective-permute-done | bytes 262176 | tf_op jit(solution)/shard_map/ppermute | solution.py:405
  149.2 6.1 %collective-permute-done.13.refs_14_.refs_15_ = bf16[128,1024]{1,0:T(8,128)(2,1)} collective-permute-done((bf16[128,1024]{1,0:T(8,128)(2,1)S(1)}, bf16[128,1024]{1,0:T(8,128)(2,1)}, u32[]{:S(2)}, u32[]{:S(2)}) %collective-permute-start.13) | collective-permute-done | bytes 262176 | tf_op jit(solution)/shard_map/ppermute | solution.py:405
  155.3 0.0 collective-permute-start.19
  155.3 1.2 all-to-all-done.2
  156.5 0.7 fusion
  157.3 0.0 collective-permute-done.17.refs_22_.refs_23_
  157.3 0.0 collective-permute-done.20.refs_28_.refs_29_
  157.3 0.0 collective-permute-done.19.refs_26_.refs_27_
  157.4 0.6 copy-done.18
  158.0 0.3 copy-done.12
  158.2 12.6 %attend.1 = bf16[128,4096]{1,0:T(8,128)(2,1)} custom-call(s32[1]{0:T(128)} %bitcast.me_ref.refs_0_, s32[16,128]{1,0:T(8,128)} %bitcast.22, bf16[128,4096]{1,0:T(8,128)(2,1)} %refs_2_.1, bf16[128,4096]{1,0:T(8,128)(2,1)} %copy-done.10, bf16[128,96]{1,0:T(8,128)(2,1)} %copy-done.11, bf16[96,4096]{1,0:T(8,128)(2,1)} %copy-done.12, bf16[128,1024]{1,0:T(8,128)(2,1)} %copy-done.9, ...), custom_call_target="tpu_custom_call" | custom-call | flops 9663676416 | bytes 4194304 | tf_op jit(solution)/shard_map/attend/pallas_call | solution.py:505
  (33 shorter events, 0.1 us)
Async XLA Ops:
  1.7 16.0 %collective-permute-start = (bf16[64,2048]{1,0:T(8,128)(2,1)S(1)}, bf16[64,2048]{1,0:T(8,128)(2,1)S(1)}, u32[]{:S(2)}, u32[]{:S(2)}) collective-permute-start(bf16[64,2048]{1,0:T(8,128)(2,1)S(1)} %slice_select_fusion), channel_id=1, source_target_pairs={{0,8},{1,9},{2,10},{3,11},{4,12},{5,13},{6,14},{7,15},{8,0},{9,1},... | collective-permute-start | bytes 786440 | tf_op jit(solution)/shard_map/ppermute | solution.py:372
  5.8 1.6 copy-start.2
  7.4 0.7 copy-start.7
  8.1 0.7 copy-start.8
  17.7 1.6 copy-start.1
  19.3 65.4 %all-to-all-start = ((bf16[16,8,12288]{2,1,0:T(8,128)(2,1)}), bf16[16,8,12288]{2,1,0:T(8,128)(2,1)S(1)}, u32[]{:S(2)}, u32[]{:S(2)}) async-start(bf16[16,8,12288]{2,1,0:T(8,128)(2,1)} %bitcast.13), calls=%async_computation | async-start | bytes 6291456 | tf_op jit(solution)/shard_map/all_to_all | solution.py:527
  25.2 8.6 %collective-permute-start.1 = (bf16[64,2048]{1,0:T(8,128)(2,1)S(1)}, bf16[64,2048]{1,0:T(8,128)(2,1)S(1)}, u32[]{:S(2)}, u32[]{:S(2)}) collective-permute-start(bf16[64,2048]{1,0:T(8,128)(2,1)S(1)} %collective-permute-done.refs_1_), channel_id=1, source_target_pairs={{0,16},{16,0},{1,17},{17,1},{2,18},{18,2},{3,19},{19,3},{4,20},{20... | collective-permute-start | bytes 786440 | tf_op jit(solution)/shard_map/ppermute | solution.py:385
  26.8 38.7 %collective-permute-start.2 = (bf16[64,4096]{1,0:T(8,128)(2,1)}, bf16[64,4096]{1,0:T(8,128)(2,1)}, u32[]{:S(2)}, u32[]{:S(2)}) collective-permute-start(bf16[64,4096]{1,0:T(8,128)(2,1)} %bitcast.17), channel_id=1, source_target_pairs={{0,2},{1,3},{2,0},{3,1},{4,6},{5,7},{6,4},{7,5},{8,10},{9,11},{10,... | collective-permute-start | bytes 1572872 | tf_op jit(solution)/shard_map/ppermute | solution.py:392
  34.7 43.6 %collective-permute-start.3 = (bf16[64,4096]{1,0:T(8,128)(2,1)}, bf16[64,4096]{1,0:T(8,128)(2,1)}, u32[]{:S(2)}, u32[]{:S(2)}) collective-permute-start(bf16[64,4096]{1,0:T(8,128)(2,1)} %pad_maximum_fusion.refs_0_.refs_4_), channel_id=1, source_target_pairs={{0,2},{1,3},{2,0},{3,1},{4,6},{5,7},{6,4},{7,5},{8,10},{9,11},{10,... | collective-permute-start | bytes 1572872 | tf_op jit(solution)/shard_map/ppermute | solution.py:392
  36.4 47.8 %collective-permute-start.4 = (bf16[64,4096]{1,0:T(8,128)(2,1)}, bf16[64,4096]{1,0:T(8,128)(2,1)}, u32[]{:S(2)}, u32[]{:S(2)}) collective-permute-start(bf16[64,4096]{1,0:T(8,128)(2,1)} %bitcast.18), channel_id=1, source_target_pairs={{0,1},{1,0},{2,3},{3,2},{4,5},{5,4},{6,7},{7,6},{8,9},{9,8},{10,11... | collective-permute-start | bytes 1572872 | tf_op jit(solution)/shard_map/ppermute | solution.py:392
  36.4 47.8 %collective-permute-start.5 = (bf16[64,4096]{1,0:T(8,128)(2,1)}, bf16[64,4096]{1,0:T(8,128)(2,1)}, u32[]{:S(2)}, u32[]{:S(2)}) collective-permute-start(bf16[64,4096]{1,0:T(8,128)(2,1)} %pad_maximum_fusion.refs_0_.refs_4_), channel_id=1, source_target_pairs={{0,1},{1,0},{2,3},{3,2},{4,5},{5,4},{6,7},{7,6},{8,9},{9,8},{10,11... | collective-permute-start | bytes 1572872 | tf_op jit(solution)/shard_map/ppermute | solution.py:392
  65.5 18.8 %collective-permute-start.6 = (bf16[64,4096]{1,0:T(8,128)(2,1)}, bf16[64,4096]{1,0:T(8,128)(2,1)}, u32[]{:S(2)}, u32[]{:S(2)}) collective-permute-start(bf16[64,4096]{1,0:T(8,128)(2,1)} %collective-permute-done.2.refs_1_.refs_2_), channel_id=1, source_target_pairs={{0,1},{1,0},{2,3},{3,2},{4,5},{5,4},{6,7},{7,6},{8,9},{9,8},{10,11... | collective-permute-start | bytes 1572872 | tf_op jit(solution)/shard_map/ppermute | solution.py:392
  78.3 5.9 %collective-permute-start.7 = (bf16[64,4096]{1,0:T(8,128)(2,1)}, bf16[64,4096]{1,0:T(8,128)(2,1)}, u32[]{:S(2)}, u32[]{:S(2)}) collective-permute-start(bf16[64,4096]{1,0:T(8,128)(2,1)} %collective-permute-done.3.refs_2_.refs_6_), channel_id=1, source_target_pairs={{0,1},{1,0},{2,3},{3,2},{4,5},{5,4},{6,7},{7,6},{8,9},{9,8},{10,11... | collective-permute-start | bytes 1572872 | tf_op jit(solution)/shard_map/ppermute | solution.py:392
  84.2 0.9 copy-start.4
  85.1 2.2 %copy-start = (bf16[1,8192,192]{2,1,0:T(8,128)(2,1)S(1)}, bf16[1,8192,192]{2,1,0:T(8,128)(2,1)}, u32[]{:S(2)}) copy-start(bf16[1,8192,192]{2,1,0:T(8,128)(2,1)} %copy.14.refs_3_.refs_4_) | copy-start | bytes 9437188
  87.3 30.0 %copy-start.5 = (bf16[128,512]{1,0:T(8,128)(2,1)S(1)}, bf16[128,512]{1,0:T(8,128)(2,1)}, u32[]{:S(2)}) copy-start(bf16[128,512]{1,0:T(8,128)(2,1)} %sk_ref.1) | copy-start | bytes 393220
  87.3 30.0 %copy-start.6 = (bf16[128,512]{1,0:T(8,128)(2,1)S(1)}, bf16[128,512]{1,0:T(8,128)(2,1)}, u32[]{:S(2)}) copy-start(bf16[128,512]{1,0:T(8,128)(2,1)} %sv_ref.1) | copy-start | bytes 393220
  117.8 20.6 %copy-start.9 = (bf16[128,1024]{1,0:T(8,128)(2,1)}, bf16[128,1024]{1,0:T(8,128)(2,1)S(1)}, u32[]{:S(2)}) copy-start(bf16[128,1024]{1,0:T(8,128)(2,1)S(1)} %get-tuple-element.14.kv_ref.refs_6_.refs_7_) | copy-start | bytes 786436
  117.8 7.8 %collective-permute-start.8 = (bf16[128,128]{1,0:T(8,128)(2,1)S(1)}, bf16[128,128]{1,0:T(8,128)(2,1)S(1)}, u32[]{:S(2)}, u32[]{:S(2)}) collective-permute-start(bf16[128,128]{1,0:T(8,128)(2,1)S(1)} %get-tuple-element.13.own_rows_ref), channel_id=1, source_target_pairs={{0,4},{1,5},{2,6},{3,7},{4,0},{5,1},{6,2},{7,3},{8,12},{9,13},{10,... | collective-permute-start | bytes 98312 | tf_op jit(solution)/shard_map/ppermute | solution.py:564
  118.7 20.2 %collective-permute-start.12 = (bf16[128,1024]{1,0:T(8,128)(2,1)S(1)}, bf16[128,1024]{1,0:T(8,128)(2,1)S(1)}, u32[]{:S(2)}, u32[]{:S(2)}) collective-permute-start(bf16[128,1024]{1,0:T(8,128)(2,1)S(1)} %get-tuple-element.14.kv_ref.refs_6_.refs_7_), channel_id=1, source_target_pairs={{0,2},{1,3},{2,0},{3,1},{4,6},{5,7},{6,4},{7,5},{8,10},{9,11},{10,... | collective-permute-start | bytes 786440 | tf_op jit(solution)/shard_map/ppermute | solution.py:405
  119.9 19.2 %collective-permute-start.11 = (bf16[128,1024]{1,0:T(8,128)(2,1)S(1)}, bf16[128,1024]{1,0:T(8,128)(2,1)S(1)}, u32[]{:S(2)}, u32[]{:S(2)}) collective-permute-start(bf16[128,1024]{1,0:T(8,128)(2,1)S(1)} %get-tuple-element.14.kv_ref.refs_6_.refs_7_), channel_id=1, source_target_pairs={{0,8},{1,9},{2,10},{3,11},{4,12},{5,13},{6,14},{7,15},{16,24},{17,... | collective-permute-start | bytes 786440 | tf_op jit(solution)/shard_map/ppermute | solution.py:401
  123.2 17.7 %collective-permute-start.10 = (bf16[128,1024]{1,0:T(8,128)(2,1)S(1)}, bf16[128,1024]{1,0:T(8,128)(2,1)S(1)}, u32[]{:S(2)}, u32[]{:S(2)}) collective-permute-start(bf16[128,1024]{1,0:T(8,128)(2,1)S(1)} %get-tuple-element.14.kv_ref.refs_6_.refs_7_), channel_id=1, source_target_pairs={{0,4},{1,5},{2,6},{3,7},{4,8},{5,9},{6,10},{7,11},{8,12},{9,13},{1... | collective-permute-start | bytes 786440 | tf_op jit(solution)/shard_map/ppermute | solution.py:401
  125.7 1.0 copy-start.3
  131.9 1.0 copy-start.10
  132.9 0.6 copy-start.11
  133.6 23.7 %collective-permute-start.9 = (bf16[96,4096]{1,0:T(8,128)(2,1)S(1)}, bf16[96,4096]{1,0:T(8,128)(2,1)S(1)}, u32[]{:S(2)}, u32[]{:S(2)}) collective-permute-start(bf16[96,4096]{1,0:T(8,128)(2,1)S(1)} %get-tuple-element.17), channel_id=1, source_target_pairs={{0,4},{1,5},{2,6},{3,7},{4,0},{5,1},{6,2},{7,3},{8,12},{9,13},{10,... | collective-permute-start | bytes 2359304 | tf_op jit(solution)/shard_map/ppermute | solution.py:568
  133.6 23.0 %all-to-all-start.2 = ((bf16[16,8,1024]{2,1,0:T(8,128)(2,1)}), bf16[16,8,1024]{2,1,0:T(8,128)(2,1)S(1)}, u32[]{:S(2)}, u32[]{:S(2)}) async-start(bf16[16,8,1024]{2,1,0:T(8,128)(2,1)} %bitcast.8), calls=%async_computation.2 | async-start | bytes 524288 | tf_op jit(solution)/shard_map/all_to_all | solution.py:527
  138.4 2.6 %collective-permute-start.15 = (bf16[128,1024]{1,0:T(8,128)(2,1)S(1)}, bf16[128,1024]{1,0:T(8,128)(2,1)S(1)}, u32[]{:S(2)}, u32[]{:S(2)}) collective-permute-start(bf16[128,1024]{1,0:T(8,128)(2,1)S(1)} %get-tuple-element.14.kv_ref.refs_6_.refs_7_), channel_id=1, source_target_pairs={{0,1},{1,0},{2,3},{3,2},{4,5},{5,4},{6,7},{7,6},{8,9},{9,8},{10,11... | collective-permute-start | bytes 786440 | tf_op jit(solution)/shard_map/ppermute | solution.py:405
  138.9 18.4 %copy-start.13 = (bf16[128,1024]{1,0:T(8,128)(2,1)}, bf16[128,1024]{1,0:T(8,128)(2,1)S(1)}, u32[]{:S(2)}) copy-start(bf16[128,1024]{1,0:T(8,128)(2,1)S(1)} %collective-permute-done.12.refs_12_.refs_13_) | copy-start | bytes 786436
  138.9 2.2 %collective-permute-start.18 = (bf16[128,1024]{1,0:T(8,128)(2,1)S(1)}, bf16[128,1024]{1,0:T(8,128)(2,1)S(1)}, u32[]{:S(2)}, u32[]{:S(2)}) collective-permute-start(bf16[128,1024]{1,0:T(8,128)(2,1)S(1)} %collective-permute-done.12.refs_12_.refs_13_), channel_id=1, source_target_pairs={{0,1},{1,0},{2,3},{3,2},{4,5},{5,4},{6,7},{7,6},{8,9},{9,8},{10,11... | collective-permute-start | bytes 786440 | tf_op jit(solution)/shard_map/ppermute | solution.py:405
  139.0 18.3 %copy-start.14 = (bf16[128,1024]{1,0:T(8,128)(2,1)}, bf16[128,1024]{1,0:T(8,128)(2,1)S(1)}, u32[]{:S(2)}) copy-start(bf16[128,1024]{1,0:T(8,128)(2,1)S(1)} %collective-permute-done.11.refs_10_.refs_11_) | copy-start | bytes 786436
  139.0 10.2 %collective-permute-start.14 = (bf16[128,1024]{1,0:T(8,128)(2,1)S(1)}, bf16[128,1024]{1,0:T(8,128)(2,1)}, u32[]{:S(2)}, u32[]{:S(2)}) collective-permute-start(bf16[128,1024]{1,0:T(8,128)(2,1)S(1)} %collective-permute-done.11.refs_10_.refs_11_), channel_id=1, source_target_pairs={{0,2},{1,3},{2,0},{3,1},{4,6},{5,7},{6,4},{7,5},{8,10},{9,11},{10,... | collective-permute-start | bytes 786440 | tf_op jit(solution)/shard_map/ppermute | solution.py:405
  141.0 16.4 %copy-start.15 = (bf16[128,1024]{1,0:T(8,128)(2,1)}, bf16[128,1024]{1,0:T(8,128)(2,1)S(1)}, u32[]{:S(2)}) copy-start(bf16[128,1024]{1,0:T(8,128)(2,1)S(1)} %collective-permute-done.10.refs_8_.refs_9_) | copy-start | bytes 786436
  141.0 14.4 %collective-permute-start.13 = (bf16[128,1024]{1,0:T(8,128)(2,1)S(1)}, bf16[128,1024]{1,0:T(8,128)(2,1)}, u32[]{:S(2)}, u32[]{:S(2)}) collective-permute-start(bf16[128,1024]{1,0:T(8,128)(2,1)S(1)} %collective-permute-done.10.refs_8_.refs_9_), channel_id=1, source_target_pairs={{0,2},{1,3},{2,0},{3,1},{4,6},{5,7},{6,4},{7,5},{8,10},{9,11},{10,... | collective-permute-start | bytes 786440 | tf_op jit(solution)/shard_map/ppermute | solution.py:405
  141.1 16.3 %copy-start.16 = (bf16[128,1024]{1,0:T(8,128)(2,1)}, bf16[128,1024]{1,0:T(8,128)(2,1)S(1)}, u32[]{:S(2)}) copy-start(bf16[128,1024]{1,0:T(8,128)(2,1)S(1)} %collective-permute-done.15.refs_18_.refs_19_) | copy-start | bytes 786436
  141.1 16.2 %collective-permute-start.17 = (bf16[128,1024]{1,0:T(8,128)(2,1)S(1)}, bf16[128,1024]{1,0:T(8,128)(2,1)S(1)}, u32[]{:S(2)}, u32[]{:S(2)}) collective-permute-start(bf16[128,1024]{1,0:T(8,128)(2,1)S(1)} %collective-permute-done.11.refs_10_.refs_11_), channel_id=1, source_target_pairs={{0,1},{1,0},{2,3},{3,2},{4,5},{5,4},{6,7},{7,6},{8,9},{9,8},{10,11... | collective-permute-start | bytes 786440 | tf_op jit(solution)/shard_map/ppermute | solution.py:405
  141.1 16.3 %copy-start.17 = (bf16[128,1024]{1,0:T(8,128)(2,1)}, bf16[128,1024]{1,0:T(8,128)(2,1)S(1)}, u32[]{:S(2)}) copy-start(bf16[128,1024]{1,0:T(8,128)(2,1)S(1)} %collective-permute-done.18.refs_24_.refs_25_) | copy-start | bytes 786436
  141.1 16.2 %collective-permute-start.16 = (bf16[128,1024]{1,0:T(8,128)(2,1)S(1)}, bf16[128,1024]{1,0:T(8,128)(2,1)}, u32[]{:S(2)}, u32[]{:S(2)}) collective-permute-start(bf16[128,1024]{1,0:T(8,128)(2,1)S(1)} %collective-permute-done.10.refs_8_.refs_9_), channel_id=1, source_target_pairs={{0,1},{1,0},{2,3},{3,2},{4,5},{5,4},{6,7},{7,6},{8,9},{9,8},{10,11... | collective-permute-start | bytes 786440 | tf_op jit(solution)/shard_map/ppermute | solution.py:405
  149.2 8.0 %collective-permute-start.20 = (bf16[128,1024]{1,0:T(8,128)(2,1)}, bf16[128,1024]{1,0:T(8,128)(2,1)}, u32[]{:S(2)}, u32[]{:S(2)}) collective-permute-start(bf16[128,1024]{1,0:T(8,128)(2,1)} %collective-permute-done.14.refs_16_.refs_17_), channel_id=1, source_target_pairs={{0,1},{1,0},{2,3},{3,2},{4,5},{5,4},{6,7},{7,6},{8,9},{9,8},{10,11... | collective-permute-start | bytes 786440 | tf_op jit(solution)/shard_map/ppermute | solution.py:405
  155.3 1.9 %collective-permute-start.19 = (bf16[128,1024]{1,0:T(8,128)(2,1)}, bf16[128,1024]{1,0:T(8,128)(2,1)}, u32[]{:S(2)}, u32[]{:S(2)}) collective-permute-start(bf16[128,1024]{1,0:T(8,128)(2,1)} %collective-permute-done.13.refs_14_.refs_15_), channel_id=1, source_target_pairs={{0,1},{1,0},{2,3},{3,2},{4,5},{5,4},{6,7},{7,6},{8,9},{9,8},{10,11... | collective-permute-start | bytes 786440 | tf_op jit(solution)/shard_map/ppermute | solution.py:405
  157.3 0.7 copy-start.18
  157.3 0.9 copy-start.12

commit v5 on v3

--- a/solution.py
+++ b/solution.py
@@ -29,10 +29,6 @@
 
 def lane_iota(shape):
     return lax.broadcasted_iota(jnp.int32, shape, 1)
-
-
-def turned_dot(a, b):
-    return lax.dot_general(a, b, (((1,), (1,)), ((), ())), preferred_element_type=jnp.float32)
 
 
 def row_iota(shape):
@@ -143,10 +139,10 @@
 
     low, high = down_low[0], down_high[0]
     for b, (x_low, x_high) in enumerate(low_refs):
-        acc[b] += turned_dot(x_low[...], low) + turned_dot(x_high[...], high)
+        acc[b] += f32_dot(x_low[...], low) + f32_dot(x_high[...], high)
     if fold:
-        acc[full] += turned_dot(fold_ref[...], low)
-        acc[full + 1] += turned_dot(fold_ref[...], high)
+        acc[full] += f32_dot(fold_ref[...], low)
+        acc[full + 1] += f32_dot(fold_ref[...], high)
 
     @pl.when(step == steps - 1)
     def _():
@@ -176,7 +172,7 @@
 
 def project(x, down, up_kv, full, fold, *others):
     rows = x.shape[0]
-    _, ranks, width = down.shape
+    _, width, ranks = down.shape
     column = width // 8
     steps = width // 2 // column
     _, _, rank, kv_width = up_kv.shape
@@ -188,8 +184,8 @@
         in_specs.append(pl.BlockSpec((rows, column), lambda i: (0, 2 * full * steps + i)))
     blocks = len(in_specs)
     in_specs += [
-        pl.BlockSpec((1, ranks, column), lambda i: (0, 0, i)),
-        pl.BlockSpec((1, ranks, column), lambda i: (0, 0, steps + i)),
+        pl.BlockSpec((1, column, ranks), lambda i: (0, i, 0)),
+        pl.BlockSpec((1, column, ranks), lambda i: (0, steps + i, 0)),
         pl.BlockSpec(up_kv.shape, lambda i: (0, 0, 0, 0)),
     ]
     in_specs += [pl.BlockSpec(memory_space=pltpu.HBM)] * len(others)
@@ -249,59 +245,91 @@
     )(ids, back, shared_keys, shared_values)
 
 
-def expand_kernel(marks, me_ref, *refs):
-    shrunk_refs, refs = refs[:2], refs[2:]
+def packing(owner, me, rows):
+    tokens = owner.shape[0]
+    held = jnp.bitwise_and(jnp.bitwise_xor(owner, me), PLANE) == 0
+    flags = jnp.broadcast_to(held.astype(jnp.float32), (tokens, tokens)).astype(jnp.bfloat16)
+    before = (lane_iota((tokens, tokens)) < row_iota((tokens, tokens))).astype(jnp.bfloat16)
+    place = f32_dot(before, flags)[:, :1].astype(jnp.int32)
+    return ((place == lane_iota((tokens, rows))) & held).astype(jnp.bfloat16)
+
+
+def expand_kernel(marks, me_ref, own_rows_ref, far_rows_ref, kv_ref, sq_ref, *refs):
     up_refs, refs = refs[: len(marks)], refs[len(marks) :]
-    own_ref, far_refs, (wide, ups) = refs[0], refs[1:-2], refs[-2:]
+    query_ref, unpack_ref, pages_ref, far_ref, wide, ups, held, sems = refs
+    tokens, packed = unpack_ref.shape
+    parts, _, block = held.shape
     rank = up_refs[0].shape[0]
-    tokens = own_ref.shape[0]
-
-    @pl.when(pl.program_id(0) == 0)
-    def _():
-        lanes = lane_iota((tokens, 2 * rank))
-        for i, shrunk_ref in enumerate(shrunk_refs):
-            rows = shrunk_ref[...].astype(jnp.float32)
-            apart = jnp.bitwise_xor(rows[:, rank : rank + 1].astype(jnp.int32), me_ref[0])
-            twice = jnp.where(lanes < rank, rows, pltpu.roll(rows, rank, 1))
-            for k in range(0, len(marks), 2):
-                wanted = jnp.where(lanes < rank, marks[k], marks[k + 1])
-                held = jnp.where(apart == wanted, twice, 0.0).astype(jnp.bfloat16)
-                wide[i * tokens : (i + 1) * tokens, k * rank : (k + 2) * rank] = held
-
-    for k, up_ref in enumerate(up_refs):
-        ups[k * rank : (k + 1) * rank, :] = up_ref[...]
-    result = f32_dot(wide[...], ups[...]).astype(jnp.bfloat16)
-    own_ref[...] = result[:tokens]
-    for i, far_ref in enumerate(far_refs):
-
-        @pl.when(pl.program_id(0) == i)
-        def _(far_ref=far_ref):
-            far_ref[...] = result[tokens:]
-
-
-def expand(me, shrunk, far_shrunk, ups):
+    me = me_ref[0]
+
+    def fetches(g):
+        columns = slice(g * block, (g + 1) * block)
+        yield pltpu.make_async_copy(sq_ref.at[:, columns], held.at[g], sems.at[g, len(marks)])
+        for k, up_ref in enumerate(up_refs):
+            place = ups.at[g, k * rank : (k + 1) * rank, :]
+            yield pltpu.make_async_copy(up_ref.at[:, columns], place, sems.at[g, k])
+
+    for g in range(parts):
+        for copy in fetches(g):
+            copy.start()
+
+    pages_ref[...] = kv_ref[...]
+
+    def owners(rows):
+        return rows[:, rank : rank + 1].astype(jnp.float32).astype(jnp.int32)
+
+    def widen(rows, owner, at):
+        count = rows.shape[0]
+        lanes = lane_iota((count, 2 * rank))
+        apart = jnp.bitwise_xor(owner, me)
+        twice = jnp.where(lanes < rank, rows, pltpu.roll(rows, rank, 1))
+        for k in range(0, len(marks), 2):
+            wanted = jnp.where(lanes < rank, marks[k], marks[k + 1])
+            kept = jnp.where(apart == wanted, twice, 0.0).astype(jnp.bfloat16)
+            wide[at : at + count, k * rank : (k + 2) * rank] = kept
+
+    own_rows, far_rows = own_rows_ref[...], far_rows_ref[...]
+    own_owner = owners(own_rows)
+    unpack_ref[...] = packing(own_owner, jnp.bitwise_xor(me, PLANE), packed)
+    widen(own_rows.astype(jnp.float32), own_owner, 0)
+    pack = packing(owners(far_rows), me, packed)
+    far_rows = lax.dot_general(pack, far_rows, (((0,), (0,)), ((), ())), preferred_element_type=jnp.float32)
+    widen(far_rows, owners(far_rows), tokens)
+
+    for g in range(parts):
+        for copy in fetches(g):
+            copy.wait()
+        columns = slice(g * block, (g + 1) * block)
+        result = f32_dot(wide[...], ups[g]).astype(jnp.bfloat16)
+        own = result[:tokens].astype(jnp.float32)
+        query_ref[:, columns] = (held[g].astype(jnp.float32) + own).astype(jnp.bfloat16)
+        far_ref[:, columns] = result[tokens:]
+
+
+def expand(me, shrunk, far_shrunk, kv, shared_query, ups, packed):
     tokens = shrunk.shape[0]
     marks = tuple(sorted(ups))
     rank, width = ups[0].shape
     block = width // KEY_VALUE_HEADS
-    whole = pl.BlockSpec(shrunk.shape, lambda g: (0, 0))
-    part = pl.BlockSpec((tokens, block), lambda g: (0, g))
+    vmem, anywhere = pl.BlockSpec(memory_space=pltpu.VMEM), pl.BlockSpec(memory_space=pl.ANY)
     return pl.pallas_call(
         functools.partial(expand_kernel, marks),
-        grid=(KEY_VALUE_HEADS,),
-        in_specs=[pl.BlockSpec(memory_space=pltpu.SMEM), whole, whole]
-        + [pl.BlockSpec((rank, block), lambda g: (0, g))] * len(marks),
-        out_specs=[part] + [pl.BlockSpec((tokens, block), lambda g: (0, 0))] * KEY_VALUE_HEADS,
-        out_shape=[jax.ShapeDtypeStruct((tokens, width), jnp.bfloat16)]
-        + [jax.ShapeDtypeStruct((tokens, block), jnp.bfloat16)] * KEY_VALUE_HEADS,
+        in_specs=[pl.BlockSpec(memory_space=pltpu.SMEM)] + [vmem] * 3 + [anywhere] * (1 + len(marks)),
+        out_specs=[vmem] * 4,
+        out_shape=[
+            jax.ShapeDtypeStruct(shape, jnp.bfloat16)
+            for shape in ((tokens, width), (tokens, packed), kv.shape, (packed, width))
+        ],
         scratch_shapes=[
-            pltpu.VMEM((2 * tokens, len(marks) * rank), jnp.bfloat16),
-            pltpu.VMEM((len(marks) * rank, block), jnp.bfloat16),
+            pltpu.VMEM((tokens + packed, len(marks) * rank), jnp.bfloat16),
+            pltpu.VMEM((KEY_VALUE_HEADS, len(marks) * rank, block), jnp.bfloat16),
+            pltpu.VMEM((KEY_VALUE_HEADS, tokens, block), jnp.bfloat16),
+            pltpu.SemaphoreType.DMA((KEY_VALUE_HEADS, len(marks) + 1)),
         ],
         compiler_params=params(60),
         cost_estimate=cost(16 * tokens * len(marks) * rank * width, 4 * tokens * width),
         name="expand",
-    )(me, shrunk, far_shrunk, *(ups[k] for k in marks))
+    )(me, shrunk, far_shrunk, kv, shared_query, *(ups[k] for k in marks))
 
 
 def token_kernel(*refs):
@@ -311,10 +339,10 @@
 def token(*others):
     return pl.pallas_call(
         token_kernel,
-        in_specs=[pl.BlockSpec(memory_space=pltpu.HBM)] * len(others),
+        in_specs=[pl.BlockSpec(memory_space=pl.ANY)] * len(others),
         out_specs=pl.BlockSpec(memory_space=pltpu.VMEM),
         out_shape=jax.ShapeDtypeStruct((SUBLANES, 128), jnp.float32),
-        compiler_params=params(62),
+        compiler_params=params(),
         name="token",
     )(*others)
 
@@ -327,7 +355,7 @@
         out_specs=anywhere,
         out_shape=jax.ShapeDtypeStruct(rows.shape, rows.dtype),
         input_output_aliases={0: 0},
-        compiler_params=params(),
+        compiler_params=params(60),
         name="hold",
     )(rows, *others)
 
@@ -375,109 +403,130 @@
     return chunks
 
 
-def attend_kernel(reach, tags, *refs):
-    me_ref, request_ref, sq_ref, own_ref = refs[:4]
-    far_refs, refs = refs[4 : 4 + KEY_VALUE_HEADS], refs[4 + KEY_VALUE_HEADS :]
-    chunk_refs = [(refs[2 * i], refs[2 * i + 1]) for i in range(len(tags))]
-    out_ref, bias, keys, values, query, scores = refs[2 * len(tags) :]
-    head = pl.program_id(0)
+def attend_kernel(reach, tags, width, me_ref, request_ref, query_ref, unpack_ref, far_ref, *refs):
+    chunk_refs, refs = refs[: len(tags)], refs[len(tags) :]
+    out_ref, window, keys, values, query, scores, held, far_held, done, sems = refs
     me = me_ref[0]
-    tokens = sq_ref.shape[0]
-    for i, far_ref in enumerate(far_refs):
-
-        @pl.when(head == i)
-        def _(far_ref=far_ref):
-            correction = own_ref[...].astype(jnp.float32) + far_ref[...].astype(jnp.float32)
-            query[...] = (sq_ref[...].astype(jnp.float32) + correction).astype(jnp.bfloat16)
-
-    @pl.when(head == 0)
-    def _():
-        rows, lanes = row_iota((tokens, tokens)), lane_iota((tokens, tokens))
-        own = request_ref[pl.ds(me, 1), :].astype(jnp.float32)
-        own = jnp.sum(jnp.where(rows == lanes, own, 0.0), axis=1, keepdims=True)
-        for at in range(reach + 1):
-            source = me - reach + at
-            theirs = request_ref[pl.ds(jnp.maximum(source, 0), 1), :].astype(jnp.float32)
-            theirs = jnp.where(source >= 0, theirs, -1.0)
-            allowed = own == theirs
-            if at == reach:
-                allowed = allowed & (lanes <= rows)
-            bias[:, at * tokens : (at + 1) * tokens] = jnp.where(allowed, 0.0, -1e30)
-        values[:, HEAD_SIZE:] = jnp.ones((values.shape[0], HEAD_SIZE), jnp.bfloat16)
-
-    zeros = jnp.zeros((tokens, HEAD_SIZE), jnp.bfloat16)
-    for at in range(reach):
-
-        @pl.when(me - reach + at < 0)
-        def _(at=at):
-            keys[at * tokens : (at + 1) * tokens, :] = zeros
-            values[at * tokens : (at + 1) * tokens, :HEAD_SIZE] = zeros
-
-    for (back, mark), (k_ref, v_ref) in zip(tags, chunk_refs):
+    parts, tokens, block = held.shape
+    heads = block // HEAD_SIZE
+    last = len(tags)
+
+    def chunk_fetch(c):
+        back, mark = tags[c]
         source = (me // PLANE - back) * PLANE + jnp.bitwise_xor(me % PLANE, mark)
         at = source - me + reach
-
-        @pl.when((source >= 0) & (at >= 0) & (at <= reach))
-        def _(at=at, k_ref=k_ref, v_ref=v_ref):
-            place = pl.ds(pl.multiple_of(at * tokens, tokens), tokens)
-            keys[place, :] = k_ref[...]
-            values[place, :HEAD_SIZE] = v_ref[...]
-
+        place = pl.ds(pl.multiple_of(at * tokens, tokens), tokens)
+        copy = pltpu.make_async_copy(chunk_refs[c], window.at[place, :], sems.at[c])
+        return (source >= 0) & (at >= 0) & (at <= reach), copy
+
+    def columns(g):
+        return pl.ds(pl.multiple_of(g * block, block), block)
+
+    def query_fetches(g):
+        return [
+            pltpu.make_async_copy(query_ref.at[:, columns(g)], held.at[g], sems.at[last + g]),
+            pltpu.make_async_copy(far_ref.at[:, columns(g)], far_held.at[g], sems.at[last + parts + g]),
+        ]
+
+    def store(g):
+        return pltpu.make_async_copy(done.at[g], out_ref.at[:, columns(g)], sems.at[last + 2 * parts + g])
+
+    for copy in query_fetches(0):
+        copy.start()
+    for c in range(len(tags)):
+        wanted, copy = chunk_fetch(c)
+        pl.when(wanted)(copy.start)
+    for g in range(1, parts):
+        for copy in query_fetches(g):
+            copy.start()
+
+    rows, lanes = row_iota((tokens, tokens)), lane_iota((tokens, tokens))
+    own = request_ref[pl.ds(me, 1), :].astype(jnp.float32)
+    for at in range(reach + 1):
+        source = me - reach + at
+        span = slice(at * tokens, (at + 1) * tokens)
+        theirs = request_ref[pl.ds(jnp.maximum(source, 0), 1), :].astype(jnp.float32)
+        theirs = jnp.sum(jnp.where(rows == lanes, theirs, 0.0), axis=1, keepdims=True)
+        allowed = jnp.where(source >= 0, theirs, -1.0) == own
+        if at == reach:
+            allowed = allowed & (rows <= lanes)
+        keys[span, HEAD_SIZE:] = jnp.where(allowed, 0.0, -1e30).astype(jnp.bfloat16)
+
+        @pl.when(source < 0)
+        def _(span=span):
+            window[span, :] = jnp.zeros((tokens, 2 * width), jnp.bfloat16)
+
+    values[:, HEAD_SIZE:] = jnp.ones((values.shape[0], HEAD_SIZE), jnp.bfloat16)
+    for j in range(heads):
+        query[j, :, HEAD_SIZE:] = (rows == lanes).astype(jnp.bfloat16)
     factor = math.log2(math.e) / math.sqrt(HEAD_SIZE)
-    heads = query.shape[1] // HEAD_SIZE
-
-    def score(j):
-        scores[j % 2] = lax.dot_general(
-            query[:, j * HEAD_SIZE : (j + 1) * HEAD_SIZE],
-            keys[...],
-            (((1,), (1,)), ((), ())),
-            preferred_element_type=jnp.float32,
-        )
-
-    score(0)
-    for j in range(heads):
-        if j + 1 < heads:
-            score(j + 1)
-        masked = scores[j % 2] + bias[...]
-        raised = jnp.exp2((masked - jnp.max(masked, axis=1, keepdims=True)) * factor)
-        blended = f32_dot(raised.astype(jnp.bfloat16), values[...])
-        out_ref[:, j * HEAD_SIZE : (j + 1) * HEAD_SIZE] = (
-            blended[:, :HEAD_SIZE] / blended[:, HEAD_SIZE:]
-        ).astype(jnp.bfloat16)
-
-
-def attend(me, requests, shared_query, own, far, chunks, reach):
-    tokens, query_width = shared_query.shape
+    for c in range(len(tags)):
+        wanted, copy = chunk_fetch(c)
+        pl.when(wanted)(copy.wait)
+
+    @pl.loop(0, parts)
+    def _(g):
+        for copy in query_fetches(g):
+            copy.wait()
+        correction = f32_dot(unpack_ref[...], far_held[g])
+        corrected = (held[g].astype(jnp.float32) + correction).astype(jnp.bfloat16)
+        for j in range(heads):
+            query[j, :, 0:HEAD_SIZE] = corrected[:, j * HEAD_SIZE : (j + 1) * HEAD_SIZE]
+        at = pl.multiple_of(g * HEAD_SIZE, HEAD_SIZE)
+        keys[:, 0:HEAD_SIZE] = window[:, pl.ds(at, HEAD_SIZE)]
+        values[:, 0:HEAD_SIZE] = window[:, pl.ds(pl.multiple_of(width + at, HEAD_SIZE), HEAD_SIZE)]
+
+        def score(j):
+            stacked = query[4 * j : 4 * j + 4].reshape(4 * tokens, HEAD_SIZE + tokens)
+            scores[j % 2] = lax.dot_general(
+                stacked, keys[...], (((1,), (1,)), ((), ())), preferred_element_type=jnp.float32
+            )
+
+        score(0)
+        for j in range(heads // 4):
+            if j + 1 < heads // 4:
+                score(j + 1)
+            for k in range(2):
+                masked = scores[j % 2, 2 * k * tokens : 2 * (k + 1) * tokens]
+                raised = jnp.exp2((masked - jnp.max(masked, axis=1, keepdims=True)) * factor)
+                blended = f32_dot(raised.astype(jnp.bfloat16), values[...])
+                for i in range(2):
+                    head = 4 * j + 2 * k + i
+                    part = blended[i * tokens : (i + 1) * tokens]
+                    result = part[:, :HEAD_SIZE] / part[:, HEAD_SIZE:]
+                    done[g, :, head * HEAD_SIZE : (head + 1) * HEAD_SIZE] = result.astype(jnp.bfloat16)
+        store(g).start()
+
+    for g in range(parts):
+        store(g).wait()
+
+
+def attend(me, requests, query, unpack, far, chunks, reach):
+    tokens, query_width = query.shape
     block = query_width // KEY_VALUE_HEADS
-    in_specs = [
-        pl.BlockSpec(memory_space=pltpu.SMEM),
-        pl.BlockSpec(requests.shape, lambda g: (0, 0)),
-        pl.BlockSpec((tokens, block), lambda g: (0, g)),
-        pl.BlockSpec((tokens, block), lambda g: (0, g)),
-    ] + [pl.BlockSpec((tokens, block), lambda g: (0, 0))] * len(far)
-    operands = [me, requests, shared_query, own, *far]
-    for _, _, rows in chunks:
-        in_specs.append(pl.BlockSpec((tokens, HEAD_SIZE), lambda g: (0, g)))
-        in_specs.append(pl.BlockSpec((tokens, HEAD_SIZE), lambda g: (0, KEY_VALUE_HEADS + g)))
-        operands += [rows, rows]
-    window = (reach + 1) * tokens
+    length = (reach + 1) * tokens
+    width = chunks[0][2].shape[1] // 2
+    vmem, anywhere = pl.BlockSpec(memory_space=pltpu.VMEM), pl.BlockSpec(memory_space=pl.ANY)
     return pl.pallas_call(
-        functools.partial(attend_kernel, reach, tuple((b, m) for b, m, _ in chunks)),
-        grid=(KEY_VALUE_HEADS,),
-        in_specs=in_specs,
-        out_specs=pl.BlockSpec((tokens, block), lambda g: (0, g)),
+        functools.partial(attend_kernel, reach, tuple((b, m) for b, m, _ in chunks), width),
+        in_specs=[pl.BlockSpec(memory_space=pltpu.SMEM), vmem, anywhere, vmem] + [anywhere] * (1 + len(chunks)),
+        out_specs=anywhere,
         out_shape=jax.ShapeDtypeStruct((tokens, query_width), jnp.bfloat16),
         scratch_shapes=[
-            pltpu.VMEM((tokens, window), jnp.float32),
-            pltpu.VMEM((window, HEAD_SIZE), jnp.bfloat16),
-            pltpu.VMEM((window, 2 * HEAD_SIZE), jnp.bfloat16),
-            pltpu.VMEM((tokens, block), jnp.bfloat16),
-            pltpu.VMEM((2, tokens, window), jnp.float32),
+            pltpu.VMEM((length, 2 * width), jnp.bfloat16),
+            pltpu.VMEM((length, HEAD_SIZE + tokens), jnp.bfloat16),
+            pltpu.VMEM((length, 2 * HEAD_SIZE), jnp.bfloat16),
+            pltpu.VMEM((block // HEAD_SIZE, tokens, HEAD_SIZE + tokens), jnp.bfloat16),
+            pltpu.VMEM((2, 4 * tokens, length), jnp.float32),
+            pltpu.VMEM((KEY_VALUE_HEADS, tokens, block), jnp.bfloat16),
+            pltpu.VMEM((KEY_VALUE_HEADS, far.shape[0], block), jnp.bfloat16),
+            pltpu.VMEM((KEY_VALUE_HEADS, tokens, block), jnp.bfloat16),
+            pltpu.SemaphoreType.DMA((len(chunks) + 3 * KEY_VALUE_HEADS,)),
         ],
         compiler_params=params(60),
-        cost_estimate=cost(16 * tokens * query_width * window, 8 * tokens * query_width),
+        cost_estimate=cost(16 * tokens * query_width * length, 8 * tokens * query_width),
         name="attend",
-    )(*operands)
+    )(me, requests, query, unpack, far, *(rows for _, _, rows in chunks))
 
 
 def exchange(rows, devices):
@@ -515,15 +564,17 @@
     incoming = exchange(hold(outgoing, here), devices)
     ups = gathered_factors(factors, here, devices)
     early = [token(*(ups[k] for k in ups if k))]
-    back = exchange(project(incoming, jnp.swapaxes(adapter_down_factors, 1, 2), adapter_up_key_value, full, fold, *early), devices)
+    back = exchange(project(incoming, adapter_down_factors, adapter_up_key_value, full, fold, *early), devices)
     kv, shrunk = correct(ids, back, shared_key_rows, shared_value_rows, rank, full, fold)
     swap = swap_pairs(devices, PLANE)
-    own, *far = expand(me, shrunk, lax.ppermute(shrunk, "seq", swap), ups)
+    packed = min(tokens, -(-devices // 2 * most // 16) * 16)
+    far_shrunk = lax.ppermute(shrunk, "seq", swap)
+    query, unpack, pages, far = expand(me, shrunk, far_shrunk, kv, shared_query_rows, ups, packed)
     chunks = window_chunks(kv, devices, reach)
-    pages = exchange(kv, devices)
-    far = [lax.ppermute(a, "seq", swap) for a in far]
+    pages = exchange(pages, devices)
+    far = lax.ppermute(far, "seq", swap)
     requests = token_request.reshape(devices, tokens)
-    attention = attend(me, requests, shared_query_rows, own, far, chunks, reach)
+    attention = attend(me, requests, query, unpack, far, chunks, reach)
     width = pages.shape[1] // 2
     return (attention, pages[:, :width], pages[:, width:])
 

time: 180 us -> 168 us (0.933)
  waiting for transfers between devices: 73.9 us -> 66.4 us
  local copies, waits for them, and re-layouts: 8.87 us -> 16 us
  Pallas kernels: 29.6 us -> 22.9 us
  starting transfers between devices: 36.7 us -> 31.6 us
    ppermute x5 -> x2, waiting for transfers between devices: 17.5 us -> 0.01 us  [the longest x1 0.01 us: local(): far_shrunk = lax.ppermute(shrunk, 'seq', swap)]
    ppermute x9, waiting for transfers between devices: 1.05 us -> 13.4 us  [window_chunks(): lax.ppermute(rows, 'seq', swap)]
    unnamed x58 -> x47, local copies, waits for them, and re-layouts: 8.12 us -> 15.3 us
    ppermute x5 -> x2, starting transfers between devices: 4.93 us -> 0.98 us  [the longest x1 0.91 us: local(): far_shrunk = lax.ppermute(shrunk, 'seq', swap)]
    pallas_call x1, Pallas kernels: 4.85 us -> 2.5 us  [project(): pl.pallas_call(functools.partial(project_kernel, full, fold, steps), grid...]
  transfers between devices with their start and end apart: 26 -> 23, of which waited for: 11 -> 8; matrix products, arithmetic and copies ran while one was open for 0% -> 5% of each run, Pallas kernels for 6% -> 5%
where the time goes in v5:
time: 168 us; the launch traced here: 167 us
  waiting for transfers between devices  66.4 us (40%)
  starting transfers between devices  31.6 us (19%)
  blocking collectives  27.5 us (16%)
  Pallas kernels  22.9 us (14%)
  local copies, waits for them, and re-layouts  16 us (10%)
  other arithmetic  1.99 us (1%)
    ppermute x6, waiting for transfers between devices, gathered_factors(): lax.ppermute(a, 'seq', swap)  41.3 us
    all_to_all x1, blocking collectives, exchange(): lax.all_to_all(rows.reshape(devices, rows.shape[0] // devices, width), 's...  27.5 us
    unnamed x47, local copies, waits for them, and re-layouts  15.3 us
    ppermute x9, waiting for transfers between devices, window_chunks(): lax.ppermute(rows, 'seq', swap)  13.4 us
    pallas_call x1, Pallas kernels, attend(): pl.pallas_call(functools.partial(attend_kernel, reach, tuple(((b, m) for...  10.9 us
    all_to_all x2, starting transfers between devices, exchange(): lax.all_to_all(rows.reshape(devices, rows.shape[0] // devices, width), 's...  10.9 us
    ppermute x2, starting transfers between devices, window_chunks(): lax.ppermute(kv, 'seq', [(i, i + hop) for i in range(devices - hop)])  5.77 us
    pallas_call x1, Pallas kernels, expand(): pl.pallas_call(functools.partial(expand_kernel, marks), in_specs=[pl.Bloc...  5.6 us
  transfers between devices with their start and end apart: 23, of which 8 were waited for; matrix products, arithmetic and copies ran while one was open for 5% of the time, Pallas kernels for 5%

profile of v5, /device:TPU:0, one launch (start us, length us, event | category | flops | bytes accessed | tf_op | source)
XLA Modules:
  0.0 167.3 jit_solution(17321959916864530245)
XLA Ops:
  0.6 1.1 slice_select_fusion
  1.7 4.1 %collective-permute-start = (bf16[64,2048]{1,0:T(8,128)(2,1)S(1)}, bf16[64,2048]{1,0:T(8,128)(2,1)S(1)}, u32[]{:S(2)}, u32[]{:S(2)}) collective-permute-start(bf16[64,2048]{1,0:T(8,128)(2,1)S(1)} %slice_select_fusion), channel_id=1, source_target_pairs={{0,8},{1,9},{2,10},{3,11},{4,12},{5,13},{6,14},{7,15},{8,0},{9,1},... | collective-permute-start | bytes 786440 | tf_op jit(solution)/shard_map/ppermute | solution.py:368
  5.8 1.6 copy-done.2
  7.4 0.7 copy-done.6
  8.1 0.7 copy-done.7
  8.7 3.5 %dispatch.1 = (bf16[128,12288]{1,0:T(8,128)(2,1)S(1)}, s32[128,128]{1,0:T(8,128)S(1)}) custom-call(s32[1,128]{1,0:T(1,128)S(1)} %bitcast.16, s32[16]{0:T(128)S(1)} %copy-done.7, bf16[128,8192]{1,0:T(8,128)(2,1)S(1)} %copy-done.2, bf16[128,8192]{1,0:T(8,128)(2,1)S(1)} %copy-done.2), custom_call_target="tpu_custom_call" | custom-call | tf_op jit(solution)/shard_map/dispatch/pallas_call | solution.py:105
  12.2 1.6 copy-done.1
  13.8 3.9 %collective-permute-done.refs_1_ = bf16[64,2048]{1,0:T(8,128)(2,1)S(1)} collective-permute-done((bf16[64,2048]{1,0:T(8,128)(2,1)S(1)}, bf16[64,2048]{1,0:T(8,128)(2,1)S(1)}, u32[]{:S(2)}, u32[]{:S(2)}) %collective-permute-start) | collective-permute-done | bytes 262176 | tf_op jit(solution)/shard_map/ppermute | solution.py:368
  17.7 0.7 copy-done.10
  18.4 6.0 %all-to-all-start = ((bf16[16,8,12288]{2,1,0:T(8,128)(2,1)}), bf16[16,8,12288]{2,1,0:T(8,128)(2,1)S(1)}, u32[]{:S(2)}, u32[]{:S(2)}) async-start(bf16[16,8,12288]{2,1,0:T(8,128)(2,1)} %bitcast.13), calls=%async_computation | async-start | bytes 6291456 | tf_op jit(solution)/shard_map/all_to_all | solution.py:534
  24.5 1.6 collective-permute-start.1
  26.0 1.9 %collective-permute-start.2 = (bf16[64,4096]{1,0:T(8,128)(2,1)}, bf16[64,4096]{1,0:T(8,128)(2,1)}, u32[]{:S(2)}, u32[]{:S(2)}) collective-permute-start(bf16[64,4096]{1,0:T(8,128)(2,1)} %bitcast.19), channel_id=1, source_target_pairs={{0,2},{1,3},{2,0},{3,1},{4,6},{5,7},{6,4},{7,5},{8,10},{9,11},{10,... | collective-permute-start | bytes 1572872 | tf_op jit(solution)/shard_map/ppermute | solution.py:388
  27.9 5.2 %collective-permute-done.1 = bf16[64,2048]{1,0:T(8,128)(2,1)S(1)} collective-permute-done((bf16[64,2048]{1,0:T(8,128)(2,1)S(1)}, bf16[64,2048]{1,0:T(8,128)(2,1)S(1)}, u32[]{:S(2)}, u32[]{:S(2)}) %collective-permute-start.1) | collective-permute-done | bytes 262176 | tf_op jit(solution)/shard_map/ppermute | solution.py:381
  33.2 0.1 broadcast_select_fusion.1
  33.2 0.9 pad_maximum_fusion.refs_0_.refs_4_
  34.1 1.6 collective-permute-start.3
  35.7 0.0 collective-permute-start.4
  35.7 0.5 collective-permute-start.5
  36.3 28.4 %collective-permute-done.2.refs_1_.refs_2_ = bf16[64,4096]{1,0:T(8,128)(2,1)} collective-permute-done((bf16[64,4096]{1,0:T(8,128)(2,1)}, bf16[64,4096]{1,0:T(8,128)(2,1)}, u32[]{:S(2)}, u32[]{:S(2)}) %collective-permute-start.2) | collective-permute-done | bytes 524320 | tf_op jit(solution)/shard_map/ppermute | solution.py:388
  64.7 0.0 collective-permute-start.6
  64.7 12.9 %collective-permute-done.3.refs_2_.refs_6_ = bf16[64,4096]{1,0:T(8,128)(2,1)} collective-permute-done((bf16[64,4096]{1,0:T(8,128)(2,1)}, bf16[64,4096]{1,0:T(8,128)(2,1)}, u32[]{:S(2)}, u32[]{:S(2)}) %collective-permute-start.3) | collective-permute-done | bytes 524320 | tf_op jit(solution)/shard_map/ppermute | solution.py:388
  77.5 0.0 collective-permute-start.7
  77.5 5.9 %copy.14.refs_3_.refs_4_ = bf16[1,8192,192]{2,1,0:T(8,128)(2,1)} copy(bf16[1,8192,192]{1,2,0:T(8,128)(2,1)} %param.16) | data formatting | bytes 6291456 | tf_op args[6]
  83.4 0.0 collective-permute-done.4.refs_3_.refs_1_
  83.4 0.0 collective-permute-done.5.refs_4_.refs_5_
  83.4 0.0 collective-permute-done.6.refs_5_.refs_3_
  83.4 0.0 collective-permute-done.7.refs_6_.refs_7_
  83.5 0.5 all-to-all-done
  83.9 0.4 copy-done.3
  84.3 2.2 %copy-done = bf16[1,8192,192]{2,1,0:T(8,128)(2,1)S(1)} copy-done((bf16[1,8192,192]{2,1,0:T(8,128)(2,1)S(1)}, bf16[1,8192,192]{2,1,0:T(8,128)(2,1)}, u32[]{:S(2)}) %copy-start) | copy-done | bytes 3145752
  86.5 2.5 %project.1 = bf16[128,1664]{1,0:T(8,128)(2,1)S(1)} custom-call(bf16[128,12288]{1,0:T(8,128)(2,1)S(1)} %bitcast.10, bf16[128,12288]{1,0:T(8,128)(2,1)S(1)} %bitcast.11, bf16[128,12288]{1,0:T(8,128)(2,1)S(1)} %bitcast.12, bf16[1,8192,192]{2,1,0:T(8,128)(2,1)S(1)} %copy-done, bf16[1,8192,192]{2,1,0:T(8,128)(2,1)S(1)} %copy-done, ...), custom_call_target="tpu_custom_call" | custom-call | tf_op jit(solution)/shard_map/project/pallas_call | solution.py:193
  89.0 27.5 %all_to_all.15 = bf16[16,8,1664]{2,1,0:T(8,128)(2,1)S(1)} all-to-all(bf16[16,8,1664]{2,1,0:T(8,128)(2,1)S(1)} %bitcast.15), channel_id=1, replica_groups=mesh['groups'=2,'seq'=16] {'seq'}, dimensions={0} | all-to-all | bytes 851968 | tf_op jit(solution)/shard_map/all_to_all | solution.py:534
  116.6 0.5 correct.1
  117.0 0.0 copy-start.9
  117.0 0.9 collective-permute-start.8
  118.0 1.1 collective-permute-start.12
  119.1 3.4 %collective-permute-start.11 = (bf16[128,1024]{1,0:T(8,128)(2,1)S(1)}, bf16[128,1024]{1,0:T(8,128)(2,1)S(1)}, u32[]{:S(2)}, u32[]{:S(2)}) collective-permute-start(bf16[128,1024]{1,0:T(8,128)(2,1)S(1)} %get-tuple-element.14.kv_ref.refs_0_), channel_id=1, source_target_pairs={{0,8},{1,9},{2,10},{3,11},{4,12},{5,13},{6,14},{7,15},{16,24},{17,... | collective-permute-start | bytes 786440 | tf_op jit(solution)/shard_map/ppermute | solution.py:397
  122.5 2.4 %collective-permute-start.10 = (bf16[128,1024]{1,0:T(8,128)(2,1)S(1)}, bf16[128,1024]{1,0:T(8,128)(2,1)S(1)}, u32[]{:S(2)}, u32[]{:S(2)}) collective-permute-start(bf16[128,1024]{1,0:T(8,128)(2,1)S(1)} %get-tuple-element.14.kv_ref.refs_0_), channel_id=1, source_target_pairs={{0,4},{1,5},{2,6},{3,7},{4,8},{5,9},{6,10},{7,11},{8,12},{9,13},{1... | collective-permute-start | bytes 786440 | tf_op jit(solution)/shard_map/ppermute | solution.py:397
  124.9 0.0 collective-permute-done.8.far_rows_ref
  124.9 0.0 copy-start.22
  124.9 0.6 copy-done.22
  125.5 5.6 %expand.1 = (bf16[128,4096]{1,0:T(8,128)(2,1)}, bf16[128,96]{1,0:T(8,128)(2,1)}, bf16[128,1024]{1,0:T(8,128)(2,1)}, bf16[96,4096]{1,0:T(8,128)(2,1)}) custom-call(s32[1]{0:T(128)} %bitcast.me_ref, bf16[128,128]{1,0:T(8,128)(2,1)} %copy-done.9, bf16[128,128]{1,0:T(8,128)(2,1)} %copy-done.22, bf16[128,1024]{1,0:T(8,128)(2,1)} %copy-done.8, ...), custom_call_target="tpu_custom_call" | custom-call | flops 4294967296 | bytes 2097152 | tf_op jit(solution)/shard_map/expand/pallas_call | solution.py:315
  131.1 0.1 collective-permute-start.9
  131.2 4.9 %all-to-all-start.2 = ((bf16[16,8,1024]{2,1,0:T(8,128)(2,1)}), bf16[16,8,1024]{2,1,0:T(8,128)(2,1)S(1)}, u32[]{:S(2)}, u32[]{:S(2)}) async-start(bf16[16,8,1024]{2,1,0:T(8,128)(2,1)} %bitcast.22), calls=%async_computation.2 | async-start | bytes 524288 | tf_op jit(solution)/shard_map/all_to_all | solution.py:534
  136.0 0.4 collective-permute-start.15
  136.5 0.0 collective-permute-done.12.refs_3_
  136.5 0.2 collective-permute-start.18
  136.6 1.9 %collective-permute-start.14 = (bf16[128,1024]{1,0:T(8,128)(2,1)S(1)}, bf16[128,1024]{1,0:T(8,128)(2,1)S(1)}, u32[]{:S(2)}, u32[]{:S(2)}) collective-permute-start(bf16[128,1024]{1,0:T(8,128)(2,1)S(1)} %collective-permute-done.11.refs_2_), channel_id=1, source_target_pairs={{0,2},{1,3},{2,0},{3,1},{4,6},{5,7},{6,4},{7,5},{8,10},{9,11},{10,... | collective-permute-start | bytes 786440 | tf_op jit(solution)/shard_map/ppermute | solution.py:401
  138.5 0.0 collective-permute-done.10.refs_1_
  138.5 0.2 collective-permute-start.13
  138.7 0.0 collective-permute-done.15.refs_6_
  138.7 0.0 collective-permute-start.17
  138.7 0.5 collective-permute-start.16
  139.2 7.5 %collective-permute-done.14.refs_5_ = bf16[128,1024]{1,0:T(8,128)(2,1)S(1)} collective-permute-done((bf16[128,1024]{1,0:T(8,128)(2,1)S(1)}, bf16[128,1024]{1,0:T(8,128)(2,1)S(1)}, u32[]{:S(2)}, u32[]{:S(2)}) %collective-permute-start.14) | collective-permute-done | bytes 262176 | tf_op jit(solution)/shard_map/ppermute | solution.py:401
  146.7 5.8 %collective-permute-done.13.refs_4_ = bf16[128,1024]{1,0:T(8,128)(2,1)S(1)} collective-permute-done((bf16[128,1024]{1,0:T(8,128)(2,1)S(1)}, bf16[128,1024]{1,0:T(8,128)(2,1)S(1)}, u32[]{:S(2)}, u32[]{:S(2)}) %collective-permute-start.13) | collective-permute-done | bytes 262176 | tf_op jit(solution)/shard_map/ppermute | solution.py:401
  152.6 0.0 collective-permute-start.19
  152.6 2.1 %all-to-all-done.2 = bf16[16,8,1024]{2,1,0:T(8,128)(2,1)S(1)} async-done(((bf16[16,8,1024]{2,1,0:T(8,128)(2,1)}), bf16[16,8,1024]{2,1,0:T(8,128)(2,1)S(1)}, u32[]{:S(2)}, u32[]{:S(2)}) %all-to-all-start.2) | async-done | bytes 262176 | tf_op jit(solution)/shard_map/all_to_all | solution.py:534
  154.6 0.7 fusion
  155.4 0.0 collective-permute-done.20.refs_11_
  155.4 0.0 collective-permute-done.9.far_ref
  155.5 0.6 copy-done.20
  156.1 0.1 copy-done.21
  156.1 0.3 copy-done.12
  156.4 10.9 %attend.1 = bf16[128,4096]{1,0:T(8,128)(2,1)} custom-call(s32[1]{0:T(128)} %bitcast.me_ref, s32[16,128]{1,0:T(8,128)} %bitcast.23, bf16[128,4096]{1,0:T(8,128)(2,1)} %get-tuple-element.15.query_ref, bf16[128,96]{1,0:T(8,128)(2,1)} %get-tuple-element.16.unpack_ref, bf16[96,4096]{1,0:T(8,128)(2,1)} %copy-done.12, bf16[128,1024]{1,0:T(8,128)(2,1)} %copy-done.8, ...), custom_call_target="tpu_custom_call" | custom-call | flops 9663676416 | bytes 4194304 | tf_op jit(solution)/shard_map/attend/pallas_call | solution.py:510
  (41 shorter events, 0.1 us)
Async XLA Ops:
  1.7 16.0 %collective-permute-start = (bf16[64,2048]{1,0:T(8,128)(2,1)S(1)}, bf16[64,2048]{1,0:T(8,128)(2,1)S(1)}, u32[]{:S(2)}, u32[]{:S(2)}) collective-permute-start(bf16[64,2048]{1,0:T(8,128)(2,1)S(1)} %slice_select_fusion), channel_id=1, source_target_pairs={{0,8},{1,9},{2,10},{3,11},{4,12},{5,13},{6,14},{7,15},{8,0},{9,1},... | collective-permute-start | bytes 786440 | tf_op jit(solution)/shard_map/ppermute | solution.py:368
  5.8 1.6 copy-start.2
  7.4 0.7 copy-start.6
  8.1 0.7 copy-start.7
  12.2 1.6 copy-start.1
  17.7 0.7 copy-start.10
  18.4 6.0 %copy-start.11 = (bf16[64,2048]{1,0:T(8,128)(2,1)S(1)}, bf16[64,2048]{1,0:T(8,128)(2,1)}, u32[]{:S(2)}) copy-start(bf16[64,2048]{1,0:T(8,128)(2,1)} %copy-done.10) | copy-start | bytes 786436
  18.4 65.5 %all-to-all-start = ((bf16[16,8,12288]{2,1,0:T(8,128)(2,1)}), bf16[16,8,12288]{2,1,0:T(8,128)(2,1)S(1)}, u32[]{:S(2)}, u32[]{:S(2)}) async-start(bf16[16,8,12288]{2,1,0:T(8,128)(2,1)} %bitcast.13), calls=%async_computation | async-start | bytes 6291456 | tf_op jit(solution)/shard_map/all_to_all | solution.py:534
  24.5 8.7 %collective-permute-start.1 = (bf16[64,2048]{1,0:T(8,128)(2,1)S(1)}, bf16[64,2048]{1,0:T(8,128)(2,1)S(1)}, u32[]{:S(2)}, u32[]{:S(2)}) collective-permute-start(bf16[64,2048]{1,0:T(8,128)(2,1)S(1)} %copy-done.11), channel_id=1, source_target_pairs={{0,16},{16,0},{1,17},{17,1},{2,18},{18,2},{3,19},{19,3},{4,20},{20... | collective-permute-start | bytes 786440 | tf_op jit(solution)/shard_map/ppermute | solution.py:381
  26.0 38.7 %collective-permute-start.2 = (bf16[64,4096]{1,0:T(8,128)(2,1)}, bf16[64,4096]{1,0:T(8,128)(2,1)}, u32[]{:S(2)}, u32[]{:S(2)}) collective-permute-start(bf16[64,4096]{1,0:T(8,128)(2,1)} %bitcast.19), channel_id=1, source_target_pairs={{0,2},{1,3},{2,0},{3,1},{4,6},{5,7},{6,4},{7,5},{8,10},{9,11},{10,... | collective-permute-start | bytes 1572872 | tf_op jit(solution)/shard_map/ppermute | solution.py:388
  34.1 43.4 %collective-permute-start.3 = (bf16[64,4096]{1,0:T(8,128)(2,1)}, bf16[64,4096]{1,0:T(8,128)(2,1)}, u32[]{:S(2)}, u32[]{:S(2)}) collective-permute-start(bf16[64,4096]{1,0:T(8,128)(2,1)} %pad_maximum_fusion.refs_0_.refs_4_), channel_id=1, source_target_pairs={{0,2},{1,3},{2,0},{3,1},{4,6},{5,7},{6,4},{7,5},{8,10},{9,11},{10,... | collective-permute-start | bytes 1572872 | tf_op jit(solution)/shard_map/ppermute | solution.py:388
  35.7 47.7 %collective-permute-start.4 = (bf16[64,4096]{1,0:T(8,128)(2,1)}, bf16[64,4096]{1,0:T(8,128)(2,1)}, u32[]{:S(2)}, u32[]{:S(2)}) collective-permute-start(bf16[64,4096]{1,0:T(8,128)(2,1)} %bitcast.20), channel_id=1, source_target_pairs={{0,1},{1,0},{2,3},{3,2},{4,5},{5,4},{6,7},{7,6},{8,9},{9,8},{10,11... | collective-permute-start | bytes 1572872 | tf_op jit(solution)/shard_map/ppermute | solution.py:388
  35.7 47.7 %collective-permute-start.5 = (bf16[64,4096]{1,0:T(8,128)(2,1)}, bf16[64,4096]{1,0:T(8,128)(2,1)}, u32[]{:S(2)}, u32[]{:S(2)}) collective-permute-start(bf16[64,4096]{1,0:T(8,128)(2,1)} %pad_maximum_fusion.refs_0_.refs_4_), channel_id=1, source_target_pairs={{0,1},{1,0},{2,3},{3,2},{4,5},{5,4},{6,7},{7,6},{8,9},{9,8},{10,11... | collective-permute-start | bytes 1572872 | tf_op jit(solution)/shard_map/ppermute | solution.py:388
  64.7 18.8 %collective-permute-start.6 = (bf16[64,4096]{1,0:T(8,128)(2,1)}, bf16[64,4096]{1,0:T(8,128)(2,1)}, u32[]{:S(2)}, u32[]{:S(2)}) collective-permute-start(bf16[64,4096]{1,0:T(8,128)(2,1)} %collective-permute-done.2.refs_1_.refs_2_), channel_id=1, source_target_pairs={{0,1},{1,0},{2,3},{3,2},{4,5},{5,4},{6,7},{7,6},{8,9},{9,8},{10,11... | collective-permute-start | bytes 1572872 | tf_op jit(solution)/shard_map/ppermute | solution.py:388
  77.5 5.9 %collective-permute-start.7 = (bf16[64,4096]{1,0:T(8,128)(2,1)}, bf16[64,4096]{1,0:T(8,128)(2,1)}, u32[]{:S(2)}, u32[]{:S(2)}) collective-permute-start(bf16[64,4096]{1,0:T(8,128)(2,1)} %collective-permute-done.3.refs_2_.refs_6_), channel_id=1, source_target_pairs={{0,1},{1,0},{2,3},{3,2},{4,5},{5,4},{6,7},{7,6},{8,9},{9,8},{10,11... | collective-permute-start | bytes 1572872 | tf_op jit(solution)/shard_map/ppermute | solution.py:388
  83.4 0.9 copy-start.3
  84.3 2.2 %copy-start = (bf16[1,8192,192]{2,1,0:T(8,128)(2,1)S(1)}, bf16[1,8192,192]{2,1,0:T(8,128)(2,1)}, u32[]{:S(2)}) copy-start(bf16[1,8192,192]{2,1,0:T(8,128)(2,1)} %copy.14.refs_3_.refs_4_) | copy-start | bytes 9437188
  86.5 30.0 %copy-start.4 = (bf16[128,512]{1,0:T(8,128)(2,1)S(1)}, bf16[128,512]{1,0:T(8,128)(2,1)}, u32[]{:S(2)}) copy-start(bf16[128,512]{1,0:T(8,128)(2,1)} %sk_ref.1) | copy-start | bytes 393220
  86.5 30.0 %copy-start.5 = (bf16[128,512]{1,0:T(8,128)(2,1)S(1)}, bf16[128,512]{1,0:T(8,128)(2,1)}, u32[]{:S(2)}) copy-start(bf16[128,512]{1,0:T(8,128)(2,1)} %sv_ref.1) | copy-start | bytes 393220
  117.0 7.9 %copy-start.8 = (bf16[128,1024]{1,0:T(8,128)(2,1)}, bf16[128,1024]{1,0:T(8,128)(2,1)S(1)}, u32[]{:S(2)}) copy-start(bf16[128,1024]{1,0:T(8,128)(2,1)S(1)} %get-tuple-element.14.kv_ref.refs_0_) | copy-start | bytes 786436
  117.0 7.9 %copy-start.9 = (bf16[128,128]{1,0:T(8,128)(2,1)}, bf16[128,128]{1,0:T(8,128)(2,1)S(1)}, u32[]{:S(2)}) copy-start(bf16[128,128]{1,0:T(8,128)(2,1)S(1)} %get-tuple-element.13.own_rows_ref) | copy-start | bytes 98308
  117.0 7.8 %collective-permute-start.8 = (bf16[128,128]{1,0:T(8,128)(2,1)S(1)}, bf16[128,128]{1,0:T(8,128)(2,1)S(1)}, u32[]{:S(2)}, u32[]{:S(2)}) collective-permute-start(bf16[128,128]{1,0:T(8,128)(2,1)S(1)} %get-tuple-element.13.own_rows_ref), channel_id=1, source_target_pairs={{0,4},{1,5},{2,6},{3,7},{4,0},{5,1},{6,2},{7,3},{8,12},{9,13},{10,... | collective-permute-start | bytes 98312 | tf_op jit(solution)/shard_map/ppermute | solution.py:571
  118.0 18.5 %collective-permute-start.12 = (bf16[128,1024]{1,0:T(8,128)(2,1)S(1)}, bf16[128,1024]{1,0:T(8,128)(2,1)S(1)}, u32[]{:S(2)}, u32[]{:S(2)}) collective-permute-start(bf16[128,1024]{1,0:T(8,128)(2,1)S(1)} %get-tuple-element.14.kv_ref.refs_0_), channel_id=1, source_target_pairs={{0,2},{1,3},{2,0},{3,1},{4,6},{5,7},{6,4},{7,5},{8,10},{9,11},{10,... | collective-permute-start | bytes 786440 | tf_op jit(solution)/shard_map/ppermute | solution.py:401
  119.1 17.5 %collective-permute-start.11 = (bf16[128,1024]{1,0:T(8,128)(2,1)S(1)}, bf16[128,1024]{1,0:T(8,128)(2,1)S(1)}, u32[]{:S(2)}, u32[]{:S(2)}) collective-permute-start(bf16[128,1024]{1,0:T(8,128)(2,1)S(1)} %get-tuple-element.14.kv_ref.refs_0_), channel_id=1, source_target_pairs={{0,8},{1,9},{2,10},{3,11},{4,12},{5,13},{6,14},{7,15},{16,24},{17,... | collective-permute-start | bytes 786440 | tf_op jit(solution)/shard_map/ppermute | solution.py:397
  122.5 16.0 %collective-permute-start.10 = (bf16[128,1024]{1,0:T(8,128)(2,1)S(1)}, bf16[128,1024]{1,0:T(8,128)(2,1)S(1)}, u32[]{:S(2)}, u32[]{:S(2)}) collective-permute-start(bf16[128,1024]{1,0:T(8,128)(2,1)S(1)} %get-tuple-element.14.kv_ref.refs_0_), channel_id=1, source_target_pairs={{0,4},{1,5},{2,6},{3,7},{4,8},{5,9},{6,10},{7,11},{8,12},{9,13},{1... | collective-permute-start | bytes 786440 | tf_op jit(solution)/shard_map/ppermute | solution.py:397
  124.9 0.6 copy-start.22
  131.1 24.3 %collective-permute-start.9 = (bf16[96,4096]{1,0:T(8,128)(2,1)}, bf16[96,4096]{1,0:T(8,128)(2,1)S(1)}, u32[]{:S(2)}, u32[]{:S(2)}) collective-permute-start(bf16[96,4096]{1,0:T(8,128)(2,1)} %get-tuple-element.17), channel_id=1, source_target_pairs={{0,4},{1,5},{2,6},{3,7},{4,0},{5,1},{6,2},{7,3},{8,12},{9,13},{10,... | collective-permute-start | bytes 2359304 | tf_op jit(solution)/shard_map/ppermute | solution.py:575
  131.2 23.4 %all-to-all-start.2 = ((bf16[16,8,1024]{2,1,0:T(8,128)(2,1)}), bf16[16,8,1024]{2,1,0:T(8,128)(2,1)S(1)}, u32[]{:S(2)}, u32[]{:S(2)}) async-start(bf16[16,8,1024]{2,1,0:T(8,128)(2,1)} %bitcast.22), calls=%async_computation.2 | async-start | bytes 524288 | tf_op jit(solution)/shard_map/all_to_all | solution.py:534
  136.0 2.6 %collective-permute-start.15 = (bf16[128,1024]{1,0:T(8,128)(2,1)}, bf16[128,1024]{1,0:T(8,128)(2,1)S(1)}, u32[]{:S(2)}, u32[]{:S(2)}) collective-permute-start(bf16[128,1024]{1,0:T(8,128)(2,1)} %copy-done.8), channel_id=1, source_target_pairs={{0,1},{1,0},{2,3},{3,2},{4,5},{5,4},{6,7},{7,6},{8,9},{9,8},{10,11... | collective-permute-start | bytes 786440 | tf_op jit(solution)/shard_map/ppermute | solution.py:401
  136.5 18.9 %copy-start.13 = (bf16[128,1024]{1,0:T(8,128)(2,1)}, bf16[128,1024]{1,0:T(8,128)(2,1)S(1)}, u32[]{:S(2)}) copy-start(bf16[128,1024]{1,0:T(8,128)(2,1)S(1)} %collective-permute-done.12.refs_3_) | copy-start | bytes 786436
  136.5 2.2 %collective-permute-start.18 = (bf16[128,1024]{1,0:T(8,128)(2,1)S(1)}, bf16[128,1024]{1,0:T(8,128)(2,1)S(1)}, u32[]{:S(2)}, u32[]{:S(2)}) collective-permute-start(bf16[128,1024]{1,0:T(8,128)(2,1)S(1)} %collective-permute-done.12.refs_3_), channel_id=1, source_target_pairs={{0,1},{1,0},{2,3},{3,2},{4,5},{5,4},{6,7},{7,6},{8,9},{9,8},{10,11... | collective-permute-start | bytes 786440 | tf_op jit(solution)/shard_map/ppermute | solution.py:401
  136.6 18.8 %copy-start.14 = (bf16[128,1024]{1,0:T(8,128)(2,1)}, bf16[128,1024]{1,0:T(8,128)(2,1)S(1)}, u32[]{:S(2)}) copy-start(bf16[128,1024]{1,0:T(8,128)(2,1)S(1)} %collective-permute-done.11.refs_2_) | copy-start | bytes 786436
  136.6 10.1 %collective-permute-start.14 = (bf16[128,1024]{1,0:T(8,128)(2,1)S(1)}, bf16[128,1024]{1,0:T(8,128)(2,1)S(1)}, u32[]{:S(2)}, u32[]{:S(2)}) collective-permute-start(bf16[128,1024]{1,0:T(8,128)(2,1)S(1)} %collective-permute-done.11.refs_2_), channel_id=1, source_target_pairs={{0,2},{1,3},{2,0},{3,1},{4,6},{5,7},{6,4},{7,5},{8,10},{9,11},{10,... | collective-permute-start | bytes 786440 | tf_op jit(solution)/shard_map/ppermute | solution.py:401
  138.5 16.9 %copy-start.15 = (bf16[128,1024]{1,0:T(8,128)(2,1)}, bf16[128,1024]{1,0:T(8,128)(2,1)S(1)}, u32[]{:S(2)}) copy-start(bf16[128,1024]{1,0:T(8,128)(2,1)S(1)} %collective-permute-done.10.refs_1_) | copy-start | bytes 786436
  138.5 14.1 %collective-permute-start.13 = (bf16[128,1024]{1,0:T(8,128)(2,1)S(1)}, bf16[128,1024]{1,0:T(8,128)(2,1)S(1)}, u32[]{:S(2)}, u32[]{:S(2)}) collective-permute-start(bf16[128,1024]{1,0:T(8,128)(2,1)S(1)} %collective-permute-done.10.refs_1_), channel_id=1, source_target_pairs={{0,2},{1,3},{2,0},{3,1},{4,6},{5,7},{6,4},{7,5},{8,10},{9,11},{10,... | collective-permute-start | bytes 786440 | tf_op jit(solution)/shard_map/ppermute | solution.py:401
  138.7 16.8 %copy-start.16 = (bf16[128,1024]{1,0:T(8,128)(2,1)}, bf16[128,1024]{1,0:T(8,128)(2,1)S(1)}, u32[]{:S(2)}) copy-start(bf16[128,1024]{1,0:T(8,128)(2,1)S(1)} %collective-permute-done.15.refs_6_) | copy-start | bytes 786436
  138.7 16.7 %collective-permute-start.17 = (bf16[128,1024]{1,0:T(8,128)(2,1)S(1)}, bf16[128,1024]{1,0:T(8,128)(2,1)S(1)}, u32[]{:S(2)}, u32[]{:S(2)}) collective-permute-start(bf16[128,1024]{1,0:T(8,128)(2,1)S(1)} %collective-permute-done.11.refs_2_), channel_id=1, source_target_pairs={{0,1},{1,0},{2,3},{3,2},{4,5},{5,4},{6,7},{7,6},{8,9},{9,8},{10,11... | collective-permute-start | bytes 786440 | tf_op jit(solution)/shard_map/ppermute | solution.py:401
  138.7 16.8 %copy-start.17 = (bf16[128,1024]{1,0:T(8,128)(2,1)}, bf16[128,1024]{1,0:T(8,128)(2,1)S(1)}, u32[]{:S(2)}) copy-start(bf16[128,1024]{1,0:T(8,128)(2,1)S(1)} %collective-permute-done.18.refs_9_) | copy-start | bytes 786436
  138.7 16.7 %collective-permute-start.16 = (bf16[128,1024]{1,0:T(8,128)(2,1)S(1)}, bf16[128,1024]{1,0:T(8,128)(2,1)S(1)}, u32[]{:S(2)}, u32[]{:S(2)}) collective-permute-start(bf16[128,1024]{1,0:T(8,128)(2,1)S(1)} %collective-permute-done.10.refs_1_), channel_id=1, source_target_pairs={{0,1},{1,0},{2,3},{3,2},{4,5},{5,4},{6,7},{7,6},{8,9},{9,8},{10,11... | collective-permute-start | bytes 786440 | tf_op jit(solution)/shard_map/ppermute | solution.py:401
  146.7 8.7 %copy-start.18 = (bf16[128,1024]{1,0:T(8,128)(2,1)}, bf16[128,1024]{1,0:T(8,128)(2,1)S(1)}, u32[]{:S(2)}) copy-start(bf16[128,1024]{1,0:T(8,128)(2,1)S(1)} %collective-permute-done.14.refs_5_) | copy-start | bytes 786436
  146.7 8.6 %collective-permute-start.20 = (bf16[128,1024]{1,0:T(8,128)(2,1)S(1)}, bf16[128,1024]{1,0:T(8,128)(2,1)}, u32[]{:S(2)}, u32[]{:S(2)}) collective-permute-start(bf16[128,1024]{1,0:T(8,128)(2,1)S(1)} %collective-permute-done.14.refs_5_), channel_id=1, source_target_pairs={{0,1},{1,0},{2,3},{3,2},{4,5},{5,4},{6,7},{7,6},{8,9},{9,8},{10,11... | collective-permute-start | bytes 786440 | tf_op jit(solution)/shard_map/ppermute | solution.py:401
  152.6 2.9 %copy-start.19 = (bf16[128,1024]{1,0:T(8,128)(2,1)}, bf16[128,1024]{1,0:T(8,128)(2,1)S(1)}, u32[]{:S(2)}) copy-start(bf16[128,1024]{1,0:T(8,128)(2,1)S(1)} %collective-permute-done.13.refs_4_) | copy-start | bytes 786436
  152.6 2.8 %collective-permute-start.19 = (bf16[128,1024]{1,0:T(8,128)(2,1)S(1)}, bf16[128,1024]{1,0:T(8,128)(2,1)}, u32[]{:S(2)}, u32[]{:S(2)}) collective-permute-start(bf16[128,1024]{1,0:T(8,128)(2,1)S(1)} %collective-permute-done.13.refs_4_), channel_id=1, source_target_pairs={{0,1},{1,0},{2,3},{3,2},{4,5},{5,4},{6,7},{7,6},{8,9},{9,8},{10,11... | collective-permute-start | bytes 786440 | tf_op jit(solution)/shard_map/ppermute | solution.py:401
  155.3 0.7 copy-start.20
  155.4 0.8 copy-start.21
  155.4 1.0 copy-start.12

commit v6 on v5

--- a/solution.py
+++ b/solution.py
@@ -326,7 +326,7 @@
             pltpu.VMEM((KEY_VALUE_HEADS, tokens, block), jnp.bfloat16),
             pltpu.SemaphoreType.DMA((KEY_VALUE_HEADS, len(marks) + 1)),
         ],
-        compiler_params=params(60),
+        compiler_params=params(46),
         cost_estimate=cost(16 * tokens * len(marks) * rank * width, 4 * tokens * width),
         name="expand",
     )(me, shrunk, far_shrunk, kv, shared_query, *(ups[k] for k in marks))
@@ -523,10 +523,29 @@
             pltpu.VMEM((KEY_VALUE_HEADS, tokens, block), jnp.bfloat16),
             pltpu.SemaphoreType.DMA((len(chunks) + 3 * KEY_VALUE_HEADS,)),
         ],
-        compiler_params=params(60),
-        cost_estimate=cost(16 * tokens * query_width * length, 8 * tokens * query_width),
+        compiler_params=params(46),
+        cost_estimate=cost(1 * tokens * query_width * length, tokens * query_width),
         name="attend",
     )(me, requests, query, unpack, far, *(rows for _, _, rows in chunks))
+
+
+def split_kernel(rows_ref, _, left_ref, right_ref):
+    width = left_ref.shape[1]
+    left_ref[...] = rows_ref[:, :width]
+    right_ref[...] = rows_ref[:, width:]
+
+
+def split(rows, other):
+    height, width = rows.shape
+    vmem = pl.BlockSpec(memory_space=pltpu.VMEM)
+    return pl.pallas_call(
+        split_kernel,
+        in_specs=[vmem, pl.BlockSpec(memory_space=pl.ANY)],
+        out_specs=[vmem, vmem],
+        out_shape=[jax.ShapeDtypeStruct((height, width // 2), rows.dtype)] * 2,
+        compiler_params=params(),
+        name="split",
+    )(rows, other)
 
 
 def exchange(rows, devices):
@@ -575,8 +594,7 @@
     far = lax.ppermute(far, "seq", swap)
     requests = token_request.reshape(devices, tokens)
     attention = attend(me, requests, query, unpack, far, chunks, reach)
-    width = pages.shape[1] // 2
-    return (attention, pages[:, :width], pages[:, width:])
+    return (attention, *split(pages, attention))
 
 
 def solution(mesh):

time: 168 us -> 167 us (level)
  waiting for transfers between devices: 66.4 us -> 60.1 us
  starting transfers between devices: 31.6 us -> 36.6 us
  local copies, waits for them, and re-layouts: 16 us -> 17.8 us
    ppermute x9, waiting for transfers between devices: 13.4 us -> 3.28 us  [window_chunks(): lax.ppermute(rows, 'seq', swap)]
    ppermute x1, waiting for transfers between devices: 0.01 us -> 5.67 us  [local(): far = lax.ppermute(far, 'seq', swap)]
    all_to_all x2, starting transfers between devices: 10.9 us -> 15 us  [exchange(): lax.all_to_all(rows.reshape(devices, rows.shape[0] // devices, width), 's...]
    unnamed x47 -> x31, local copies, waits for them, and re-layouts: 15.3 us -> 17.8 us
    all_to_all x2, waiting for transfers between devices: 2.55 us -> 0.5 us  [exchange(): lax.all_to_all(rows.reshape(devices, rows.shape[0] // devices, width), 's...]
  transfers between devices with their start and end apart: 23 -> 23, of which waited for: 8 -> 10; matrix products, arithmetic and copies ran while one was open for 5% -> 4% of each run, Pallas kernels for 5% -> 11%
where the time goes in v6:
time: 167 us
  waiting for transfers between devices  60.1 us (36%)
  starting transfers between devices  36.6 us (22%)
  blocking collectives  27.6 us (17%)
  Pallas kernels  21.7 us (13%)
  local copies, waits for them, and re-layouts  17.8 us (11%)
  other arithmetic  2.01 us (1%)
    ppermute x6, waiting for transfers between devices, gathered_factors(): lax.ppermute(a, 'seq', swap)  41.3 us
    all_to_all x1, blocking collectives, exchange(): lax.all_to_all(rows.reshape(devices, rows.shape[0] // devices, width), 's...  27.6 us
    unnamed x31, local copies, waits for them, and re-layouts  17.8 us
    all_to_all x2, starting transfers between devices, exchange(): lax.all_to_all(rows.reshape(devices, rows.shape[0] // devices, width), 's...  15 us
    pallas_call x1, Pallas kernels, attend(): pl.pallas_call(functools.partial(attend_kernel, reach, tuple(((b, m) for...  10.4 us
    ppermute x2, starting transfers between devices, window_chunks(): lax.ppermute(kv, 'seq', [(i, i + hop) for i in range(devices - hop)])  5.77 us
    ppermute x1, waiting for transfers between devices, local(): far = lax.ppermute(far, 'seq', swap)  5.67 us
    ppermute x1, waiting for transfers between devices, gathered_factors(): there = lax.ppermute(here, 'groups', [(0, 1), (1, 0)])  5.23 us
  transfers between devices with their start and end apart: 23, of which 10 were waited for; matrix products, arithmetic and copies ran while one was open for 4% of the time, Pallas kernels for 11%

profile of v6, /device:TPU:0, one launch (start us, length us, event | category | flops | bytes accessed | tf_op | source)
XLA Modules:
  0.0 166.6 jit_solution(11446397188983448672)
XLA Ops:
  0.6 1.1 slice_select_fusion
  1.7 4.1 %collective-permute-start = (bf16[64,2048]{1,0:T(8,128)(2,1)S(1)}, bf16[64,2048]{1,0:T(8,128)(2,1)S(1)}, u32[]{:S(2)}, u32[]{:S(2)}) collective-permute-start(bf16[64,2048]{1,0:T(8,128)(2,1)S(1)} %slice_select_fusion), channel_id=1, source_target_pairs={{0,8},{1,9},{2,10},{3,11},{4,12},{5,13},{6,14},{7,15},{8,0},{9,1},... | collective-permute-start | bytes 786440 | tf_op jit(solution)/shard_map/ppermute | solution.py:368
  5.8 1.6 copy-done.2
  7.4 0.7 copy-done.10
  8.1 0.7 copy-done.11
  8.7 3.5 %dispatch.1 = (bf16[128,12288]{1,0:T(8,128)(2,1)S(1)}, s32[128,128]{1,0:T(8,128)S(1)}) custom-call(s32[1,128]{1,0:T(1,128)S(1)} %bitcast.23, s32[16]{0:T(128)S(1)} %copy-done.11, bf16[128,8192]{1,0:T(8,128)(2,1)S(1)} %copy-done.2, bf16[128,8192]{1,0:T(8,128)(2,1)S(1)} %copy-done.2), custom_call_target="tpu_custom_call" | custom-call | tf_op jit(solution)/shard_map/dispatch/pallas_call | solution.py:105
  12.2 1.6 copy-done.1
  13.8 3.9 %collective-permute-done.refs_1_ = bf16[64,2048]{1,0:T(8,128)(2,1)S(1)} collective-permute-done((bf16[64,2048]{1,0:T(8,128)(2,1)S(1)}, bf16[64,2048]{1,0:T(8,128)(2,1)S(1)}, u32[]{:S(2)}, u32[]{:S(2)}) %collective-permute-start) | collective-permute-done | bytes 262176 | tf_op jit(solution)/shard_map/ppermute | solution.py:368
  17.7 0.7 copy-done.13
  18.4 6.0 %all-to-all-start = ((bf16[16,8,12288]{2,1,0:T(8,128)(2,1)}), bf16[16,8,12288]{2,1,0:T(8,128)(2,1)S(1)}, u32[]{:S(2)}, u32[]{:S(2)}) async-start(bf16[16,8,12288]{2,1,0:T(8,128)(2,1)} %bitcast.13), calls=%async_computation | async-start | bytes 6291456 | tf_op jit(solution)/shard_map/all_to_all | solution.py:553
  24.5 1.6 collective-permute-start.1
  26.0 1.9 %collective-permute-start.2 = (bf16[64,4096]{1,0:T(8,128)(2,1)}, bf16[64,4096]{1,0:T(8,128)(2,1)}, u32[]{:S(2)}, u32[]{:S(2)}) collective-permute-start(bf16[64,4096]{1,0:T(8,128)(2,1)} %bitcast.18), channel_id=1, source_target_pairs={{0,2},{1,3},{2,0},{3,1},{4,6},{5,7},{6,4},{7,5},{8,10},{9,11},{10,... | collective-permute-start | bytes 1572872 | tf_op jit(solution)/shard_map/ppermute | solution.py:388
  27.9 5.2 %collective-permute-done.1 = bf16[64,2048]{1,0:T(8,128)(2,1)S(1)} collective-permute-done((bf16[64,2048]{1,0:T(8,128)(2,1)S(1)}, bf16[64,2048]{1,0:T(8,128)(2,1)S(1)}, u32[]{:S(2)}, u32[]{:S(2)}) %collective-permute-start.1) | collective-permute-done | bytes 262176 | tf_op jit(solution)/shard_map/ppermute | solution.py:381
  33.2 0.1 broadcast_select_fusion.1
  33.2 0.9 pad_maximum_fusion.refs_0_.refs_4_
  34.1 1.6 collective-permute-start.3
  35.8 0.0 collective-permute-start.4
  35.8 0.5 collective-permute-start.5
  36.3 28.4 %collective-permute-done.2.refs_1_.refs_2_ = bf16[64,4096]{1,0:T(8,128)(2,1)} collective-permute-done((bf16[64,4096]{1,0:T(8,128)(2,1)}, bf16[64,4096]{1,0:T(8,128)(2,1)}, u32[]{:S(2)}, u32[]{:S(2)}) %collective-permute-start.2) | collective-permute-done | bytes 524320 | tf_op jit(solution)/shard_map/ppermute | solution.py:388
  64.7 0.0 collective-permute-start.6
  64.7 12.9 %collective-permute-done.3.refs_2_.refs_6_ = bf16[64,4096]{1,0:T(8,128)(2,1)} collective-permute-done((bf16[64,4096]{1,0:T(8,128)(2,1)}, bf16[64,4096]{1,0:T(8,128)(2,1)}, u32[]{:S(2)}, u32[]{:S(2)}) %collective-permute-start.3) | collective-permute-done | bytes 524320 | tf_op jit(solution)/shard_map/ppermute | solution.py:388
  77.5 0.0 collective-permute-start.7
  77.5 5.9 %copy.14.refs_3_.refs_4_ = bf16[1,8192,192]{2,1,0:T(8,128)(2,1)} copy(bf16[1,8192,192]{1,2,0:T(8,128)(2,1)} %param.16) | data formatting | bytes 6291456 | tf_op args[6]
  83.4 0.0 collective-permute-done.4.refs_3_.refs_1_
  83.4 0.0 collective-permute-done.6.refs_5_.refs_3_
  83.4 0.5 all-to-all-done
  83.9 0.4 copy-done.6
  84.3 2.2 %copy-done = bf16[1,8192,192]{2,1,0:T(8,128)(2,1)S(1)} copy-done((bf16[1,8192,192]{2,1,0:T(8,128)(2,1)S(1)}, bf16[1,8192,192]{2,1,0:T(8,128)(2,1)}, u32[]{:S(2)}) %copy-start) | copy-done | bytes 3145752
  86.5 2.5 %project.1 = bf16[128,1664]{1,0:T(8,128)(2,1)S(1)} custom-call(bf16[128,12288]{1,0:T(8,128)(2,1)S(1)} %bitcast.10, bf16[128,12288]{1,0:T(8,128)(2,1)S(1)} %bitcast.11, bf16[128,12288]{1,0:T(8,128)(2,1)S(1)} %bitcast.12, bf16[1,8192,192]{2,1,0:T(8,128)(2,1)S(1)} %copy-done, bf16[1,8192,192]{2,1,0:T(8,128)(2,1)S(1)} %copy-done, ...), custom_call_target="tpu_custom_call" | custom-call | tf_op jit(solution)/shard_map/project/pallas_call | solution.py:193
  89.0 27.6 %all_to_all.15 = bf16[16,8,1664]{2,1,0:T(8,128)(2,1)S(1)} all-to-all(bf16[16,8,1664]{2,1,0:T(8,128)(2,1)S(1)} %bitcast.15), channel_id=1, replica_groups=mesh['groups'=2,'seq'=16] {'seq'}, dimensions={0} | all-to-all | bytes 851968 | tf_op jit(solution)/shard_map/all_to_all | solution.py:553
  116.6 0.5 correct.1
  117.0 0.9 collective-permute-start.8
  117.9 1.1 collective-permute-start.12
  119.1 3.4 %collective-permute-start.11 = (bf16[128,1024]{1,0:T(8,128)(2,1)S(1)}, bf16[128,1024]{1,0:T(8,128)(2,1)S(1)}, u32[]{:S(2)}, u32[]{:S(2)}) collective-permute-start(bf16[128,1024]{1,0:T(8,128)(2,1)S(1)} %get-tuple-element.16.kv_ref.refs_0_), channel_id=1, source_target_pairs={{0,8},{1,9},{2,10},{3,11},{4,12},{5,13},{6,14},{7,15},{16,24},{17,... | collective-permute-start | bytes 786440 | tf_op jit(solution)/shard_map/ppermute | solution.py:397
  122.4 2.4 %collective-permute-start.10 = (bf16[128,1024]{1,0:T(8,128)(2,1)S(1)}, bf16[128,1024]{1,0:T(8,128)(2,1)S(1)}, u32[]{:S(2)}, u32[]{:S(2)}) collective-permute-start(bf16[128,1024]{1,0:T(8,128)(2,1)S(1)} %get-tuple-element.16.kv_ref.refs_0_), channel_id=1, source_target_pairs={{0,4},{1,5},{2,6},{3,7},{4,8},{5,9},{6,10},{7,11},{8,12},{9,13},{1... | collective-permute-start | bytes 786440 | tf_op jit(solution)/shard_map/ppermute | solution.py:397
  124.8 0.0 collective-permute-done.8.far_rows_ref
  124.9 0.0 copy-start.4
  124.9 1.0 copy-done.4
  125.9 1.2 copy-done.12
  127.1 4.2 %expand.1 = (bf16[128,4096]{1,0:T(8,128)(2,1)S(1)}, bf16[128,96]{1,0:T(8,128)(2,1)S(1)}, bf16[128,1024]{1,0:T(8,128)(2,1)S(1)}, bf16[96,4096]{1,0:T(8,128)(2,1)}) custom-call(s32[1]{0:T(128)} %bitcast.me_ref, bf16[128,128]{1,0:T(8,128)(2,1)S(1)} %get-tuple-element.15.own_rows_ref, bf16[128,128]{1,0:T(8,128)(2,1)S(1)} %collective-permute-done.8.far_rows_ref, ...), custom_call_target="tpu_custom_call" | custom-call | flops 4294967296 | bytes 2097152 | tf_op jit(solution)/shard_map/expand/pallas_call | solution.py:315
  131.3 0.7 copy-done.5
  132.0 0.0 collective-permute-start.9
  132.0 0.5 collective-permute-start.18
  132.5 0.0 collective-permute-done.11.refs_2_
  132.5 2.0 %collective-permute-start.14 = (bf16[128,1024]{1,0:T(8,128)(2,1)S(1)}, bf16[128,1024]{1,0:T(8,128)(2,1)}, u32[]{:S(2)}, u32[]{:S(2)}) collective-permute-start(bf16[128,1024]{1,0:T(8,128)(2,1)S(1)} %collective-permute-done.11.refs_2_), channel_id=1, source_target_pairs={{0,2},{1,3},{2,0},{3,1},{4,6},{5,7},{6,4},{7,5},{8,10},{9,11},{10,... | collective-permute-start | bytes 786440 | tf_op jit(solution)/shard_map/ppermute | solution.py:401
  134.5 0.2 collective-permute-done.10.refs_1_
  134.8 0.5 collective-permute-start.13
  135.3 9.0 %all-to-all-start.2 = ((bf16[16,8,1024]{2,1,0:T(8,128)(2,1)}), bf16[16,8,1024]{2,1,0:T(8,128)(2,1)S(1)}, u32[]{:S(2)}, u32[]{:S(2)}) async-start(bf16[16,8,1024]{2,1,0:T(8,128)(2,1)} %bitcast.21), calls=%async_computation.2 | async-start | bytes 524288 | tf_op jit(solution)/shard_map/all_to_all | solution.py:553
  144.3 0.0 collective-permute-done.15.refs_6_
  144.3 0.5 collective-permute-start.17
  144.8 0.0 collective-permute-done.18.refs_9_
  144.8 0.1 collective-permute-start.16
  144.9 0.4 collective-permute-start.20
  145.3 1.5 collective-permute-done.13.refs_4_
  146.8 0.0 collective-permute-done.17.refs_8_
  146.8 0.0 collective-permute-done.16.refs_7_
  146.8 0.1 collective-permute-done.20.refs_11_
  146.9 1.7 %collective-permute-done.19.refs_10_ = bf16[128,1024]{1,0:T(8,128)(2,1)S(1)} collective-permute-done((bf16[128,1024]{1,0:T(8,128)(2,1)}, bf16[128,1024]{1,0:T(8,128)(2,1)S(1)}, u32[]{:S(2)}, u32[]{:S(2)}) %collective-permute-start.19) | collective-permute-done | bytes 262176 | tf_op jit(solution)/shard_map/ppermute | solution.py:401
  148.6 5.7 %collective-permute-done.9.far_ref = bf16[96,4096]{1,0:T(8,128)(2,1)S(1)} collective-permute-done((bf16[96,4096]{1,0:T(8,128)(2,1)}, bf16[96,4096]{1,0:T(8,128)(2,1)S(1)}, u32[]{:S(2)}, u32[]{:S(2)}) %collective-permute-start.9) | collective-permute-done | bytes 786464 | tf_op jit(solution)/shard_map/ppermute | solution.py:594
  154.2 10.4 %attend.1._ = bf16[128,4096]{1,0:T(8,128)(2,1)} custom-call(s32[1]{0:T(128)} %bitcast.me_ref, s32[16,128]{1,0:T(8,128)S(1)} %bitcast.22, bf16[128,4096]{1,0:T(8,128)(2,1)S(1)} %get-tuple-element.17.query_ref, bf16[128,96]{1,0:T(8,128)(2,1)S(1)} %get-tuple-element.18.unpack_ref, bf16[96,4096]{1,0:T(8,128)(2,1)S(1)} %collective-permute-done.9.far_ref, ...), custom_call_target="tpu_custom_call" | custom-call | flops 603979776 | bytes 524288 | tf_op jit(solution)/shard_map/attend/pallas_call | solution.py:510
  164.6 0.0 all-to-all-done.2
  164.7 0.0 copy-start.3
  164.7 1.2 copy-done.3
  165.9 0.7 split.1
  (25 shorter events, 0.0 us)
Async XLA Ops:
  1.7 16.0 %collective-permute-start = (bf16[64,2048]{1,0:T(8,128)(2,1)S(1)}, bf16[64,2048]{1,0:T(8,128)(2,1)S(1)}, u32[]{:S(2)}, u32[]{:S(2)}) collective-permute-start(bf16[64,2048]{1,0:T(8,128)(2,1)S(1)} %slice_select_fusion), channel_id=1, source_target_pairs={{0,8},{1,9},{2,10},{3,11},{4,12},{5,13},{6,14},{7,15},{8,0},{9,1},... | collective-permute-start | bytes 786440 | tf_op jit(solution)/shard_map/ppermute | solution.py:368
  5.8 1.6 copy-start.2
  7.4 0.7 copy-start.10
  8.1 0.7 copy-start.11
  12.2 1.6 copy-start.1
  17.7 0.7 copy-start.13
  18.4 6.0 %copy-start.14 = (bf16[64,2048]{1,0:T(8,128)(2,1)S(1)}, bf16[64,2048]{1,0:T(8,128)(2,1)}, u32[]{:S(2)}) copy-start(bf16[64,2048]{1,0:T(8,128)(2,1)} %copy-done.13) | copy-start | bytes 786436
  18.4 65.5 %all-to-all-start = ((bf16[16,8,12288]{2,1,0:T(8,128)(2,1)}), bf16[16,8,12288]{2,1,0:T(8,128)(2,1)S(1)}, u32[]{:S(2)}, u32[]{:S(2)}) async-start(bf16[16,8,12288]{2,1,0:T(8,128)(2,1)} %bitcast.13), calls=%async_computation | async-start | bytes 6291456 | tf_op jit(solution)/shard_map/all_to_all | solution.py:553
  24.5 8.7 %collective-permute-start.1 = (bf16[64,2048]{1,0:T(8,128)(2,1)S(1)}, bf16[64,2048]{1,0:T(8,128)(2,1)S(1)}, u32[]{:S(2)}, u32[]{:S(2)}) collective-permute-start(bf16[64,2048]{1,0:T(8,128)(2,1)S(1)} %copy-done.14), channel_id=1, source_target_pairs={{0,16},{16,0},{1,17},{17,1},{2,18},{18,2},{3,19},{19,3},{4,20},{20... | collective-permute-start | bytes 786440 | tf_op jit(solution)/shard_map/ppermute | solution.py:381
  26.0 38.7 %collective-permute-start.2 = (bf16[64,4096]{1,0:T(8,128)(2,1)}, bf16[64,4096]{1,0:T(8,128)(2,1)}, u32[]{:S(2)}, u32[]{:S(2)}) collective-permute-start(bf16[64,4096]{1,0:T(8,128)(2,1)} %bitcast.18), channel_id=1, source_target_pairs={{0,2},{1,3},{2,0},{3,1},{4,6},{5,7},{6,4},{7,5},{8,10},{9,11},{10,... | collective-permute-start | bytes 1572872 | tf_op jit(solution)/shard_map/ppermute | solution.py:388
  34.1 43.4 %collective-permute-start.3 = (bf16[64,4096]{1,0:T(8,128)(2,1)}, bf16[64,4096]{1,0:T(8,128)(2,1)}, u32[]{:S(2)}, u32[]{:S(2)}) collective-permute-start(bf16[64,4096]{1,0:T(8,128)(2,1)} %pad_maximum_fusion.refs_0_.refs_4_), channel_id=1, source_target_pairs={{0,2},{1,3},{2,0},{3,1},{4,6},{5,7},{6,4},{7,5},{8,10},{9,11},{10,... | collective-permute-start | bytes 1572872 | tf_op jit(solution)/shard_map/ppermute | solution.py:388
  35.8 47.7 %collective-permute-start.4 = (bf16[64,4096]{1,0:T(8,128)(2,1)}, bf16[64,4096]{1,0:T(8,128)(2,1)}, u32[]{:S(2)}, u32[]{:S(2)}) collective-permute-start(bf16[64,4096]{1,0:T(8,128)(2,1)} %bitcast.19), channel_id=1, source_target_pairs={{0,1},{1,0},{2,3},{3,2},{4,5},{5,4},{6,7},{7,6},{8,9},{9,8},{10,11... | collective-permute-start | bytes 1572872 | tf_op jit(solution)/shard_map/ppermute | solution.py:388
  35.8 47.7 %collective-permute-start.5 = (bf16[64,4096]{1,0:T(8,128)(2,1)}, bf16[64,4096]{1,0:T(8,128)(2,1)}, u32[]{:S(2)}, u32[]{:S(2)}) collective-permute-start(bf16[64,4096]{1,0:T(8,128)(2,1)} %pad_maximum_fusion.refs_0_.refs_4_), channel_id=1, source_target_pairs={{0,1},{1,0},{2,3},{3,2},{4,5},{5,4},{6,7},{7,6},{8,9},{9,8},{10,11... | collective-permute-start | bytes 1572872 | tf_op jit(solution)/shard_map/ppermute | solution.py:388
  64.7 18.7 %collective-permute-start.6 = (bf16[64,4096]{1,0:T(8,128)(2,1)}, bf16[64,4096]{1,0:T(8,128)(2,1)}, u32[]{:S(2)}, u32[]{:S(2)}) collective-permute-start(bf16[64,4096]{1,0:T(8,128)(2,1)} %collective-permute-done.2.refs_1_.refs_2_), channel_id=1, source_target_pairs={{0,1},{1,0},{2,3},{3,2},{4,5},{5,4},{6,7},{7,6},{8,9},{9,8},{10,11... | collective-permute-start | bytes 1572872 | tf_op jit(solution)/shard_map/ppermute | solution.py:388
  77.5 5.9 %collective-permute-start.7 = (bf16[64,4096]{1,0:T(8,128)(2,1)}, bf16[64,4096]{1,0:T(8,128)(2,1)}, u32[]{:S(2)}, u32[]{:S(2)}) collective-permute-start(bf16[64,4096]{1,0:T(8,128)(2,1)} %collective-permute-done.3.refs_2_.refs_6_), channel_id=1, source_target_pairs={{0,1},{1,0},{2,3},{3,2},{4,5},{5,4},{6,7},{7,6},{8,9},{9,8},{10,11... | collective-permute-start | bytes 1572872 | tf_op jit(solution)/shard_map/ppermute | solution.py:388
  83.4 0.9 copy-start.6
  84.3 2.2 %copy-start = (bf16[1,8192,192]{2,1,0:T(8,128)(2,1)S(1)}, bf16[1,8192,192]{2,1,0:T(8,128)(2,1)}, u32[]{:S(2)}) copy-start(bf16[1,8192,192]{2,1,0:T(8,128)(2,1)} %copy.14.refs_3_.refs_4_) | copy-start | bytes 9437188
  86.5 30.1 %copy-start.7 = (bf16[128,512]{1,0:T(8,128)(2,1)S(1)}, bf16[128,512]{1,0:T(8,128)(2,1)}, u32[]{:S(2)}) copy-start(bf16[128,512]{1,0:T(8,128)(2,1)} %sk_ref.1) | copy-start | bytes 393220
  86.5 30.1 %copy-start.8 = (bf16[128,512]{1,0:T(8,128)(2,1)S(1)}, bf16[128,512]{1,0:T(8,128)(2,1)}, u32[]{:S(2)}) copy-start(bf16[128,512]{1,0:T(8,128)(2,1)} %sv_ref.1) | copy-start | bytes 393220
  117.0 7.8 %collective-permute-start.8 = (bf16[128,128]{1,0:T(8,128)(2,1)S(1)}, bf16[128,128]{1,0:T(8,128)(2,1)S(1)}, u32[]{:S(2)}, u32[]{:S(2)}) collective-permute-start(bf16[128,128]{1,0:T(8,128)(2,1)S(1)} %get-tuple-element.15.own_rows_ref), channel_id=1, source_target_pairs={{0,4},{1,5},{2,6},{3,7},{4,0},{5,1},{6,2},{7,3},{8,12},{9,13},{10,... | collective-permute-start | bytes 98312 | tf_op jit(solution)/shard_map/ppermute | solution.py:590
  117.9 14.1 %collective-permute-start.12 = (bf16[128,1024]{1,0:T(8,128)(2,1)S(1)}, bf16[128,1024]{1,0:T(8,128)(2,1)S(1)}, u32[]{:S(2)}, u32[]{:S(2)}) collective-permute-start(bf16[128,1024]{1,0:T(8,128)(2,1)S(1)} %get-tuple-element.16.kv_ref.refs_0_), channel_id=1, source_target_pairs={{0,2},{1,3},{2,0},{3,1},{4,6},{5,7},{6,4},{7,5},{8,10},{9,11},{10,... | collective-permute-start | bytes 786440 | tf_op jit(solution)/shard_map/ppermute | solution.py:401
  119.1 13.5 %collective-permute-start.11 = (bf16[128,1024]{1,0:T(8,128)(2,1)S(1)}, bf16[128,1024]{1,0:T(8,128)(2,1)S(1)}, u32[]{:S(2)}, u32[]{:S(2)}) collective-permute-start(bf16[128,1024]{1,0:T(8,128)(2,1)S(1)} %get-tuple-element.16.kv_ref.refs_0_), channel_id=1, source_target_pairs={{0,8},{1,9},{2,10},{3,11},{4,12},{5,13},{6,14},{7,15},{16,24},{17,... | collective-permute-start | bytes 786440 | tf_op jit(solution)/shard_map/ppermute | solution.py:397
  122.4 12.3 %collective-permute-start.10 = (bf16[128,1024]{1,0:T(8,128)(2,1)S(1)}, bf16[128,1024]{1,0:T(8,128)(2,1)S(1)}, u32[]{:S(2)}, u32[]{:S(2)}) collective-permute-start(bf16[128,1024]{1,0:T(8,128)(2,1)S(1)} %get-tuple-element.16.kv_ref.refs_0_), channel_id=1, source_target_pairs={{0,4},{1,5},{2,6},{3,7},{4,8},{5,9},{6,10},{7,11},{8,12},{9,13},{1... | collective-permute-start | bytes 786440 | tf_op jit(solution)/shard_map/ppermute | solution.py:397
  124.9 1.0 copy-start.4
  125.9 1.2 copy-start.12
  127.1 27.1 %copy-start.9 = (s32[2048]{0:T(1024)S(1)}, s32[2048]{0:T(1024)}, u32[]{:S(2)}) copy-start(s32[2048]{0:T(1024)} %param.19) | copy-start | bytes 24580
  131.3 0.7 copy-start.5
  132.0 22.2 %collective-permute-start.9 = (bf16[96,4096]{1,0:T(8,128)(2,1)}, bf16[96,4096]{1,0:T(8,128)(2,1)S(1)}, u32[]{:S(2)}, u32[]{:S(2)}) collective-permute-start(bf16[96,4096]{1,0:T(8,128)(2,1)} %get-tuple-element.19), channel_id=1, source_target_pairs={{0,4},{1,5},{2,6},{3,7},{4,0},{5,1},{6,2},{7,3},{8,12},{9,13},{10,... | collective-permute-start | bytes 2359304 | tf_op jit(solution)/shard_map/ppermute | solution.py:594
  132.0 12.3 %collective-permute-start.15 = (bf16[128,1024]{1,0:T(8,128)(2,1)S(1)}, bf16[128,1024]{1,0:T(8,128)(2,1)S(1)}, u32[]{:S(2)}, u32[]{:S(2)}) collective-permute-start(bf16[128,1024]{1,0:T(8,128)(2,1)S(1)} %get-tuple-element.16.kv_ref.refs_0_), channel_id=1, source_target_pairs={{0,1},{1,0},{2,3},{3,2},{4,5},{5,4},{6,7},{7,6},{8,9},{9,8},{10,11... | collective-permute-start | bytes 786440 | tf_op jit(solution)/shard_map/ppermute | solution.py:401
  132.0 12.8 %collective-permute-start.18 = (bf16[128,1024]{1,0:T(8,128)(2,1)S(1)}, bf16[128,1024]{1,0:T(8,128)(2,1)}, u32[]{:S(2)}, u32[]{:S(2)}) collective-permute-start(bf16[128,1024]{1,0:T(8,128)(2,1)S(1)} %collective-permute-done.12.refs_3_), channel_id=1, source_target_pairs={{0,1},{1,0},{2,3},{3,2},{4,5},{5,4},{6,7},{7,6},{8,9},{9,8},{10,11... | collective-permute-start | bytes 786440 | tf_op jit(solution)/shard_map/ppermute | solution.py:401
  132.5 12.3 %collective-permute-start.14 = (bf16[128,1024]{1,0:T(8,128)(2,1)S(1)}, bf16[128,1024]{1,0:T(8,128)(2,1)}, u32[]{:S(2)}, u32[]{:S(2)}) collective-permute-start(bf16[128,1024]{1,0:T(8,128)(2,1)S(1)} %collective-permute-done.11.refs_2_), channel_id=1, source_target_pairs={{0,2},{1,3},{2,0},{3,1},{4,6},{5,7},{6,4},{7,5},{8,10},{9,11},{10,... | collective-permute-start | bytes 786440 | tf_op jit(solution)/shard_map/ppermute | solution.py:401
  134.8 12.1 %collective-permute-start.13 = (bf16[128,1024]{1,0:T(8,128)(2,1)S(1)}, bf16[128,1024]{1,0:T(8,128)(2,1)}, u32[]{:S(2)}, u32[]{:S(2)}) collective-permute-start(bf16[128,1024]{1,0:T(8,128)(2,1)S(1)} %collective-permute-done.10.refs_1_), channel_id=1, source_target_pairs={{0,2},{1,3},{2,0},{3,1},{4,6},{5,7},{6,4},{7,5},{8,10},{9,11},{10,... | collective-permute-start | bytes 786440 | tf_op jit(solution)/shard_map/ppermute | solution.py:401
  135.3 29.4 %all-to-all-start.2 = ((bf16[16,8,1024]{2,1,0:T(8,128)(2,1)}), bf16[16,8,1024]{2,1,0:T(8,128)(2,1)S(1)}, u32[]{:S(2)}, u32[]{:S(2)}) async-start(bf16[16,8,1024]{2,1,0:T(8,128)(2,1)} %bitcast.21), calls=%async_computation.2 | async-start | bytes 524288 | tf_op jit(solution)/shard_map/all_to_all | solution.py:553
  144.3 2.5 %collective-permute-start.17 = (bf16[128,1024]{1,0:T(8,128)(2,1)S(1)}, bf16[128,1024]{1,0:T(8,128)(2,1)S(1)}, u32[]{:S(2)}, u32[]{:S(2)}) collective-permute-start(bf16[128,1024]{1,0:T(8,128)(2,1)S(1)} %collective-permute-done.11.refs_2_), channel_id=1, source_target_pairs={{0,1},{1,0},{2,3},{3,2},{4,5},{5,4},{6,7},{7,6},{8,9},{9,8},{10,11... | collective-permute-start | bytes 786440 | tf_op jit(solution)/shard_map/ppermute | solution.py:401
  144.8 2.1 %collective-permute-start.16 = (bf16[128,1024]{1,0:T(8,128)(2,1)S(1)}, bf16[128,1024]{1,0:T(8,128)(2,1)S(1)}, u32[]{:S(2)}, u32[]{:S(2)}) collective-permute-start(bf16[128,1024]{1,0:T(8,128)(2,1)S(1)} %collective-permute-done.10.refs_1_), channel_id=1, source_target_pairs={{0,1},{1,0},{2,3},{3,2},{4,5},{5,4},{6,7},{7,6},{8,9},{9,8},{10,11... | collective-permute-start | bytes 786440 | tf_op jit(solution)/shard_map/ppermute | solution.py:401
  144.9 2.0 %collective-permute-start.20 = (bf16[128,1024]{1,0:T(8,128)(2,1)}, bf16[128,1024]{1,0:T(8,128)(2,1)S(1)}, u32[]{:S(2)}, u32[]{:S(2)}) collective-permute-start(bf16[128,1024]{1,0:T(8,128)(2,1)} %collective-permute-done.14.refs_5_), channel_id=1, source_target_pairs={{0,1},{1,0},{2,3},{3,2},{4,5},{5,4},{6,7},{7,6},{8,9},{9,8},{10,11... | collective-permute-start | bytes 786440 | tf_op jit(solution)/shard_map/ppermute | solution.py:401
  146.8 1.7 %collective-permute-start.19 = (bf16[128,1024]{1,0:T(8,128)(2,1)}, bf16[128,1024]{1,0:T(8,128)(2,1)S(1)}, u32[]{:S(2)}, u32[]{:S(2)}) collective-permute-start(bf16[128,1024]{1,0:T(8,128)(2,1)} %collective-permute-done.13.refs_4_), channel_id=1, source_target_pairs={{0,1},{1,0},{2,3},{3,2},{4,5},{5,4},{6,7},{7,6},{8,9},{9,8},{10,11... | collective-permute-start | bytes 786440 | tf_op jit(solution)/shard_map/ppermute | solution.py:401
  164.7 1.2 copy-start.3

commit v7 on v6

--- a/solution.py
+++ b/solution.py
@@ -125,81 +125,51 @@
     )(token_adapter.reshape(1, tokens), table, normed, normed)
 
 
-def project_kernel(full, fold, steps, *refs):
-    refs = list(refs)
-    low_refs = [(refs.pop(0), refs.pop(0)) for _ in range(full)]
-    fold_ref = refs.pop(0) if fold else None
-    (down_low, down_high, up_kv), (out_ref, acc) = refs[:3], refs[-2:]
-    step = pl.program_id(0)
+def project_kernel(full, fold, x_ref, down_ref, up_kv, *refs):
+    out_ref = refs[-1]
     rank = up_kv.shape[2]
-
-    @pl.when(step == 0)
-    def _():
-        acc[...] = jnp.zeros_like(acc)
-
-    low, high = down_low[0], down_high[0]
-    for b, (x_low, x_high) in enumerate(low_refs):
-        acc[b] += f32_dot(x_low[...], low) + f32_dot(x_high[...], high)
+    width = down_ref.shape[1]
+    blocks = [f32_dot(x_ref[:, b * width : (b + 1) * width], down_ref[0]) for b in range(full)]
     if fold:
-        acc[full] += f32_dot(fold_ref[...], low)
-        acc[full + 1] += f32_dot(fold_ref[...], high)
-
-    @pl.when(step == steps - 1)
-    def _():
-        kv_width = up_kv.shape[3]
-        queries = []
-        for b in range(full):
-            shrunk = acc[b].astype(jnp.bfloat16)
-            at = b * 2 * kv_width
-            for i in range(2):
-                piece = shrunk[:, (i + 1) * rank : (i + 2) * rank]
-                out_ref[:, at + i * kv_width : at + (i + 1) * kv_width] = f32_dot(piece, up_kv[0, i]).astype(jnp.bfloat16)
-            queries.append(shrunk[:, :rank])
-        if fold:
-            rows = acc.shape[1]
-            upper = (row_iota((rows, 1)) % SUBLANES) >= 4
-            mixed = jnp.where(upper, acc[full + 1], acc[full]).reshape(rows // SUBLANES, SUBLANES, 3 * rank)
-            both = mixed + jnp.concatenate([mixed[:, 4:], mixed[:, :4]], axis=1)
-            shrunk = both.reshape(rows, 3 * rank).astype(jnp.bfloat16)
-            delta = [f32_dot(shrunk[:, (i + 1) * rank : (i + 2) * rank], up_kv[0, i]) for i in range(2)]
-            at = full * 2 * kv_width
-            out_ref[:, at : at + kv_width] = jnp.where(upper, delta[1], delta[0]).astype(jnp.bfloat16)
-            queries.append(shrunk[:, :rank])
-        if len(queries) % 2:
-            queries.append(jnp.zeros_like(queries[0]))
-        out_ref[:, (2 * full + fold) * kv_width :] = jnp.concatenate(queries, axis=1)
+        rows = x_ref[:, full * width :]
+        low, high = f32_dot(rows, down_ref[0, : width // 2]), f32_dot(rows, down_ref[0, width // 2 :])
+    kv_width = up_kv.shape[3]
+    queries = []
+    for b in range(full):
+        shrunk = blocks[b].astype(jnp.bfloat16)
+        at = b * 2 * kv_width
+        for i in range(2):
+            piece = shrunk[:, (i + 1) * rank : (i + 2) * rank]
+            out_ref[:, at + i * kv_width : at + (i + 1) * kv_width] = f32_dot(piece, up_kv[0, i]).astype(jnp.bfloat16)
+        queries.append(shrunk[:, :rank])
+    if fold:
+        rows = x_ref.shape[0]
+        upper = (row_iota((rows, 1)) % SUBLANES) >= 4
+        mixed = jnp.where(upper, high, low).reshape(rows // SUBLANES, SUBLANES, 3 * rank)
+        both = mixed + jnp.concatenate([mixed[:, 4:], mixed[:, :4]], axis=1)
+        shrunk = both.reshape(rows, 3 * rank).astype(jnp.bfloat16)
+        delta = [f32_dot(shrunk[:, (i + 1) * rank : (i + 2) * rank], up_kv[0, i]) for i in range(2)]
+        at = full * 2 * kv_width
+        out_ref[:, at : at + kv_width] = jnp.where(upper, delta[1], delta[0]).astype(jnp.bfloat16)
+        queries.append(shrunk[:, :rank])
+    if len(queries) % 2:
+        queries.append(jnp.zeros_like(queries[0]))
+    out_ref[:, (2 * full + fold) * kv_width :] = jnp.concatenate(queries, axis=1)
 
 
 def project(x, down, up_kv, full, fold, *others):
     rows = x.shape[0]
-    _, width, ranks = down.shape
-    column = width // 8
-    steps = width // 2 // column
     _, _, rank, kv_width = up_kv.shape
-    in_specs = []
-    for b in range(full):
-        in_specs.append(pl.BlockSpec((rows, column), lambda i, b=b: (0, 2 * b * steps + i)))
-        in_specs.append(pl.BlockSpec((rows, column), lambda i, b=b: (0, (2 * b + 1) * steps + i)))
-    if fold:
-        in_specs.append(pl.BlockSpec((rows, column), lambda i: (0, 2 * full * steps + i)))
-    blocks = len(in_specs)
-    in_specs += [
-        pl.BlockSpec((1, column, ranks), lambda i: (0, i, 0)),
-        pl.BlockSpec((1, column, ranks), lambda i: (0, steps + i, 0)),
-        pl.BlockSpec(up_kv.shape, lambda i: (0, 0, 0, 0)),
-    ]
-    in_specs += [pl.BlockSpec(memory_space=pltpu.HBM)] * len(others)
     shape = (rows, (2 * full + fold) * kv_width + (full + fold + 1) // 2 * 2 * rank)
-    return pl.pallas_call(
-        functools.partial(project_kernel, full, fold, steps),
-        grid=(steps,),
-        in_specs=in_specs,
-        out_specs=pl.BlockSpec(shape, lambda i: (0, 0)),
+    vmem = pl.BlockSpec(memory_space=pltpu.VMEM)
+    return pl.pallas_call(
+        functools.partial(project_kernel, full, fold),
+        in_specs=[vmem] * 3 + [pl.BlockSpec(memory_space=pl.ANY)] * len(others),
+        out_specs=vmem,
         out_shape=jax.ShapeDtypeStruct(shape, jnp.bfloat16),
-        scratch_shapes=[pltpu.VMEM((full + 2 * fold, rows, ranks), jnp.float32)],
         compiler_params=params(),
         name="project",
-    )(*([x] * blocks), down, down, up_kv, *others)
+    )(x, down, up_kv, *others)
 
 
 def picks(at, chosen, rows):
@@ -392,7 +362,7 @@
 
 def window_chunks(kv, devices, reach):
     chunks = [(0, 0, kv)]
-    for back in range(1, reach // PLANE + 1):
+    for back in range(reach // PLANE, 0, -1):
         hop = back * PLANE
         chunks.append((back, 0, lax.ppermute(kv, "seq", [(i, i + hop) for i in range(devices - hop)])))
     bit = PLANE // 2

time: 167 us -> 166 us (level)
  waiting for transfers between devices: 60.1 us -> 58.3 us
  transfers between devices with their start and end apart: 23 -> 23, of which waited for: 10 -> 11; matrix products, arithmetic and copies ran while one was open for 4% -> 4% of each run, Pallas kernels for 11% -> 11%
where the time goes in v7:
time: 166 us; the launch traced here: 165 us
  waiting for transfers between devices  58.3 us (35%)
  starting transfers between devices  38 us (23%)
  blocking collectives  27.5 us (17%)
  Pallas kernels  20.8 us (13%)
  local copies, waits for them, and re-layouts  17.8 us (11%)
  other arithmetic  2.01 us (1%)
    ppermute x6, waiting for transfers between devices, gathered_factors(): lax.ppermute(a, 'seq', swap)  41.3 us
    all_to_all x1, blocking collectives, exchange(): lax.all_to_all(rows.reshape(devices, rows.shape[0] // devices, width), 's...  27.5 us
    unnamed x31, local copies, waits for them, and re-layouts  17.8 us
    all_to_all x2, starting transfers between devices, exchange(): lax.all_to_all(rows.reshape(devices, rows.shape[0] // devices, width), 's...  16.6 us
    pallas_call x1, Pallas kernels, attend(): pl.pallas_call(functools.partial(attend_kernel, reach, tuple(((b, m) for...  10.4 us
    ppermute x2, starting transfers between devices, window_chunks(): lax.ppermute(kv, 'seq', [(i, i + hop) for i in range(devices - hop)])  5.76 us
    ppermute x1, waiting for transfers between devices, local(): far = lax.ppermute(far, 'seq', swap)  5.32 us
    ppermute x1, waiting for transfers between devices, gathered_factors(): there = lax.ppermute(here, 'groups', [(0, 1), (1, 0)])  5.23 us
  transfers between devices with their start and end apart: 23, of which 11 were waited for; matrix products, arithmetic and copies ran while one was open for 4% of the time, Pallas kernels for 11%

profile of v7, /device:TPU:0, one launch (start us, length us, event | category | flops | bytes accessed | tf_op | source)
XLA Modules:
  0.0 165.3 jit_solution(4396344557957724015)
XLA Ops:
  0.6 1.1 slice_select_fusion
  1.7 4.1 %collective-permute-start = (bf16[64,2048]{1,0:T(8,128)(2,1)S(1)}, bf16[64,2048]{1,0:T(8,128)(2,1)S(1)}, u32[]{:S(2)}, u32[]{:S(2)}) collective-permute-start(bf16[64,2048]{1,0:T(8,128)(2,1)S(1)} %slice_select_fusion), channel_id=1, source_target_pairs={{0,8},{1,9},{2,10},{3,11},{4,12},{5,13},{6,14},{7,15},{8,0},{9,1},... | collective-permute-start | bytes 786440 | tf_op jit(solution)/shard_map/ppermute | solution.py:338
  5.8 1.6 copy-done.2
  7.4 0.7 copy-done.10
  8.1 0.7 copy-done.11
  8.7 3.5 %dispatch.1 = (bf16[128,12288]{1,0:T(8,128)(2,1)S(1)}, s32[128,128]{1,0:T(8,128)S(1)}) custom-call(s32[1,128]{1,0:T(1,128)S(1)} %bitcast.21, s32[16]{0:T(128)S(1)} %copy-done.11, bf16[128,8192]{1,0:T(8,128)(2,1)S(1)} %copy-done.2, bf16[128,8192]{1,0:T(8,128)(2,1)S(1)} %copy-done.2), custom_call_target="tpu_custom_call" | custom-call | tf_op jit(solution)/shard_map/dispatch/pallas_call | solution.py:105
  12.2 1.6 copy-done.1
  13.8 3.9 %collective-permute-done.refs_1_ = bf16[64,2048]{1,0:T(8,128)(2,1)S(1)} collective-permute-done((bf16[64,2048]{1,0:T(8,128)(2,1)S(1)}, bf16[64,2048]{1,0:T(8,128)(2,1)S(1)}, u32[]{:S(2)}, u32[]{:S(2)}) %collective-permute-start) | collective-permute-done | bytes 262176 | tf_op jit(solution)/shard_map/ppermute | solution.py:338
  17.7 0.7 copy-done.13
  18.4 6.0 %all-to-all-start = ((bf16[16,8,12288]{2,1,0:T(8,128)(2,1)}), bf16[16,8,12288]{2,1,0:T(8,128)(2,1)S(1)}, u32[]{:S(2)}, u32[]{:S(2)}) async-start(bf16[16,8,12288]{2,1,0:T(8,128)(2,1)} %bitcast.11), calls=%async_computation | async-start | bytes 6291456 | tf_op jit(solution)/shard_map/all_to_all | solution.py:523
  24.5 1.6 collective-permute-start.1
  26.0 1.9 %collective-permute-start.2 = (bf16[64,4096]{1,0:T(8,128)(2,1)}, bf16[64,4096]{1,0:T(8,128)(2,1)}, u32[]{:S(2)}, u32[]{:S(2)}) collective-permute-start(bf16[64,4096]{1,0:T(8,128)(2,1)} %bitcast.16), channel_id=1, source_target_pairs={{0,2},{1,3},{2,0},{3,1},{4,6},{5,7},{6,4},{7,5},{8,10},{9,11},{10,... | collective-permute-start | bytes 1572872 | tf_op jit(solution)/shard_map/ppermute | solution.py:358
  27.9 5.2 %collective-permute-done.1 = bf16[64,2048]{1,0:T(8,128)(2,1)S(1)} collective-permute-done((bf16[64,2048]{1,0:T(8,128)(2,1)S(1)}, bf16[64,2048]{1,0:T(8,128)(2,1)S(1)}, u32[]{:S(2)}, u32[]{:S(2)}) %collective-permute-start.1) | collective-permute-done | bytes 262176 | tf_op jit(solution)/shard_map/ppermute | solution.py:351
  33.2 0.1 broadcast_select_fusion.1
  33.2 0.9 pad_maximum_fusion.refs_0_.refs_4_
  34.1 1.6 collective-permute-start.3
  35.8 0.0 collective-permute-start.4
  35.8 0.5 collective-permute-start.5
  36.3 28.4 %collective-permute-done.2.refs_1_.refs_2_ = bf16[64,4096]{1,0:T(8,128)(2,1)} collective-permute-done((bf16[64,4096]{1,0:T(8,128)(2,1)}, bf16[64,4096]{1,0:T(8,128)(2,1)}, u32[]{:S(2)}, u32[]{:S(2)}) %collective-permute-start.2) | collective-permute-done | bytes 524320 | tf_op jit(solution)/shard_map/ppermute | solution.py:358
  64.7 0.0 collective-permute-start.6
  64.7 12.9 %collective-permute-done.3.refs_2_.refs_6_ = bf16[64,4096]{1,0:T(8,128)(2,1)} collective-permute-done((bf16[64,4096]{1,0:T(8,128)(2,1)}, bf16[64,4096]{1,0:T(8,128)(2,1)}, u32[]{:S(2)}, u32[]{:S(2)}) %collective-permute-start.3) | collective-permute-done | bytes 524320 | tf_op jit(solution)/shard_map/ppermute | solution.py:358
  77.5 0.0 collective-permute-start.7
  77.5 5.9 %copy.14.down_ref = bf16[1,8192,192]{2,1,0:T(8,128)(2,1)} copy(bf16[1,8192,192]{1,2,0:T(8,128)(2,1)} %param.16) | data formatting | bytes 6291456 | tf_op args[6]
  83.4 0.0 collective-permute-done.4.refs_3_.refs_1_
  83.4 0.0 collective-permute-done.5.refs_4_.refs_5_
  83.4 0.0 collective-permute-done.7.refs_6_.refs_7_
  83.4 0.5 all-to-all-done
  83.9 0.4 copy-done.6
  84.3 2.2 %copy-done = bf16[1,8192,192]{2,1,0:T(8,128)(2,1)S(1)} copy-done((bf16[1,8192,192]{2,1,0:T(8,128)(2,1)S(1)}, bf16[1,8192,192]{2,1,0:T(8,128)(2,1)}, u32[]{:S(2)}) %copy-start) | copy-done | bytes 3145752
  86.5 1.6 project.1
  88.1 27.5 %all_to_all.15 = bf16[16,8,1664]{2,1,0:T(8,128)(2,1)S(1)} all-to-all(bf16[16,8,1664]{2,1,0:T(8,128)(2,1)S(1)} %bitcast.13), channel_id=1, replica_groups=mesh['groups'=2,'seq'=16] {'seq'}, dimensions={0} | all-to-all | bytes 851968 | tf_op jit(solution)/shard_map/all_to_all | solution.py:523
  115.6 0.4 correct.1
  116.1 0.9 collective-permute-start.8
  117.0 1.1 collective-permute-start.12
  118.1 2.2 %collective-permute-start.11 = (bf16[128,1024]{1,0:T(8,128)(2,1)S(1)}, bf16[128,1024]{1,0:T(8,128)(2,1)S(1)}, u32[]{:S(2)}, u32[]{:S(2)}) collective-permute-start(bf16[128,1024]{1,0:T(8,128)(2,1)S(1)} %get-tuple-element.16.kv_ref.refs_0_), channel_id=1, source_target_pairs={{0,4},{1,5},{2,6},{3,7},{4,8},{5,9},{6,10},{7,11},{8,12},{9,13},{1... | collective-permute-start | bytes 786440 | tf_op jit(solution)/shard_map/ppermute | solution.py:367
  120.4 3.5 %collective-permute-start.10 = (bf16[128,1024]{1,0:T(8,128)(2,1)S(1)}, bf16[128,1024]{1,0:T(8,128)(2,1)S(1)}, u32[]{:S(2)}, u32[]{:S(2)}) collective-permute-start(bf16[128,1024]{1,0:T(8,128)(2,1)S(1)} %get-tuple-element.16.kv_ref.refs_0_), channel_id=1, source_target_pairs={{0,8},{1,9},{2,10},{3,11},{4,12},{5,13},{6,14},{7,15},{16,24},{17,... | collective-permute-start | bytes 786440 | tf_op jit(solution)/shard_map/ppermute | solution.py:367
  123.9 0.0 copy-start.4
  123.9 1.0 copy-done.4
  124.9 1.2 copy-done.12
  126.2 4.2 %expand.1 = (bf16[128,4096]{1,0:T(8,128)(2,1)S(1)}, bf16[128,96]{1,0:T(8,128)(2,1)S(1)}, bf16[128,1024]{1,0:T(8,128)(2,1)S(1)}, bf16[96,4096]{1,0:T(8,128)(2,1)}) custom-call(s32[1]{0:T(128)} %bitcast.me_ref, bf16[128,128]{1,0:T(8,128)(2,1)S(1)} %get-tuple-element.15.own_rows_ref, bf16[128,128]{1,0:T(8,128)(2,1)S(1)} %collective-permute-done.8.far_rows_ref, ...), custom_call_target="tpu_custom_call" | custom-call | flops 4294967296 | bytes 2097152 | tf_op jit(solution)/shard_map/expand/pallas_call | solution.py:285
  130.4 0.7 copy-done.5
  131.0 0.0 collective-permute-start.9
  131.0 0.0 collective-permute-start.15
  131.1 0.0 collective-permute-done.12.refs_3_
  131.1 0.5 collective-permute-start.18
  131.6 0.0 collective-permute-done.11.refs_2_
  131.6 2.0 %collective-permute-start.14 = (bf16[128,1024]{1,0:T(8,128)(2,1)S(1)}, bf16[128,1024]{1,0:T(8,128)(2,1)}, u32[]{:S(2)}, u32[]{:S(2)}) collective-permute-start(bf16[128,1024]{1,0:T(8,128)(2,1)S(1)} %collective-permute-done.11.refs_2_), channel_id=1, source_target_pairs={{0,2},{1,3},{2,0},{3,1},{4,6},{5,7},{6,4},{7,5},{8,10},{9,11},{10,... | collective-permute-start | bytes 786440 | tf_op jit(solution)/shard_map/ppermute | solution.py:371
  133.6 0.0 collective-permute-done.10.refs_1_
  133.6 0.3 collective-permute-start.13
  133.9 10.6 %all-to-all-start.2 = ((bf16[16,8,1024]{2,1,0:T(8,128)(2,1)}), bf16[16,8,1024]{2,1,0:T(8,128)(2,1)S(1)}, u32[]{:S(2)}, u32[]{:S(2)}) async-start(bf16[16,8,1024]{2,1,0:T(8,128)(2,1)} %bitcast.19), calls=%async_computation.2 | async-start | bytes 524288 | tf_op jit(solution)/shard_map/all_to_all | solution.py:523
  144.5 0.5 collective-permute-start.17
  145.0 0.1 collective-permute-start.16
  145.1 0.0 collective-permute-done.14.refs_5_
  145.1 0.4 collective-permute-start.20
  145.5 0.4 collective-permute-done.13.refs_4_
  145.9 0.3 collective-permute-done.17.refs_8_
  146.1 0.4 collective-permute-done.16.refs_7_
  146.5 0.6 collective-permute-done.20.refs_11_
  147.1 0.5 collective-permute-done.19.refs_10_
  147.6 5.3 %collective-permute-done.9.far_ref = bf16[96,4096]{1,0:T(8,128)(2,1)S(1)} collective-permute-done((bf16[96,4096]{1,0:T(8,128)(2,1)}, bf16[96,4096]{1,0:T(8,128)(2,1)S(1)}, u32[]{:S(2)}, u32[]{:S(2)}) %collective-permute-start.9) | collective-permute-done | bytes 786464 | tf_op jit(solution)/shard_map/ppermute | solution.py:564
  152.9 10.4 %attend.1._ = bf16[128,4096]{1,0:T(8,128)(2,1)} custom-call(s32[1]{0:T(128)} %bitcast.me_ref, s32[16,128]{1,0:T(8,128)S(1)} %bitcast.20, bf16[128,4096]{1,0:T(8,128)(2,1)S(1)} %get-tuple-element.17.query_ref, bf16[128,96]{1,0:T(8,128)(2,1)S(1)} %get-tuple-element.18.unpack_ref, bf16[96,4096]{1,0:T(8,128)(2,1)S(1)} %collective-permute-done.9.far_ref, ...), custom_call_target="tpu_custom_call" | custom-call | flops 603979776 | bytes 524288 | tf_op jit(solution)/shard_map/attend/pallas_call | solution.py:480
  163.4 0.0 copy-start.3
  163.4 1.2 copy-done.3
  164.6 0.7 split.1
  (25 shorter events, 0.0 us)
Async XLA Ops:
  1.7 16.0 %collective-permute-start = (bf16[64,2048]{1,0:T(8,128)(2,1)S(1)}, bf16[64,2048]{1,0:T(8,128)(2,1)S(1)}, u32[]{:S(2)}, u32[]{:S(2)}) collective-permute-start(bf16[64,2048]{1,0:T(8,128)(2,1)S(1)} %slice_select_fusion), channel_id=1, source_target_pairs={{0,8},{1,9},{2,10},{3,11},{4,12},{5,13},{6,14},{7,15},{8,0},{9,1},... | collective-permute-start | bytes 786440 | tf_op jit(solution)/shard_map/ppermute | solution.py:338
  5.8 1.6 copy-start.2
  7.4 0.7 copy-start.10
  8.1 0.7 copy-start.11
  12.2 1.6 copy-start.1
  17.7 0.7 copy-start.13
  18.4 6.0 %copy-start.14 = (bf16[64,2048]{1,0:T(8,128)(2,1)S(1)}, bf16[64,2048]{1,0:T(8,128)(2,1)}, u32[]{:S(2)}) copy-start(bf16[64,2048]{1,0:T(8,128)(2,1)} %copy-done.13) | copy-start | bytes 786436
  18.4 65.5 %all-to-all-start = ((bf16[16,8,12288]{2,1,0:T(8,128)(2,1)}), bf16[16,8,12288]{2,1,0:T(8,128)(2,1)S(1)}, u32[]{:S(2)}, u32[]{:S(2)}) async-start(bf16[16,8,12288]{2,1,0:T(8,128)(2,1)} %bitcast.11), calls=%async_computation | async-start | bytes 6291456 | tf_op jit(solution)/shard_map/all_to_all | solution.py:523
  24.5 8.7 %collective-permute-start.1 = (bf16[64,2048]{1,0:T(8,128)(2,1)S(1)}, bf16[64,2048]{1,0:T(8,128)(2,1)S(1)}, u32[]{:S(2)}, u32[]{:S(2)}) collective-permute-start(bf16[64,2048]{1,0:T(8,128)(2,1)S(1)} %copy-done.14), channel_id=1, source_target_pairs={{0,16},{16,0},{1,17},{17,1},{2,18},{18,2},{3,19},{19,3},{4,20},{20... | collective-permute-start | bytes 786440 | tf_op jit(solution)/shard_map/ppermute | solution.py:351
  26.0 38.7 %collective-permute-start.2 = (bf16[64,4096]{1,0:T(8,128)(2,1)}, bf16[64,4096]{1,0:T(8,128)(2,1)}, u32[]{:S(2)}, u32[]{:S(2)}) collective-permute-start(bf16[64,4096]{1,0:T(8,128)(2,1)} %bitcast.16), channel_id=1, source_target_pairs={{0,2},{1,3},{2,0},{3,1},{4,6},{5,7},{6,4},{7,5},{8,10},{9,11},{10,... | collective-permute-start | bytes 1572872 | tf_op jit(solution)/shard_map/ppermute | solution.py:358
  34.1 43.4 %collective-permute-start.3 = (bf16[64,4096]{1,0:T(8,128)(2,1)}, bf16[64,4096]{1,0:T(8,128)(2,1)}, u32[]{:S(2)}, u32[]{:S(2)}) collective-permute-start(bf16[64,4096]{1,0:T(8,128)(2,1)} %pad_maximum_fusion.refs_0_.refs_4_), channel_id=1, source_target_pairs={{0,2},{1,3},{2,0},{3,1},{4,6},{5,7},{6,4},{7,5},{8,10},{9,11},{10,... | collective-permute-start | bytes 1572872 | tf_op jit(solution)/shard_map/ppermute | solution.py:358
  35.8 47.7 %collective-permute-start.4 = (bf16[64,4096]{1,0:T(8,128)(2,1)}, bf16[64,4096]{1,0:T(8,128)(2,1)}, u32[]{:S(2)}, u32[]{:S(2)}) collective-permute-start(bf16[64,4096]{1,0:T(8,128)(2,1)} %bitcast.17), channel_id=1, source_target_pairs={{0,1},{1,0},{2,3},{3,2},{4,5},{5,4},{6,7},{7,6},{8,9},{9,8},{10,11... | collective-permute-start | bytes 1572872 | tf_op jit(solution)/shard_map/ppermute | solution.py:358
  35.8 47.7 %collective-permute-start.5 = (bf16[64,4096]{1,0:T(8,128)(2,1)}, bf16[64,4096]{1,0:T(8,128)(2,1)}, u32[]{:S(2)}, u32[]{:S(2)}) collective-permute-start(bf16[64,4096]{1,0:T(8,128)(2,1)} %pad_maximum_fusion.refs_0_.refs_4_), channel_id=1, source_target_pairs={{0,1},{1,0},{2,3},{3,2},{4,5},{5,4},{6,7},{7,6},{8,9},{9,8},{10,11... | collective-permute-start | bytes 1572872 | tf_op jit(solution)/shard_map/ppermute | solution.py:358
  64.7 18.7 %collective-permute-start.6 = (bf16[64,4096]{1,0:T(8,128)(2,1)}, bf16[64,4096]{1,0:T(8,128)(2,1)}, u32[]{:S(2)}, u32[]{:S(2)}) collective-permute-start(bf16[64,4096]{1,0:T(8,128)(2,1)} %collective-permute-done.2.refs_1_.refs_2_), channel_id=1, source_target_pairs={{0,1},{1,0},{2,3},{3,2},{4,5},{5,4},{6,7},{7,6},{8,9},{9,8},{10,11... | collective-permute-start | bytes 1572872 | tf_op jit(solution)/shard_map/ppermute | solution.py:358
  77.5 5.9 %collective-permute-start.7 = (bf16[64,4096]{1,0:T(8,128)(2,1)}, bf16[64,4096]{1,0:T(8,128)(2,1)}, u32[]{:S(2)}, u32[]{:S(2)}) collective-permute-start(bf16[64,4096]{1,0:T(8,128)(2,1)} %collective-permute-done.3.refs_2_.refs_6_), channel_id=1, source_target_pairs={{0,1},{1,0},{2,3},{3,2},{4,5},{5,4},{6,7},{7,6},{8,9},{9,8},{10,11... | collective-permute-start | bytes 1572872 | tf_op jit(solution)/shard_map/ppermute | solution.py:358
  83.4 0.9 copy-start.6
  84.3 2.2 %copy-start = (bf16[1,8192,192]{2,1,0:T(8,128)(2,1)S(1)}, bf16[1,8192,192]{2,1,0:T(8,128)(2,1)}, u32[]{:S(2)}) copy-start(bf16[1,8192,192]{2,1,0:T(8,128)(2,1)} %copy.14.down_ref) | copy-start | bytes 9437188
  86.5 29.1 %copy-start.7 = (bf16[128,512]{1,0:T(8,128)(2,1)S(1)}, bf16[128,512]{1,0:T(8,128)(2,1)}, u32[]{:S(2)}) copy-start(bf16[128,512]{1,0:T(8,128)(2,1)} %sk_ref.1) | copy-start | bytes 393220
  86.5 29.1 %copy-start.8 = (bf16[128,512]{1,0:T(8,128)(2,1)S(1)}, bf16[128,512]{1,0:T(8,128)(2,1)}, u32[]{:S(2)}) copy-start(bf16[128,512]{1,0:T(8,128)(2,1)} %sv_ref.1) | copy-start | bytes 393220
  116.1 7.8 %collective-permute-start.8 = (bf16[128,128]{1,0:T(8,128)(2,1)S(1)}, bf16[128,128]{1,0:T(8,128)(2,1)S(1)}, u32[]{:S(2)}, u32[]{:S(2)}) collective-permute-start(bf16[128,128]{1,0:T(8,128)(2,1)S(1)} %get-tuple-element.15.own_rows_ref), channel_id=1, source_target_pairs={{0,4},{1,5},{2,6},{3,7},{4,0},{5,1},{6,2},{7,3},{8,12},{9,13},{10,... | collective-permute-start | bytes 98312 | tf_op jit(solution)/shard_map/ppermute | solution.py:560
  117.0 14.1 %collective-permute-start.12 = (bf16[128,1024]{1,0:T(8,128)(2,1)S(1)}, bf16[128,1024]{1,0:T(8,128)(2,1)S(1)}, u32[]{:S(2)}, u32[]{:S(2)}) collective-permute-start(bf16[128,1024]{1,0:T(8,128)(2,1)S(1)} %get-tuple-element.16.kv_ref.refs_0_), channel_id=1, source_target_pairs={{0,2},{1,3},{2,0},{3,1},{4,6},{5,7},{6,4},{7,5},{8,10},{9,11},{10,... | collective-permute-start | bytes 786440 | tf_op jit(solution)/shard_map/ppermute | solution.py:371
  118.1 13.4 %collective-permute-start.11 = (bf16[128,1024]{1,0:T(8,128)(2,1)S(1)}, bf16[128,1024]{1,0:T(8,128)(2,1)S(1)}, u32[]{:S(2)}, u32[]{:S(2)}) collective-permute-start(bf16[128,1024]{1,0:T(8,128)(2,1)S(1)} %get-tuple-element.16.kv_ref.refs_0_), channel_id=1, source_target_pairs={{0,4},{1,5},{2,6},{3,7},{4,8},{5,9},{6,10},{7,11},{8,12},{9,13},{1... | collective-permute-start | bytes 786440 | tf_op jit(solution)/shard_map/ppermute | solution.py:367
  120.4 13.2 %collective-permute-start.10 = (bf16[128,1024]{1,0:T(8,128)(2,1)S(1)}, bf16[128,1024]{1,0:T(8,128)(2,1)S(1)}, u32[]{:S(2)}, u32[]{:S(2)}) collective-permute-start(bf16[128,1024]{1,0:T(8,128)(2,1)S(1)} %get-tuple-element.16.kv_ref.refs_0_), channel_id=1, source_target_pairs={{0,8},{1,9},{2,10},{3,11},{4,12},{5,13},{6,14},{7,15},{16,24},{17,... | collective-permute-start | bytes 786440 | tf_op jit(solution)/shard_map/ppermute | solution.py:367
  123.9 1.0 copy-start.4
  124.9 1.2 copy-start.12
  126.2 26.8 %copy-start.9 = (s32[2048]{0:T(1024)S(1)}, s32[2048]{0:T(1024)}, u32[]{:S(2)}) copy-start(s32[2048]{0:T(1024)} %param.19) | copy-start | bytes 24580
  130.4 0.7 copy-start.5
  131.0 21.9 %collective-permute-start.9 = (bf16[96,4096]{1,0:T(8,128)(2,1)}, bf16[96,4096]{1,0:T(8,128)(2,1)S(1)}, u32[]{:S(2)}, u32[]{:S(2)}) collective-permute-start(bf16[96,4096]{1,0:T(8,128)(2,1)} %get-tuple-element.19), channel_id=1, source_target_pairs={{0,4},{1,5},{2,6},{3,7},{4,0},{5,1},{6,2},{7,3},{8,12},{9,13},{10,... | collective-permute-start | bytes 2359304 | tf_op jit(solution)/shard_map/ppermute | solution.py:564
  131.0 13.5 %collective-permute-start.15 = (bf16[128,1024]{1,0:T(8,128)(2,1)S(1)}, bf16[128,1024]{1,0:T(8,128)(2,1)S(1)}, u32[]{:S(2)}, u32[]{:S(2)}) collective-permute-start(bf16[128,1024]{1,0:T(8,128)(2,1)S(1)} %get-tuple-element.16.kv_ref.refs_0_), channel_id=1, source_target_pairs={{0,1},{1,0},{2,3},{3,2},{4,5},{5,4},{6,7},{7,6},{8,9},{9,8},{10,11... | collective-permute-start | bytes 786440 | tf_op jit(solution)/shard_map/ppermute | solution.py:371
  131.1 13.9 %collective-permute-start.18 = (bf16[128,1024]{1,0:T(8,128)(2,1)S(1)}, bf16[128,1024]{1,0:T(8,128)(2,1)}, u32[]{:S(2)}, u32[]{:S(2)}) collective-permute-start(bf16[128,1024]{1,0:T(8,128)(2,1)S(1)} %collective-permute-done.12.refs_3_), channel_id=1, source_target_pairs={{0,1},{1,0},{2,3},{3,2},{4,5},{5,4},{6,7},{7,6},{8,9},{9,8},{10,11... | collective-permute-start | bytes 786440 | tf_op jit(solution)/shard_map/ppermute | solution.py:371
  131.6 13.5 %collective-permute-start.14 = (bf16[128,1024]{1,0:T(8,128)(2,1)S(1)}, bf16[128,1024]{1,0:T(8,128)(2,1)}, u32[]{:S(2)}, u32[]{:S(2)}) collective-permute-start(bf16[128,1024]{1,0:T(8,128)(2,1)S(1)} %collective-permute-done.11.refs_2_), channel_id=1, source_target_pairs={{0,2},{1,3},{2,0},{3,1},{4,6},{5,7},{6,4},{7,5},{8,10},{9,11},{10,... | collective-permute-start | bytes 786440 | tf_op jit(solution)/shard_map/ppermute | solution.py:371
  133.6 12.3 %collective-permute-start.13 = (bf16[128,1024]{1,0:T(8,128)(2,1)S(1)}, bf16[128,1024]{1,0:T(8,128)(2,1)}, u32[]{:S(2)}, u32[]{:S(2)}) collective-permute-start(bf16[128,1024]{1,0:T(8,128)(2,1)S(1)} %collective-permute-done.10.refs_1_), channel_id=1, source_target_pairs={{0,2},{1,3},{2,0},{3,1},{4,6},{5,7},{6,4},{7,5},{8,10},{9,11},{10,... | collective-permute-start | bytes 786440 | tf_op jit(solution)/shard_map/ppermute | solution.py:371
  133.9 29.4 %all-to-all-start.2 = ((bf16[16,8,1024]{2,1,0:T(8,128)(2,1)}), bf16[16,8,1024]{2,1,0:T(8,128)(2,1)S(1)}, u32[]{:S(2)}, u32[]{:S(2)}) async-start(bf16[16,8,1024]{2,1,0:T(8,128)(2,1)} %bitcast.19), calls=%async_computation.2 | async-start | bytes 524288 | tf_op jit(solution)/shard_map/all_to_all | solution.py:523
  144.5 1.6 collective-permute-start.17
  145.0 1.5 collective-permute-start.16
  145.1 2.0 %collective-permute-start.20 = (bf16[128,1024]{1,0:T(8,128)(2,1)}, bf16[128,1024]{1,0:T(8,128)(2,1)S(1)}, u32[]{:S(2)}, u32[]{:S(2)}) collective-permute-start(bf16[128,1024]{1,0:T(8,128)(2,1)} %collective-permute-done.14.refs_5_), channel_id=1, source_target_pairs={{0,1},{1,0},{2,3},{3,2},{4,5},{5,4},{6,7},{7,6},{8,9},{9,8},{10,11... | collective-permute-start | bytes 786440 | tf_op jit(solution)/shard_map/ppermute | solution.py:371
  145.9 1.7 %collective-permute-start.19 = (bf16[128,1024]{1,0:T(8,128)(2,1)}, bf16[128,1024]{1,0:T(8,128)(2,1)S(1)}, u32[]{:S(2)}, u32[]{:S(2)}) collective-permute-start(bf16[128,1024]{1,0:T(8,128)(2,1)} %collective-permute-done.13.refs_4_), channel_id=1, source_target_pairs={{0,1},{1,0},{2,3},{3,2},{4,5},{5,4},{6,7},{7,6},{8,9},{9,8},{10,11... | collective-permute-start | bytes 786440 | tf_op jit(solution)/shard_map/ppermute | solution.py:371
  163.4 1.2 copy-start.3
